TPU v7x, 32 devices: a whole 2x2x4 slice. The times are simulated.
32 devices in a mesh: rows: 4 (over y, x), pts: 8 (over z, core).
Axes of the slice: x: 2, y: 2, z: 4, core: 2. Of those that a mesh axis runs over, the one named last changes fastest.
Arguments:
- env_desc: bfloat16 [2048, 1024], P('rows', 'pts'), may hold values from -6 to 6
- point_desc: bfloat16 [16384, 1024], P('pts', 'rows'), may hold values from -6 to 6
- pool_index: int32 [1024, 4], P('rows'), may hold values from 0 to 511
- pool_count: int32 [1024], P('rows'), may hold values from 1 to 4
- pool_weight: float32 [1024, 4], P('rows'), may hold values from -3 to 3
- row_dest: int32 [1024], P('rows'), may hold values from -1 to 511, as said below
Outputs:
- design: float32 [512, 16384], P('rows', 'pts')
- gram: float32 [16384, 16384], P('rows', 'pts')
Inputs may be any that keep to these rules, and one draw needn't show every extreme that they name: Slot s pools environments (s // 256) * 512 + pool_index[s, j] of its own structure group. Slot s pools its first pool_count[s] entries. `row_dest`: -1 marks an empty slot; every row 0 .. 511 is named by exactly one slot; the slots of one structure group (aligned blocks of 256 slots) name at most 64 rows of any aligned block of 128 rows, and in every draw some structure group names exactly 64 rows of every such block.
All inputs are finite; a program needn't handle non-finite values.
Results may differ from a plain program's by a relative error of at most 0.0003.
Values may be sent and summed in bfloat16 or wider, within the bound.
No kernel may reach another device: no remote copies, remote signals or barrier semaphores. Data moves between devices by JAX's collectives and lax.ppermute only.
A program may use at most 128 MiB of HBM per device.

v0:
```python
import jax
import jax.numpy as jnp
from jax import lax
from jax.sharding import PartitionSpec as P

damping = 0.5


def from_root(value, axis, source):
    kept = jnp.where(lax.axis_index(axis) == source, value, 0).astype(value.dtype)
    return lax.psum(kept, axis)


def kernel_values(left, right):
    products = lax.dot_general(
        left, right, (((1,), (1,)), ((), ())), preferred_element_type=jnp.float32
    )
    scaled = products * left.shape[1] ** (-0.5)
    squared = scaled * scaled
    return 0.25 * squared * squared


def live_weights(pool_count, pool_weight):
    members = jnp.arange(pool_weight.shape[1], dtype=jnp.int32)
    return jnp.where(members[None, :] < pool_count[:, None], pool_weight, 0.0)


def pool_rows(kernel_table, env_index, weights_live):
    pooled = jnp.zeros((env_index.shape[0], kernel_table.shape[1]), jnp.float32)
    for member in range(env_index.shape[1]):
        pooled = pooled + weights_live[:, member : member + 1] * kernel_table[env_index[:, member]]
    return pooled


def on_device(env_desc, point_desc, pool_index, pool_count, pool_weight, row_dest):
    groups = lax.axis_size("rows")
    slot_total = pool_index.shape[0]
    balanced = slot_total // 2
    slot_share = slot_total // groups
    points = lax.all_gather(point_desc, "rows", axis=1, tiled=True)
    width_pts = points.shape[0]
    weights_live = live_weights(pool_count, pool_weight)
    live_slot = row_dest >= 0
    owner_group = jnp.where(live_slot, row_dest // balanced, groups)
    within = jnp.where(live_slot, row_dest % balanced, balanced)
    owner_table = (owner_group[:, None] == jnp.arange(groups, dtype=jnp.int32)[None, :]).astype(
        jnp.int32
    )
    earlier = jnp.cumsum(owner_table, axis=0) - owner_table
    slot_rank = jnp.sum(earlier * owner_table, axis=1)
    outbox_place = (
        jnp.full((groups, slot_share), balanced, jnp.int32)
        .at[owner_group, slot_rank]
        .set(within, mode="drop")
    )
    features = lax.all_gather(env_desc, "pts", axis=1, tiled=True)
    slot_rows = pool_rows(kernel_values(features, points), pool_index, weights_live)
    outbox = (
        jnp.zeros((groups, slot_share, width_pts), jnp.float32)
        .at[owner_group, slot_rank]
        .set(slot_rows, mode="drop")
    )
    inbox_rows, inbox_place = (
        lax.all_to_all(outbox, "rows", split_axis=0, concat_axis=0, tiled=True),
        lax.all_to_all(outbox_place, "rows", split_axis=0, concat_axis=0, tiled=True),
    )
    design = (
        jnp.zeros((balanced, width_pts), jnp.float32)
        .at[inbox_place.reshape(-1)]
        .set(inbox_rows.reshape(-1, width_pts), mode="drop")
    )
    all_rows = lax.all_gather(design, "rows", axis=0, tiled=True)
    per_group = lax.axis_size("pts") // groups
    row_group = lax.axis_index("rows")
    pieces = []
    for part_index in range(per_group):
        diagonal_panel = from_root(all_rows, "pts", row_group * per_group + part_index)
        pieces.append(
            lax.dot_general(
                diagonal_panel,
                all_rows,
                (((0,), (0,)), ((), ())),
                precision=lax.Precision.HIGHEST,
                preferred_element_type=jnp.float32,
            )
        )
    gram_tile = jnp.concatenate(pieces, axis=0) * (1.0 / all_rows.shape[0])
    tile_rows = gram_tile.shape[0]
    row_ids = row_group * tile_rows + jnp.arange(tile_rows, dtype=jnp.int32)
    col_ids = lax.axis_index("pts") * width_pts + jnp.arange(width_pts, dtype=jnp.int32)
    gram_tile = gram_tile + jnp.where(row_ids[:, None] == col_ids[None, :], damping, 0.0)
    return (design, gram_tile)


def solution(mesh):
    in_specs = (
        P("rows", "pts"),
        P("pts", "rows"),
        P("rows", None),
        P("rows"),
        P("rows", None),
        P("rows"),
    )
    out_specs = (P("rows", "pts"), P("rows", "pts"))
    return jax.shard_map(
        on_device, mesh=mesh, in_specs=in_specs, out_specs=out_specs, check_vma=False
    )
```

profile of v0, /device:TPU:0, one launch (start us, length us, event | category | flops | bytes accessed | tf_op | source)
XLA Modules:
  0.0 533.5 jit_solution(1396050597013215383)
XLA Ops:
  7.2 0.0 all-gather.4.cloned.1.call-start
  7.2 0.7 all-gather.4.cloned.1.call-update
  7.9 0.0 all-gather.6.cloned.1.call-start
  7.9 0.7 all-gather.6.cloned.1.call-update
  8.6 0.7 compare_select_fusion.6
  9.4 1.2 reduce-window.6
  10.6 0.1 slice.52
  10.7 0.1 copy.12
  10.8 0.1 copy.13
  10.9 0.1 add_bitcast_fusion
  11.0 0.6 broadcast_in_dim.49
  11.6 35.4 %scatter_fusion = s32[4,64]{1,0:T(4,128)} fusion(s32[4,64]{1,0:T(4,128)} %broadcast_in_dim.49, s32[256]{0:T(256)S(1)} %bitcast.45, s32[256]{0:T(256)S(1)} %get-tuple-element.16), kind=kCustom, calls=%fused_computation.4 | custom fusion | bytes 5120 | tf_op jit(solution)/shard_map/scatter | solution.py:54
  46.9 8.2 %all-to-all-start = ((s32[4,1,64]{2,1,0:T(1,128)}), s32[4,1,64]{2,1,0:T(1,128)S(1)}, u32[]{:S(2)}, u32[]{:S(2)}) async-start(s32[4,1,64]{2,1,0:T(1,128)} %bitcast.7), calls=%async_computation | async-start | bytes 4096 | tf_op jit(solution)/shard_map/all_to_all | solution.py:65
  55.2 0.8 compare_select_fusion.3
  56.1 0.7 fusion.6
  56.8 0.0 all-gather.4.cloned.1.call-done
  56.8 32.6 %all-gather.6.cloned.1.call-done = bf16[2048,1024]{1,0:T(8,128)(2,1)} async-done(((bf16[2048,256]{1,0:T(8,128)(2,1)}), bf16[2048,1024]{1,0:T(8,128)(2,1)}) %all-gather.6.cloned.1.call-update) | async-done | bytes 4194320 | tf_op jit(solution)/shard_map/all_gather | solution.py:40
  89.4 6.9 %multiply_multiply_fusion = f32[512,2048]{1,0:T(8,128)} fusion(bf16[512,1024]{1,0:T(8,128)(2,1)} %all-gather.4.cloned.1.call-done, bf16[2048,1024]{1,0:T(8,128)(2,1)} %all-gather.6.cloned.1.call-done), kind=kOutput, calls=%fused_computation.9 | convolution fusion | flops 2151677952 | bytes 9437184 | tf_op jit(solution)/shard_map/dot_general | solution.py:15
  96.3 4.6 gather_fusion.2
  100.9 5.8 %gather_fusion.3 = f32[256,2048]{1,0:T(8,128)} fusion(f32[512,2048]{1,0:T(8,128)} %multiply_multiply_fusion, s32[1024]{0:T(1024)S(1)} %pad_clamp_fusion), kind=kCustom, calls=%fused_computation.3 | custom fusion | bytes 4195328 | tf_op jit(solution)/shard_map/gather | solution.py:31
  106.7 5.8 %gather_fusion = f32[256,2048]{1,0:T(8,128)} fusion(f32[512,2048]{1,0:T(8,128)} %multiply_multiply_fusion, s32[1024]{0:T(1024)S(1)} %pad_clamp_fusion.3), kind=kCustom, calls=%fused_computation | custom fusion | bytes 4195328 | tf_op jit(solution)/shard_map/gather | solution.py:31
  112.5 5.8 %gather_fusion.1 = f32[256,2048]{1,0:T(8,128)} fusion(f32[512,2048]{1,0:T(8,128)} %multiply_multiply_fusion, s32[1024]{0:T(1024)S(1)} %pad_clamp_fusion.2), kind=kCustom, calls=%fused_computation.1 | custom fusion | bytes 4195328 | tf_op jit(solution)/shard_map/gather | solution.py:31
  118.3 4.8 multiply_add_fusion
  123.1 1.6 broadcast_in_dim.52
  124.6 48.9 %scatter_fusion.1 = f32[4,64,2048]{2,1,0:T(8,128)} fusion(f32[4,64,2048]{2,1,0:T(8,128)} %broadcast_in_dim.52, s32[256]{0:T(256)S(1)} %bitcast.46, f32[256,2048]{1,0:T(8,128)} %multiply_add_fusion), kind=kCustom, calls=%fused_computation.5 | custom fusion | bytes 6293504 | tf_op jit(solution)/shard_map/scatter | solution.py:61
  173.6 0.0 all-to-all-done
  173.6 3.6 all-to-all-start.1
  177.2 0.2 all-gather.8.cloned.1.call-start
  177.4 0.5 broadcast.186
  177.9 0.7 reduce.3
  178.6 0.1 reshape.80
  178.7 23.6 %all-to-all-done.1 = f32[4,64,2048]{2,1,0:T(8,128)S(1)} async-done(((f32[4,64,2048]{2,1,0:T(8,128)}), f32[4,64,2048]{2,1,0:T(8,128)S(1)}, u32[]{:S(2)}, u32[]{:S(2)}) %all-to-all-start.1) | async-done | bytes 2097184 | tf_op jit(solution)/shard_map/all_to_all | solution.py:64
  202.3 2.8 scatter_custom_fusion.2
  205.1 0.0 all-gather.8.cloned.1.call-update
  205.2 0.0 all-reduce.3.cloned.1.call-start
  205.2 52.8 %all-gather.8.cloned.1.call-done = f32[512,2048]{1,0:T(8,128)} async-done(((f32[128,2048]{1,0:T(8,128)}), f32[512,2048]{1,0:T(8,128)}) %all-gather.8.cloned.1.call-update) | async-done | bytes 4194320 | tf_op jit(solution)/shard_map/all_gather | solution.py:72
  258.0 6.9 %broadcast_select_fusion.1 = (f32[512,2048]{1,0:T(8,128)}, f32[512,2048]{1,0:T(8,128)}) fusion(f32[512,2048]{1,0:T(8,128)} %all-gather.8.cloned.1.call-done, pred[]{:T(512)S(6)} %eq.54, pred[]{:T(512)S(6)} %eq.55), kind=kLoop, calls=%fused_computation.11 | loop fusion | flops 2097152 | bytes 12582914 | tf_op jit(solution)/shard_map/jit(_where)/select_n | solution.py:10
  264.9 0.0 all-reduce.3.cloned.1.call-update
  265.0 176.1 %all-reduce.3.cloned.1.call-done = (f32[512,2048]{1,0:T(8,128)}, f32[512,2048]{1,0:T(8,128)}) async-done(((f32[512,2048]{1,0:T(8,128)}, f32[512,2048]{1,0:T(8,128)}), (f32[512,2048]{1,0:T(8,128)}, f32[512,2048]{1,0:T(8,128)})) %all-reduce.3.cloned.1.call-update) | async-done | bytes 8388624 | tf_op jit(solution)/shard_map/psum | solution.py:11
  441.0 0.0 copy-start
  441.0 0.0 copy-start.1
  441.0 31.6 %fusion.13 = f32[2048,2048]{1,0:T(8,128)} fusion(f32[512,2048]{1,0:T(8,128)} %get-tuple-element.2, f32[512,2048]{1,0:T(8,128)} %all-gather.8.cloned.1.call-done), kind=kOutput, calls=%fused_computation.53 | convolution fusion | flops 25769803776 | bytes 25165824 | tf_op jit(solution)/shard_map/dot_general | solution.py:79
  472.6 0.0 copy-done
  472.6 0.0 copy-done.1
  472.6 30.2 %fusion.12 = f32[2048,2048]{1,0:T(8,128)} fusion(f32[512,2048]{1,0:T(8,128)S(1)} %copy-done.1, f32[512,2048]{1,0:T(8,128)S(1)} %copy-done), kind=kOutput, calls=%fused_computation.52 | convolution fusion | flops 25769803776 | bytes 25165824 | tf_op jit(solution)/shard_map/dot_general | solution.py:79
  502.9 24.1 %fusion = f32[4096,2048]{1,0:T(8,128)} fusion(f32[2048,2048]{1,0:T(8,128)} %fusion.13, f32[2048,2048]{1,0:T(8,128)} %fusion.12, s32[2048]{0:T(1024)S(1)} %iota_add_fusion.1, s32[4096]{0:T(1024)S(1)} %iota_add_fusion), kind=kLoop, calls=%fused_computation.8 | loop fusion | flops 41943040 | bytes 67133440 | tf_op jit(solution)/shard_map/add | solution.py:91
  (13 shorter events, 0.1 us)
Async XLA Ops:
  7.2 49.7 %all-gather.4.cloned.1.call-start = ((), (), s32[]{:S(2)}) async-start(), calls=%async_computation.2 | async-start | bytes 1179648 | tf_op jit(solution)/shard_map/all_gather | solution.py:56
  7.9 81.5 %all-gather.6.cloned.1.call-start = ((), (), s32[]{:S(2)}) async-start(), calls=%async_computation.3 | async-start | bytes 5242880 | tf_op jit(solution)/shard_map/all_gather | solution.py:40
  46.9 126.6 %all-to-all-start = ((s32[4,1,64]{2,1,0:T(1,128)}), s32[4,1,64]{2,1,0:T(1,128)S(1)}, u32[]{:S(2)}, u32[]{:S(2)}) async-start(s32[4,1,64]{2,1,0:T(1,128)} %bitcast.7), calls=%async_computation | async-start | bytes 4096 | tf_op jit(solution)/shard_map/all_to_all | solution.py:65
  173.6 28.7 %all-to-all-start.1 = ((f32[4,64,2048]{2,1,0:T(8,128)}), f32[4,64,2048]{2,1,0:T(8,128)S(1)}, u32[]{:S(2)}, u32[]{:S(2)}) async-start(f32[4,64,2048]{2,1,0:T(8,128)} %scatter_fusion.1), calls=%async_computation.1 | async-start | bytes 4194304 | tf_op jit(solution)/shard_map/all_to_all | solution.py:64
  177.2 80.8 %all-gather.8.cloned.1.call-start = ((), (), s32[]{:S(2)}) async-start(), calls=%async_computation.4 | async-start | bytes 5242880 | tf_op jit(solution)/shard_map/all_gather | solution.py:72
  205.2 235.9 %all-reduce.3.cloned.1.call-start = ((), (), s32[]{:S(2)}) async-start(), calls=%async_computation.5 | async-start | bytes 16777216 | tf_op jit(solution)/shard_map/psum | solution.py:11
  441.0 31.6 %copy-start = (f32[512,2048]{1,0:T(8,128)S(1)}, f32[512,2048]{1,0:T(8,128)}, u32[]{:S(2)}) copy-start(f32[512,2048]{1,0:T(8,128)} %all-gather.8.cloned.1.call-done) | copy-start | bytes 12582916
  441.0 31.6 %copy-start.1 = (f32[512,2048]{1,0:T(8,128)S(1)}, f32[512,2048]{1,0:T(8,128)}, u32[]{:S(2)}) copy-start(f32[512,2048]{1,0:T(8,128)} %get-tuple-element.3) | copy-start | bytes 12582916
Sparse Core Ops, SparseCore 0:
  9.6 26.6 all-gather.3
  38.1 51.2 all-gather.5
  205.3 52.6 all-gather.7
  265.0 175.9 all-reduce.2
where the time goes:
time: 535 us; the launch traced here: 533 us
  waiting for transfers between devices  286 us (53%)
  local copies, waits for them, and re-layouts  112 us (21%)
  matrix products  68.7 us (13%)
  other arithmetic  40.1 us (7%)
  between operations  13.9 us (3%)
  starting transfers between devices  12.2 us (2%)
    psum x1, waiting for transfers between devices, from_root(): return lax.psum(kept, axis)  176 us
    dot_general x2, matrix products, on_device(): lax.dot_general(diagonal_panel, all_rows, (((0,), (0,)), ((), ())), preci...  61.8 us
    all_gather x1, waiting for transfers between devices, on_device(): all_rows = lax.all_gather(design, 'rows', axis=0, tiled=True)  52.8 us
    scatter x1, local copies, waits for them, and re-layouts, on_device(): outbox = jnp.zeros((groups, slot_share, width_pts), jnp.float32).at[owner...  48.9 us
    scatter x1, local copies, waits for them, and re-layouts, on_device(): outbox_place = jnp.full((groups, slot_share), balanced, jnp.int32).at[own...  35.4 us
    all_gather x1, waiting for transfers between devices, on_device(): points = lax.all_gather(point_desc, 'rows', axis=1, tiled=True)  32.6 us
    add x1, other arithmetic, on_device(): gram_tile + jnp.where(row_ids[:, None] == col_ids[None, :], damping, 0.0)  24.1 us
    all_to_all x1, waiting for transfers between devices, on_device(): lax.all_to_all(outbox, 'rows', split_axis=0, concat_axis=0, tiled=True)  23.6 us
  transfers between devices with their start and end apart: 6, of which 4 were waited for; matrix products, arithmetic and copies ran while one was open for 23% of the time, Pallas kernels for 0%

commit v1 on v0

--- a/solution.py
+++ b/solution.py
@@ -1,9 +1,18 @@
+import functools
+
 import jax
 import jax.numpy as jnp
 from jax import lax
+from jax.experimental import pallas as pl
+from jax.experimental.pallas import tpu as pltpu
 from jax.sharding import PartitionSpec as P
 
 damping = 0.5
+CODE_TOP = 32700.0
+BOTH = ("rows", "pts")
+MIB = 1 << 20
+F32 = jnp.float32
+BF16 = jnp.bfloat16
 
 
 def from_root(value, axis, source):
@@ -32,7 +41,7 @@
     return pooled
 
 
-def on_device(env_desc, point_desc, pool_index, pool_count, pool_weight, row_dest):
+def on_any_device(env_desc, point_desc, pool_index, pool_count, pool_weight, row_dest):
     groups = lax.axis_size("rows")
     slot_total = pool_index.shape[0]
     balanced = slot_total // 2
@@ -92,6 +101,347 @@
     return (design, gram_tile)
 
 
+def dot_nn(a, b):
+    return lax.dot_general(a, b, (((1,), (0,)), ((), ())), preferred_element_type=F32)
+
+
+def dot_nt(a, b):
+    return lax.dot_general(a, b, (((1,), (1,)), ((), ())), preferred_element_type=F32)
+
+
+def split(value):
+    high = value.astype(BF16)
+    return high, (value - high.astype(F32)).astype(BF16)
+
+
+def encode(value, code_ref):
+    n = value.shape[0]
+    size = jnp.abs(value)
+    top = jnp.maximum(jnp.max(size, axis=0, keepdims=True), 1e-30)
+    exponent = jnp.ceil(jnp.log(top) * 1.4426950408889634)
+    root = jnp.sqrt(size * jnp.exp2(-exponent))
+    code = jnp.minimum(root * CODE_TOP + 0.5, 32767.0).astype(jnp.int32)
+    code_ref[pl.ds(0, n), :] = jnp.where(value < 0, -code, code).astype(jnp.int16)
+    pad = code_ref.shape[0] - n
+    code_ref[pl.ds(n, pad), :] = jnp.broadcast_to(
+        exponent.astype(jnp.int32), (pad, value.shape[1])
+    ).astype(jnp.int16)
+
+
+def lane_scale(exponent_rows, extra):
+    exponent = exponent_rows.astype(jnp.int32).astype(F32)[0:1, :]
+    return jnp.exp2(exponent) * (extra / (CODE_TOP * CODE_TOP))
+
+
+def decode(codes, scale):
+    root = codes.astype(jnp.int32).astype(F32)
+    return root * jnp.abs(root) * scale
+
+
+def weights_kernel(table_ref, high_ref, low_ref):
+    groups, rows, envs = high_ref.shape
+    table = table_ref[...]
+    slots = table.shape[0]
+    row_id = lax.broadcasted_iota(jnp.int32, (slots, rows), 1).astype(F32)
+    chosen = jnp.where(table[:, 8:9] == row_id, 1.0, 0.0)
+    by_row = lax.dot_general(
+        chosen,
+        table,
+        (((0,), (0,)), ((), ())),
+        precision=lax.Precision.HIGHEST,
+        preferred_element_type=F32,
+    )
+    env_id = lax.broadcasted_iota(jnp.int32, (rows, envs), 1).astype(F32)
+    index = jnp.floor(by_row + 0.5)
+    for group in range(groups):
+        ids = env_id + float(group * envs)
+        total = jnp.zeros((rows, envs), F32)
+        for member in range(4):
+            total = total + jnp.where(
+                index[:, member : member + 1] == ids, by_row[:, 4 + member : 5 + member], 0.0
+            )
+        high, low = split(total)
+        high_ref[group] = high
+        low_ref[group] = low
+
+
+def design_kernel(
+    at_ref,
+    own0,
+    own1,
+    own2,
+    own3,
+    swap0,
+    swap1,
+    swap2,
+    swap3,
+    cols_ref,
+    pan0,
+    pan1,
+    pan2,
+    pan3,
+    high_ref,
+    low_ref,
+    cols_code,
+    panel_code,
+    rows_out,
+    env,
+    pts,
+    cols_sum,
+    panel_sum,
+):
+    q, z, core = at_ref[0], at_ref[1], at_ref[2]
+    n_pts = cols_ref.shape[1]
+    comps = cols_ref.shape[2]
+    part = own0.shape[2]
+    tile = 256
+    for j in range(4):
+        pts[pl.ds(0, n_pts), pl.ds(j * comps, comps)] = cols_ref[j]
+    for t, ref in enumerate((pan0, pan1, pan2, pan3)):
+        at = pl.multiple_of(jnp.bitwise_xor(z, t) * comps, comps)
+        pts[pl.ds(n_pts, n_pts), pl.ds(at, comps)] = ref[...]
+    for d, (own, swap) in enumerate(
+        zip((own0, own1, own2, own3), (swap0, swap1, swap2, swap3))
+    ):
+        group = jnp.bitwise_xor(q, d)
+        for r in range(4):
+            base = jnp.bitwise_xor(z, r) * comps
+            mine = pl.multiple_of(base + core * part, part)
+            other = pl.multiple_of(base + (1 - core) * part, part)
+            env[:, pl.ds(mine, part)] = own[r]
+            env[:, pl.ds(other, part)] = swap[r]
+        features = env[...]
+        high, low = high_ref[group], low_ref[group]
+        scale = env.shape[1] ** (-0.5)
+        for i in range(n_pts // tile):
+            lanes = pl.ds(i * tile, tile)
+            s = dot_nt(features, pts[lanes, :]) * scale
+            s = s * s
+            k_high, k_low = split(0.25 * s * s)
+            part_sum = dot_nn(high, k_high) + dot_nn(high, k_low) + dot_nn(low, k_high)
+            cols_sum[:, lanes] = part_sum if d == 0 else cols_sum[:, lanes] + part_sum
+        for i in range(n_pts // tile):
+            rows = pl.ds(i * tile, tile)
+            s = dot_nt(pts[pl.ds(n_pts + i * tile, tile), :], features) * scale
+            s = s * s
+            k_high, k_low = split(0.25 * s * s)
+            part_sum = dot_nt(k_high, high) + dot_nt(k_low, high) + dot_nt(k_high, low)
+            panel_sum[rows, :] = part_sum if d == 0 else panel_sum[rows, :] + part_sum
+    encode(cols_sum[...], cols_code)
+    encode(panel_sum[...], panel_code)
+    share = rows_out.shape[0]
+    rows_out[...] = cols_sum[pl.ds(pl.multiple_of(q * share, share), share), :]
+
+
+def columns_kernel(at_ref, codes_ref, rows_ref, triple_ref, design_ref):
+    n = pl.program_id(0)
+    q = at_ref[0]
+    rows = triple_ref.shape[0] // 3
+    share = design_ref.shape[0]
+    scale = lane_scale(codes_ref[0, pl.ds(rows, 16), :], 1.0)
+    value = decode(codes_ref[0, pl.ds(0, rows), :], scale)
+    high, low = split(value)
+    triple_ref[pl.ds(0, rows), :] = high
+    triple_ref[pl.ds(rows, rows), :] = high
+    triple_ref[pl.ds(2 * rows, rows), :] = low
+
+    @pl.when(n == q)
+    def _():
+        design_ref[...] = rows_ref[...]
+
+    @pl.when(n != q)
+    def _():
+        start = pl.multiple_of(q * share, share)
+        design_ref[...] = decode(codes_ref[0, pl.ds(start, share), :], scale)
+
+
+def gram_kernel(at_ref, own_ref, swap_ref, triple_ref, *refs):
+    out_ref, left = refs[-2], refs[-1]
+    j = pl.program_id(0)
+    k, z, core, source = at_ref[0], at_ref[1], at_ref[2], at_ref[3]
+    n_pts = out_ref.shape[1]
+    rows = own_ref.shape[1]
+
+    @pl.when(j == 0)
+    def _():
+        for ref, side in ((own_ref, core), (swap_ref, 1 - core)):
+            scale = lane_scale(ref[pl.ds(n_pts, 16), :], 1.0 / rows)
+            high, low = split(decode(ref[pl.ds(0, n_pts), :], scale))
+            left[side, :, pl.ds(0, rows)] = high
+            left[side, :, pl.ds(rows, rows)] = low
+            left[side, :, pl.ds(2 * rows, rows)] = high
+
+    for side in range(2):
+        out_ref[side] = dot_nn(left[side], triple_ref[...])
+
+    @pl.when((k == z) & (j == source))
+    def _():
+        eye = lax.broadcasted_iota(jnp.int32, out_ref.shape[1:], 0) == lax.broadcasted_iota(
+            jnp.int32, out_ref.shape[1:], 1
+        )
+        out_ref[core] = out_ref[core] + jnp.where(eye, damping, 0.0)
+
+
+def whole(shape):
+    return pl.BlockSpec(shape, lambda *_: (0,) * len(shape))
+
+
+def on_device(env_desc, point_desc, pool_index, pool_count, pool_weight, row_dest):
+    groups, planes = 4, 4
+    q = lax.axis_index("rows")
+    p = lax.axis_index("pts")
+    z, core = p // 2, p % 2
+    at = jnp.stack([q, z, core, z]).astype(jnp.int32)
+    n_rows = pool_index.shape[0] * groups // 2
+    envs, part = env_desc.shape
+    n_pts = point_desc.shape[0] // planes
+    comps = point_desc.shape[1]
+    n_pool = pool_index.shape[1]
+    pad = n_rows + 16
+
+    def permutation(to):
+        return [
+            (r * 8 + s, to(r, s // 2, s % 2)[0] * 8 + to(r, s // 2, s % 2)[1] * 2 + to(r, s // 2, s % 2)[2])
+            for r in range(groups)
+            for s in range(planes * 2)
+        ]
+
+    def moved(value, to):
+        return lax.ppermute(value, BOTH, permutation(to))
+
+    along_x = lambda r, h, c: (r ^ 1, h, c)
+    along_y = lambda r, h, c: (r ^ 2, h, c)
+    to_core = lambda r, h, c: (r, h, 1 - c)
+    ring = (1, 3, 0, 2)
+    along_z = lambda r, h, c: (r, ring[h], c)
+
+    pair = jnp.stack([env_desc, moved(env_desc, lambda r, h, c: (r, h ^ 1, c))])
+    own = jnp.concatenate([pair, moved(pair, lambda r, h, c: (r, h ^ 2, c))])
+
+    quarters = point_desc.reshape(planes, n_pts, comps)
+    cols_pts = lax.all_to_all(quarters, "rows", 0, 0, tiled=True)
+    panel_pts = [
+        moved(
+            lax.dynamic_index_in_dim(quarters, q ^ t, 0, keepdims=False),
+            lambda r, h, c, t=t: (h, r ^ t, c),
+        )
+        for t in range(planes)
+    ]
+
+    members = jnp.arange(n_pool, dtype=jnp.int32)
+    live = jnp.where(members[None, :] < pool_count[:, None], pool_weight, 0.0)
+    table = jnp.concatenate(
+        [
+            (pool_index + q * envs).astype(F32),
+            live,
+            row_dest[:, None].astype(F32),
+            jnp.zeros((pool_index.shape[0], 7), F32),
+        ],
+        axis=1,
+    )
+    table = lax.all_gather(table, "rows", axis=0, tiled=True)
+    high, low = pl.pallas_call(
+        weights_kernel,
+        out_shape=[jax.ShapeDtypeStruct((groups, n_rows, envs), BF16)] * 2,
+        compiler_params=pltpu.CompilerParams(vmem_limit_bytes=48 * MIB),
+        name="pool_weights",
+    )(table)
+
+    from_x, from_y = moved(own, along_x), moved(own, along_y)
+    from_xy = jnp.concatenate([moved(from_x[:2], along_y), moved(from_y[2:], along_x)])
+    mine = (own, from_x, from_y, from_xy)
+    swapped = [moved(e, to_core) for e in mine]
+
+    env_spec = whole((planes, envs, part))
+    cols_code, panel_code, own_rows = pl.pallas_call(
+        design_kernel,
+        grid_spec=pltpu.PrefetchScalarGridSpec(
+            num_scalar_prefetch=1,
+            grid=(1,),
+            in_specs=[env_spec] * 8
+            + [whole((groups, n_pts, comps))]
+            + [whole((n_pts, comps))] * 4
+            + [whole((groups, n_rows, envs))] * 2,
+            out_specs=[
+                whole((pad, n_pts)),
+                whole((n_pts + 16, n_rows)),
+                whole((n_rows // groups, n_pts)),
+            ],
+            scratch_shapes=[
+                pltpu.VMEM((envs, groups * comps), BF16),
+                pltpu.VMEM((2 * n_pts, groups * comps), BF16),
+                pltpu.VMEM((n_rows, n_pts), F32),
+                pltpu.VMEM((n_pts, n_rows), F32),
+            ],
+        ),
+        out_shape=[
+            jax.ShapeDtypeStruct((pad, n_pts), jnp.int16),
+            jax.ShapeDtypeStruct((n_pts + 16, n_rows), jnp.int16),
+            jax.ShapeDtypeStruct((n_rows // groups, n_pts), F32),
+        ],
+        compiler_params=pltpu.CompilerParams(vmem_limit_bytes=56 * MIB),
+        name="design_values",
+    )(at, *mine, *swapped, cols_pts, *panel_pts, high, low)
+
+    codes = lax.all_to_all(
+        jnp.broadcast_to(cols_code[None], (groups, pad, n_pts)), "rows", 0, 0, tiled=True
+    )
+    width = groups * n_pts
+    triple, design = pl.pallas_call(
+        columns_kernel,
+        grid_spec=pltpu.PrefetchScalarGridSpec(
+            num_scalar_prefetch=1,
+            grid=(groups,),
+            in_specs=[
+                pl.BlockSpec((1, pad, n_pts), lambda n, _: (n, 0, 0)),
+                whole((n_rows // groups, n_pts)),
+            ],
+            out_specs=[
+                pl.BlockSpec((3 * n_rows, n_pts), lambda n, _: (0, n)),
+                pl.BlockSpec((n_rows // groups, n_pts), lambda n, _: (0, n)),
+            ],
+        ),
+        out_shape=[
+            jax.ShapeDtypeStruct((3 * n_rows, width), BF16),
+            jax.ShapeDtypeStruct((n_rows // groups, width), F32),
+        ],
+        compiler_params=pltpu.CompilerParams(vmem_limit_bytes=48 * MIB),
+        name="columns",
+    )(at, codes, own_rows)
+
+    held, source = panel_code, z
+    gram = None
+    for step in range(planes):
+        other = moved(held, to_core)
+        passed = moved(held, along_z) if step < planes - 1 else None
+        in_specs = [
+            whole((n_pts + 16, n_rows)),
+            whole((n_pts + 16, n_rows)),
+            pl.BlockSpec((3 * n_rows, n_pts), lambda j, _: (0, j)),
+        ]
+        operands = [jnp.stack([q, z, core, source]).astype(jnp.int32), held, other, triple]
+        if gram is not None:
+            in_specs.append(pl.BlockSpec(memory_space=pl.ANY))
+            operands.append(gram)
+        gram = pl.pallas_call(
+            gram_kernel,
+            grid_spec=pltpu.PrefetchScalarGridSpec(
+                num_scalar_prefetch=1,
+                grid=(groups,),
+                in_specs=in_specs,
+                out_specs=pl.BlockSpec((2, n_pts, n_pts), lambda j, s: (0, s[3], j)),
+                scratch_shapes=[pltpu.VMEM((2, n_pts, 3 * n_rows), BF16)],
+            ),
+            out_shape=jax.ShapeDtypeStruct((2, planes * n_pts, width), F32),
+            input_output_aliases={} if gram is None else {4: 0},
+            compiler_params=pltpu.CompilerParams(vmem_limit_bytes=48 * MIB),
+            name="gram_rows",
+        )(*operands)
+        held = passed
+        source = jnp.take(jnp.array([2, 0, 3, 1], jnp.int32), source)
+    return design, gram.reshape(2 * planes * n_pts, width)
+
+
 def solution(mesh):
     in_specs = (
         P("rows", "pts"),
@@ -102,6 +452,5 @@
         P("rows"),
     )
     out_specs = (P("rows", "pts"), P("rows", "pts"))
-    return jax.shard_map(
-        on_device, mesh=mesh, in_specs=in_specs, out_specs=out_specs, check_vma=False
-    )
+    body = on_device if dict(mesh.shape) == {"rows": 4, "pts": 8} else on_any_device
+    return jax.shard_map(body, mesh=mesh, in_specs=in_specs, out_specs=out_specs, check_vma=False)

time: 535 us -> 214 us (0.40)
  waiting for transfers between devices: 286 us -> 63.6 us
  local copies, waits for them, and re-layouts: 112 us -> 14 us
  Pallas kernels: 0 us -> 76.7 us
  matrix products: 68.7 us -> 0 us
  other arithmetic: 40.1 us -> 2.64 us
  starting transfers between devices: 12.2 us -> 43.2 us
  between operations: 13.9 us -> 2.73 us
  blocking collectives: 0 us -> 8.57 us
    psum x1 -> x0, waiting for transfers between devices: 176 us -> none  [from_root(): return lax.psum(kept, axis)]
    scatter x3 -> x0, local copies, waits for them, and re-layouts: 87.1 us -> none  [the longest x1 48.9 us: on_device(): outbox = jnp.zeros((groups, slot_share, width_pts), jnp.float32).at[owner...]
    all_gather x3 -> x0, waiting for transfers between devices: 85.4 us -> none  [the longest x1 52.8 us: on_device(): all_rows = lax.all_gather(design, 'rows', axis=0, tiled=True)]
    pallas_call x0 -> x7, Pallas kernels: none -> 76.7 us  [the longest x4 46.9 us: on_device(): pl.pallas_call(gram_kernel, grid_spec=pltpu.PrefetchScalarGridSpec(num_sc...]
    dot_general x3 -> x0, matrix products: 68.7 us -> none  [the longest x2 61.8 us: on_device(): lax.dot_general(diagonal_panel, all_rows, (((0,), (0,)), ((), ())), preci...]
    ppermute x0 -> x21, waiting for transfers between devices: none -> 63.6 us  [moved(): return lax.ppermute(value, BOTH, permutation(to))]
    ppermute x0 -> x21, starting transfers between devices: none -> 31.5 us  [moved(): return lax.ppermute(value, BOTH, permutation(to))]
    add x4 -> x0, other arithmetic: 28.9 us -> none  [the longest x1 24.1 us: on_device(): gram_tile + jnp.where(row_ids[:, None] == col_ids[None, :], damping, 0.0)]
  transfers between devices with their start and end apart: 6 -> 23, of which waited for: 4 -> 9; matrix products, arithmetic and copies ran while one was open for 23% -> 5% of each run, Pallas kernels for 0% -> 21%
where the time goes in v1:
time: 214 us; the launch traced here: 211 us
  Pallas kernels  76.7 us (36%)
  waiting for transfers between devices  63.6 us (30%)
  starting transfers between devices  43.2 us (20%)
  local copies, waits for them, and re-layouts  14 us (7%)
  blocking collectives  8.57 us (4%)
  between operations  2.73 us (1%)
  other arithmetic  2.64 us (1%)
    ppermute x21, waiting for transfers between devices, moved(): return lax.ppermute(value, BOTH, permutation(to))  63.6 us
    pallas_call x4, Pallas kernels, on_device(): pl.pallas_call(gram_kernel, grid_spec=pltpu.PrefetchScalarGridSpec(num_sc...  46.9 us
    ppermute x21, starting transfers between devices, moved(): return lax.ppermute(value, BOTH, permutation(to))  31.5 us
    pallas_call x1, Pallas kernels, on_device(): pl.pallas_call(design_kernel, grid_spec=pltpu.PrefetchScalarGridSpec(num_...  20.8 us
    all_gather x1, blocking collectives, on_device(): table = lax.all_gather(table, 'rows', axis=0, tiled=True)  8.57 us
    all_to_all x1, starting transfers between devices, on_device(): lax.all_to_all(jnp.broadcast_to(cols_code[None], (groups, pad, n_pts)), '...  8.15 us
    unnamed x31, local copies, waits for them, and re-layouts  5.61 us
    pallas_call x1, Pallas kernels, on_device(): pl.pallas_call(weights_kernel, out_shape=[jax.ShapeDtypeStruct((groups, n...  4.75 us
  transfers between devices with their start and end apart: 23, of which 9 were waited for; matrix products, arithmetic and copies ran while one was open for 5% of the time, Pallas kernels for 21%

profile of v1, /device:TPU:0, one launch (start us, length us, event | category | flops | bytes accessed | tf_op | source)
XLA Modules:
  0.0 211.4 jit_solution(15792299997002676236)
XLA Ops:
  0.7 3.1 %collective-permute-start = (bf16[512,128]{1,0:T(8,128)(2,1)}, bf16[512,128]{1,0:T(8,128)(2,1)S(1)}, u32[]{:S(2)}, u32[]{:S(2)}) collective-permute-start(bf16[512,128]{1,0:T(8,128)(2,1)} %param.9), channel_id=1, source_target_pairs={{0,2},{1,3},{2,0},{3,1},{4,6},{5,7},{6,4},{7,5},{8,10},{9,11},{10,... | collective-permute-start | bytes 393224 | tf_op jit(solution)/shard_map/ppermute | solution.py:310
  3.8 3.7 %collective-permute-done = bf16[512,128]{1,0:T(8,128)(2,1)S(1)} collective-permute-done((bf16[512,128]{1,0:T(8,128)(2,1)}, bf16[512,128]{1,0:T(8,128)(2,1)S(1)}, u32[]{:S(2)}, u32[]{:S(2)}) %collective-permute-start) | collective-permute-done | bytes 131104 | tf_op jit(solution)/shard_map/ppermute | solution.py:310
  7.5 0.9 pad_maximum_fusion.1
  8.4 2.8 %collective-permute-start.1 = (bf16[2,512,128]{2,1,0:T(8,128)(2,1)S(1)}, bf16[2,512,128]{2,1,0:T(8,128)(2,1)S(1)}, u32[]{:S(2)}, u32[]{:S(2)}) collective-permute-start(bf16[2,512,128]{2,1,0:T(8,128)(2,1)S(1)} %pad_maximum_fusion.1), channel_id=1, source_target_pairs={{0,4},{1,5},{2,6},{3,7},{4,0},{5,1},{6,2},{7,3},{8,12},{9,13},{10,... | collective-permute-start | bytes 786440 | tf_op jit(solution)/shard_map/ppermute | solution.py:310
  11.2 11.3 %collective-permute-done.1 = bf16[2,512,128]{2,1,0:T(8,128)(2,1)S(1)} collective-permute-done((bf16[2,512,128]{2,1,0:T(8,128)(2,1)S(1)}, bf16[2,512,128]{2,1,0:T(8,128)(2,1)S(1)}, u32[]{:S(2)}, u32[]{:S(2)}) %collective-permute-start.1) | collective-permute-done | bytes 262176 | tf_op jit(solution)/shard_map/ppermute | solution.py:310
  22.5 1.0 pad_maximum_fusion.own0
  23.5 1.4 collective-permute-start.2
  24.9 1.5 collective-permute-start.3
  26.4 3.5 %all-to-all-start = ((bf16[4,512,256]{2,1,0:T(8,128)(2,1)}), bf16[4,512,256]{2,1,0:T(8,128)(2,1)S(1)}, u32[]{:S(2)}, u32[]{:S(2)}) async-start(bf16[4,512,256]{2,1,0:T(8,128)(2,1)} %bitcast.22), calls=%async_computation | async-start | bytes 2097152 | tf_op jit(solution)/shard_map/all_to_all | solution.py:322
  29.9 2.1 dynamic-slice_bitcast_fusion
  32.0 3.6 %collective-permute-start.10 = (bf16[512,256]{1,0:T(8,128)(2,1)}, bf16[512,256]{1,0:T(8,128)(2,1)}, u32[]{:S(2)}, u32[]{:S(2)}) collective-permute-start(bf16[512,256]{1,0:T(8,128)(2,1)} %get-tuple-element.81), channel_id=1, source_target_pairs={{0,0},{1,1},{2,8},{3,9},{4,16},{5,17},{6,24},{7,25},{8,2},{9,3},{1... | collective-permute-start | bytes 786440 | tf_op jit(solution)/shard_map/ppermute | solution.py:310
  35.6 1.8 collective-permute-start.11
  37.4 1.0 collective-permute-start.12
  38.5 3.2 %collective-permute-start.4 = (bf16[2,512,128]{2,1,0:T(8,128)(2,1)S(1)}, bf16[2,512,128]{2,1,0:T(8,128)(2,1)}, u32[]{:S(2)}, u32[]{:S(2)}) collective-permute-start(bf16[2,512,128]{2,1,0:T(8,128)(2,1)S(1)} %slice.23), channel_id=1, source_target_pairs={{0,16},{1,17},{2,18},{3,19},{4,20},{5,21},{6,22},{7,23},{8,24},{9,... | collective-permute-start | bytes 786440 | tf_op jit(solution)/shard_map/ppermute | solution.py:310
  41.7 4.5 %collective-permute-done.3.own2 = bf16[4,512,128]{2,1,0:T(8,128)(2,1)S(1)} collective-permute-done((bf16[4,512,128]{2,1,0:T(8,128)(2,1)S(1)}, bf16[4,512,128]{2,1,0:T(8,128)(2,1)S(1)}, u32[]{:S(2)}, u32[]{:S(2)}) %collective-permute-start.3) | collective-permute-done | bytes 524320 | tf_op jit(solution)/shard_map/ppermute | solution.py:310
  46.2 0.8 slice.24
  47.0 4.0 %collective-permute-start.5 = (bf16[2,512,128]{2,1,0:T(8,128)(2,1)}, bf16[2,512,128]{2,1,0:T(8,128)(2,1)}, u32[]{:S(2)}, u32[]{:S(2)}) collective-permute-start(bf16[2,512,128]{2,1,0:T(8,128)(2,1)} %slice.24), channel_id=1, source_target_pairs={{0,8},{1,9},{2,10},{3,11},{4,12},{5,13},{6,14},{7,15},{8,0},{9,1},... | collective-permute-start | bytes 786440 | tf_op jit(solution)/shard_map/ppermute | solution.py:310
  51.0 0.6 dynamic-slice.12
  52.3 12.2 %collective-permute-done.4 = bf16[2,512,128]{2,1,0:T(8,128)(2,1)} collective-permute-done((bf16[2,512,128]{2,1,0:T(8,128)(2,1)S(1)}, bf16[2,512,128]{2,1,0:T(8,128)(2,1)}, u32[]{:S(2)}, u32[]{:S(2)}) %collective-permute-start.4) | collective-permute-done | bytes 262176 | tf_op jit(solution)/shard_map/ppermute | solution.py:310
  64.5 1.0 constant_dynamic-update-slice_fusion.1
  65.4 0.5 collective-permute-done.5
  66.0 1.0 constant_dynamic-update-slice_fusion.own3
  67.0 0.5 collective-permute-start.8
  67.5 0.1 collective-permute-start.9
  67.7 5.6 %collective-permute-start.13 = (bf16[512,256]{1,0:T(8,128)(2,1)}, bf16[512,256]{1,0:T(8,128)(2,1)}, u32[]{:S(2)}, u32[]{:S(2)}) collective-permute-start(bf16[512,256]{1,0:T(8,128)(2,1)} %get-tuple-element.78), channel_id=1, source_target_pairs={{0,6},{1,7},{2,14},{3,15},{4,22},{5,23},{6,30},{7,31},{8,4},{9,5},... | collective-permute-start | bytes 786440 | tf_op jit(solution)/shard_map/ppermute | solution.py:310
  73.4 0.6 dynamic-slice.13
  74.7 0.6 dynamic-slice.14
  75.3 8.6 %all_gather.3.table_ref = f32[1024,16]{1,0:T(8,128)S(1)} all-gather(f32[256,16]{1,0:T(8,128)S(1)} %copy.25), channel_id=1, replica_groups=mesh['rows'=4,'pts'=8] {'rows'}, dimensions={0}, use_global_device_ids=true | all-gather | bytes 81920 | tf_op jit(solution)/shard_map/all_gather | solution.py:342
  83.9 4.7 %pool_weights.1 = (bf16[4,512,512]{2,1,0:T(8,128)(2,1)S(1)}, bf16[4,512,512]{2,1,0:T(8,128)(2,1)S(1)}) custom-call(f32[1024,16]{1,0:T(8,128)S(1)} %all_gather.3.table_ref), custom_call_target="tpu_custom_call" | custom-call | tf_op jit(solution)/shard_map/pool_weights/pallas_call | solution.py:343
  88.7 1.3 copy-done
  90.0 1.3 copy-done.1
  92.0 0.6 pad_add_fusion.3
  92.7 0.9 copy-done.5
  93.6 20.8 %design_values.1 = (s16[528,512]{1,0:T(8,128)(2,1)}, s16[528,512]{1,0:T(8,128)(2,1)}, f32[128,512]{1,0:T(8,128)}) custom-call(s32[4]{0:T(128)} %get-tuple-element.84.at_ref, bf16[4,512,128]{2,1,0:T(8,128)(2,1)} %copy-done.6, bf16[4,512,128]{2,1,0:T(8,128)(2,1)} %copy-done.7, bf16[4,512,128]{2,1,0:T(8,128)(2,1)} %copy-done.8, bf16[4,512,128]{2,1,0:T(8,128)(2,1)} %copy-done.9, ...), custom_call_target="tpu_custom_call" | custom-call | tf_op jit(solution)/shard_map/design_values/pallas_call | solution.py:356
  114.3 0.6 collective-permute-start.14
  114.9 2.6 %broadcast_in_dim.28 = s16[4,528,512]{2,1,0:T(8,128)(2,1)} broadcast(s16[528,512]{1,0:T(8,128)(2,1)} %get-tuple-element.11), dimensions={1,2} | broadcast | bytes 2703360 | tf_op jit(solution)/shard_map/broadcast_in_dim | solution.py:387
  117.5 8.1 %all-to-all-start.1 = ((s16[4,528,512]{2,1,0:T(8,128)(2,1)}), s16[4,528,512]{2,1,0:T(8,128)(2,1)S(1)}, u32[]{:S(2)}, u32[]{:S(2)}) async-start(s16[4,528,512]{2,1,0:T(8,128)(2,1)} %broadcast_in_dim.28), calls=%async_computation.1 | async-start | bytes 4325376 | tf_op jit(solution)/shard_map/all_to_all | solution.py:386
  125.6 6.1 %collective-permute-done.14.own_ref = s16[528,512]{1,0:T(8,128)(2,1)S(1)} collective-permute-done((s16[528,512]{1,0:T(8,128)(2,1)}, s16[528,512]{1,0:T(8,128)(2,1)S(1)}, u32[]{:S(2)}, u32[]{:S(2)}) %collective-permute-start.14) | collective-permute-done | bytes 540704 | tf_op jit(solution)/shard_map/ppermute | solution.py:310
  131.8 1.7 collective-permute-start.15
  133.5 12.4 %collective-permute-done.15.own_ref = s16[528,512]{1,0:T(8,128)(2,1)} collective-permute-done((s16[528,512]{1,0:T(8,128)(2,1)S(1)}, s16[528,512]{1,0:T(8,128)(2,1)}, u32[]{:S(2)}, u32[]{:S(2)}) %collective-permute-start.15) | collective-permute-done | bytes 540704 | tf_op jit(solution)/shard_map/ppermute | solution.py:310
  145.9 0.5 collective-permute-start.19
  146.4 12.8 %collective-permute-done.16.own_ref = s16[528,512]{1,0:T(8,128)(2,1)S(1)} collective-permute-done((s16[528,512]{1,0:T(8,128)(2,1)}, s16[528,512]{1,0:T(8,128)(2,1)S(1)}, u32[]{:S(2)}, u32[]{:S(2)}) %collective-permute-start.16) | collective-permute-done | bytes 540704 | tf_op jit(solution)/shard_map/ppermute | solution.py:310
  159.2 4.3 %columns.1 = (bf16[1536,2048]{1,0:T(8,128)(2,1)}, f32[128,2048]{1,0:T(8,128)}) custom-call(s32[4]{0:T(128)S(1)} %copy-done.4, s16[4,528,512]{2,1,0:T(8,128)(2,1)S(1)} %all-to-all-done.1.codes_ref, f32[128,512]{1,0:T(8,128)S(1)} %copy-done.3), custom_call_target="tpu_custom_call" | custom-call | tf_op jit(solution)/shard_map/columns/pallas_call | solution.py:390
  163.5 1.0 copy-done.2
  164.6 11.7 %gram_rows.4.refs_0_ = f32[2,2048,2048]{2,1,0:T(8,128)} custom-call(s32[4]{0:T(128)S(1)} %copy-done.4, s16[528,512]{1,0:T(8,128)(2,1)S(1)} %copy-done.2, s16[528,512]{1,0:T(8,128)(2,1)} %collective-permute-done.20.swap_ref, bf16[1536,2048]{1,0:T(8,128)(2,1)} %get-tuple-element.15.triple_ref), custom_call_target="tpu_custom_call" | custom-call | tf_op jit(solution)/shard_map/gram_rows/pallas_call | solution.py:426
  176.3 11.6 %gram_rows.5.refs_0_ = f32[2,2048,2048]{2,1,0:T(8,128)} custom-call(s32[4]{0:T(128)S(1)} %get-tuple-element.76.at_ref, s16[528,512]{1,0:T(8,128)(2,1)S(1)} %collective-permute-done.14.own_ref, s16[528,512]{1,0:T(8,128)(2,1)} %collective-permute-done.19.swap_ref, bf16[1536,2048]{1,0:T(8,128)(2,1)} %get-tuple-element.15.triple_ref, ...), custom_call_target="tpu_custom_call", output_to_operand_aliasing={{}: (4, {})} | custom-call | tf_op jit(solution)/shard_map/gram_rows/pallas_call | solution.py:426
  187.9 11.9 %gram_rows.6.refs_0_ = f32[2,2048,2048]{2,1,0:T(8,128)} custom-call(s32[4]{0:T(128)S(1)} %get-tuple-element.82.at_ref, s16[528,512]{1,0:T(8,128)(2,1)} %collective-permute-done.15.own_ref, s16[528,512]{1,0:T(8,128)(2,1)} %collective-permute-done.18.swap_ref, bf16[1536,2048]{1,0:T(8,128)(2,1)} %get-tuple-element.15.triple_ref, ...), custom_call_target="tpu_custom_call", output_to_operand_aliasing={{}: (4, {})} | custom-call | tf_op jit(solution)/shard_map/gram_rows/pallas_call | solution.py:426
  199.8 11.7 %gram_rows.7 = f32[2,2048,2048]{2,1,0:T(8,128)} custom-call(s32[4]{0:T(128)S(1)} %get-tuple-element.83.at_ref, s16[528,512]{1,0:T(8,128)(2,1)S(1)} %collective-permute-done.16.own_ref, s16[528,512]{1,0:T(8,128)(2,1)} %collective-permute-done.17.swap_ref, bf16[1536,2048]{1,0:T(8,128)(2,1)} %get-tuple-element.15.triple_ref, ...), custom_call_target="tpu_custom_call", output_to_operand_aliasing={{}: (4, {})} | custom-call | tf_op jit(solution)/shard_map/gram_rows/pallas_call | solution.py:426
  (56 shorter events, 0.7 us)
Async XLA Ops:
  0.6 50.4 %copy-start.14 = (s32[4]{0:T(128)S(1)}, s32[4]{0:T(128)}, u32[]{:S(2)}) copy-start(s32[4]{0:T(128)} %constant.80.clone..sunk.6) | copy-start | bytes 52
  0.6 41.0 %copy-start.12 = (s32[256]{0:T(256)S(1)}, s32[256]{0:T(256)}, u32[]{:S(2)}) copy-start(s32[256]{0:T(256)} %param.12) | copy-start | bytes 3076
  0.7 41.0 %copy-start.10 = (f32[256,4]{0,1:T(4,128)S(1)}, f32[256,4]{0,1:T(4,128)}, u32[]{:S(2)}) copy-start(f32[256,4]{0,1:T(4,128)} %param.13) | copy-start | bytes 12292
  0.7 50.4 %copy-start.11 = (s32[256,4]{0,1:T(4,128)S(1)}, s32[256,4]{0,1:T(4,128)}, u32[]{:S(2)}) copy-start(s32[256,4]{0,1:T(4,128)} %param.11) | copy-start | bytes 12292
  0.7 51.0 %copy-start.13 = (s32[256]{0:T(256)S(1)}, s32[256]{0:T(256)}, u32[]{:S(2)}) copy-start(s32[256]{0:T(256)} %param.14) | copy-start | bytes 3076
  0.7 6.8 %collective-permute-start = (bf16[512,128]{1,0:T(8,128)(2,1)}, bf16[512,128]{1,0:T(8,128)(2,1)S(1)}, u32[]{:S(2)}, u32[]{:S(2)}) collective-permute-start(bf16[512,128]{1,0:T(8,128)(2,1)} %param.9), channel_id=1, source_target_pairs={{0,2},{1,3},{2,0},{3,1},{4,6},{5,7},{6,4},{7,5},{8,10},{9,11},{10,... | collective-permute-start | bytes 393224 | tf_op jit(solution)/shard_map/ppermute | solution.py:310
  8.4 14.1 %collective-permute-start.1 = (bf16[2,512,128]{2,1,0:T(8,128)(2,1)S(1)}, bf16[2,512,128]{2,1,0:T(8,128)(2,1)S(1)}, u32[]{:S(2)}, u32[]{:S(2)}) collective-permute-start(bf16[2,512,128]{2,1,0:T(8,128)(2,1)S(1)} %pad_maximum_fusion.1), channel_id=1, source_target_pairs={{0,4},{1,5},{2,6},{3,7},{4,0},{5,1},{6,2},{7,3},{8,12},{9,13},{10,... | collective-permute-start | bytes 786440 | tf_op jit(solution)/shard_map/ppermute | solution.py:310
  23.4 69.2 %copy-start.6 = (bf16[4,512,128]{2,1,0:T(8,128)(2,1)}, bf16[4,512,128]{2,1,0:T(8,128)(2,1)S(1)}, u32[]{:S(2)}) copy-start(bf16[4,512,128]{2,1,0:T(8,128)(2,1)S(1)} %pad_maximum_fusion.own0) | copy-start | bytes 1572868
  23.5 15.0 %collective-permute-start.2 = (bf16[4,512,128]{2,1,0:T(8,128)(2,1)S(1)}, bf16[4,512,128]{2,1,0:T(8,128)(2,1)S(1)}, u32[]{:S(2)}, u32[]{:S(2)}) collective-permute-start(bf16[4,512,128]{2,1,0:T(8,128)(2,1)S(1)} %pad_maximum_fusion.own0), channel_id=1, source_target_pairs={{0,8},{1,9},{2,10},{3,11},{4,12},{5,13},{6,14},{7,15},{8,0},{9,1},... | collective-permute-start | bytes 1572872 | tf_op jit(solution)/shard_map/ppermute | solution.py:310
  24.9 21.4 %collective-permute-start.3 = (bf16[4,512,128]{2,1,0:T(8,128)(2,1)S(1)}, bf16[4,512,128]{2,1,0:T(8,128)(2,1)S(1)}, u32[]{:S(2)}, u32[]{:S(2)}) collective-permute-start(bf16[4,512,128]{2,1,0:T(8,128)(2,1)S(1)} %pad_maximum_fusion.own0), channel_id=1, source_target_pairs={{0,16},{1,17},{2,18},{3,19},{4,20},{5,21},{6,22},{7,23},{8,24},{9,... | collective-permute-start | bytes 1572872 | tf_op jit(solution)/shard_map/ppermute | solution.py:310
  26.4 66.2 %all-to-all-start = ((bf16[4,512,256]{2,1,0:T(8,128)(2,1)}), bf16[4,512,256]{2,1,0:T(8,128)(2,1)S(1)}, u32[]{:S(2)}, u32[]{:S(2)}) async-start(bf16[4,512,256]{2,1,0:T(8,128)(2,1)} %bitcast.22), calls=%async_computation | async-start | bytes 2097152 | tf_op jit(solution)/shard_map/all_to_all | solution.py:322
  32.0 35.0 %collective-permute-start.10 = (bf16[512,256]{1,0:T(8,128)(2,1)}, bf16[512,256]{1,0:T(8,128)(2,1)}, u32[]{:S(2)}, u32[]{:S(2)}) collective-permute-start(bf16[512,256]{1,0:T(8,128)(2,1)} %get-tuple-element.81), channel_id=1, source_target_pairs={{0,0},{1,1},{2,8},{3,9},{4,16},{5,17},{6,24},{7,25},{8,2},{9,3},{1... | collective-permute-start | bytes 786440 | tf_op jit(solution)/shard_map/ppermute | solution.py:310
  35.6 31.9 %collective-permute-start.11 = (bf16[512,256]{1,0:T(8,128)(2,1)}, bf16[512,256]{1,0:T(8,128)(2,1)}, u32[]{:S(2)}, u32[]{:S(2)}) collective-permute-start(bf16[512,256]{1,0:T(8,128)(2,1)} %get-tuple-element.80), channel_id=1, source_target_pairs={{0,2},{1,3},{2,10},{3,11},{4,18},{5,19},{6,26},{7,27},{8,0},{9,1},... | collective-permute-start | bytes 786440 | tf_op jit(solution)/shard_map/ppermute | solution.py:310
  37.4 30.3 %collective-permute-start.12 = (bf16[512,256]{1,0:T(8,128)(2,1)S(1)}, bf16[512,256]{1,0:T(8,128)(2,1)}, u32[]{:S(2)}, u32[]{:S(2)}) collective-permute-start(bf16[512,256]{1,0:T(8,128)(2,1)S(1)} %get-tuple-element.79), channel_id=1, source_target_pairs={{0,4},{1,5},{2,12},{3,13},{4,20},{5,21},{6,28},{7,29},{8,6},{9,7},... | collective-permute-start | bytes 786440 | tf_op jit(solution)/shard_map/ppermute | solution.py:310
  38.4 54.2 %copy-start.7 = (bf16[4,512,128]{2,1,0:T(8,128)(2,1)}, bf16[4,512,128]{2,1,0:T(8,128)(2,1)S(1)}, u32[]{:S(2)}) copy-start(bf16[4,512,128]{2,1,0:T(8,128)(2,1)S(1)} %collective-permute-done.2.own1) | copy-start | bytes 1572868
  38.5 26.0 %collective-permute-start.4 = (bf16[2,512,128]{2,1,0:T(8,128)(2,1)S(1)}, bf16[2,512,128]{2,1,0:T(8,128)(2,1)}, u32[]{:S(2)}, u32[]{:S(2)}) collective-permute-start(bf16[2,512,128]{2,1,0:T(8,128)(2,1)S(1)} %slice.23), channel_id=1, source_target_pairs={{0,16},{1,17},{2,18},{3,19},{4,20},{5,21},{6,22},{7,23},{8,24},{9,... | collective-permute-start | bytes 786440 | tf_op jit(solution)/shard_map/ppermute | solution.py:310
  46.2 46.4 %copy-start.8 = (bf16[4,512,128]{2,1,0:T(8,128)(2,1)}, bf16[4,512,128]{2,1,0:T(8,128)(2,1)S(1)}, u32[]{:S(2)}) copy-start(bf16[4,512,128]{2,1,0:T(8,128)(2,1)S(1)} %collective-permute-done.3.own2) | copy-start | bytes 1572868
  47.0 18.9 %collective-permute-start.5 = (bf16[2,512,128]{2,1,0:T(8,128)(2,1)}, bf16[2,512,128]{2,1,0:T(8,128)(2,1)}, u32[]{:S(2)}, u32[]{:S(2)}) collective-permute-start(bf16[2,512,128]{2,1,0:T(8,128)(2,1)} %slice.24), channel_id=1, source_target_pairs={{0,8},{1,9},{2,10},{3,11},{4,12},{5,13},{6,14},{7,15},{8,0},{9,1},... | collective-permute-start | bytes 786440 | tf_op jit(solution)/shard_map/ppermute | solution.py:310
  64.5 28.1 %collective-permute-start.6 = (bf16[4,512,128]{2,1,0:T(8,128)(2,1)S(1)}, bf16[4,512,128]{2,1,0:T(8,128)(2,1)}, u32[]{:S(2)}, u32[]{:S(2)}) collective-permute-start(bf16[4,512,128]{2,1,0:T(8,128)(2,1)S(1)} %pad_maximum_fusion.own0), channel_id=1, source_target_pairs={{0,1},{1,0},{2,3},{3,2},{4,5},{5,4},{6,7},{7,6},{8,9},{9,8},{10,11... | collective-permute-start | bytes 1572872 | tf_op jit(solution)/shard_map/ppermute | solution.py:310
  65.9 26.7 %collective-permute-start.7 = (bf16[4,512,128]{2,1,0:T(8,128)(2,1)S(1)}, bf16[4,512,128]{2,1,0:T(8,128)(2,1)}, u32[]{:S(2)}, u32[]{:S(2)}) collective-permute-start(bf16[4,512,128]{2,1,0:T(8,128)(2,1)S(1)} %collective-permute-done.2.own1), channel_id=1, source_target_pairs={{0,1},{1,0},{2,3},{3,2},{4,5},{5,4},{6,7},{7,6},{8,9},{9,8},{10,11... | collective-permute-start | bytes 1572872 | tf_op jit(solution)/shard_map/ppermute | solution.py:310
  67.0 25.6 %copy-start.9 = (bf16[4,512,128]{2,1,0:T(8,128)(2,1)}, bf16[4,512,128]{2,1,0:T(8,128)(2,1)S(1)}, u32[]{:S(2)}) copy-start(bf16[4,512,128]{2,1,0:T(8,128)(2,1)S(1)} %constant_dynamic-update-slice_fusion.own3) | copy-start | bytes 1572868
  67.0 25.6 %collective-permute-start.8 = (bf16[4,512,128]{2,1,0:T(8,128)(2,1)S(1)}, bf16[4,512,128]{2,1,0:T(8,128)(2,1)}, u32[]{:S(2)}, u32[]{:S(2)}) collective-permute-start(bf16[4,512,128]{2,1,0:T(8,128)(2,1)S(1)} %collective-permute-done.3.own2), channel_id=1, source_target_pairs={{0,1},{1,0},{2,3},{3,2},{4,5},{5,4},{6,7},{7,6},{8,9},{9,8},{10,11... | collective-permute-start | bytes 1572872 | tf_op jit(solution)/shard_map/ppermute | solution.py:310
  67.5 25.1 %collective-permute-start.9 = (bf16[4,512,128]{2,1,0:T(8,128)(2,1)S(1)}, bf16[4,512,128]{2,1,0:T(8,128)(2,1)}, u32[]{:S(2)}, u32[]{:S(2)}) collective-permute-start(bf16[4,512,128]{2,1,0:T(8,128)(2,1)S(1)} %constant_dynamic-update-slice_fusion.own3), channel_id=1, source_target_pairs={{0,1},{1,0},{2,3},{3,2},{4,5},{5,4},{6,7},{7,6},{8,9},{9,8},{10,11... | collective-permute-start | bytes 1572872 | tf_op jit(solution)/shard_map/ppermute | solution.py:310
  67.7 24.9 %collective-permute-start.13 = (bf16[512,256]{1,0:T(8,128)(2,1)}, bf16[512,256]{1,0:T(8,128)(2,1)}, u32[]{:S(2)}, u32[]{:S(2)}) collective-permute-start(bf16[512,256]{1,0:T(8,128)(2,1)} %get-tuple-element.78), channel_id=1, source_target_pairs={{0,6},{1,7},{2,14},{3,15},{4,22},{5,23},{6,30},{7,31},{8,4},{9,5},... | collective-permute-start | bytes 786440 | tf_op jit(solution)/shard_map/ppermute | solution.py:310
  88.7 1.3 copy-start
  90.0 1.4 copy-start.1
  92.6 1.0 copy-start.5
  93.6 65.7 %copy-start.4 = (s32[4]{0:T(128)S(1)}, s32[4]{0:T(128)}, u32[]{:S(2)}) copy-start(s32[4]{0:T(128)} %get-tuple-element.84.at_ref) | copy-start | bytes 52
  114.3 44.9 %copy-start.3 = (f32[128,512]{1,0:T(8,128)S(1)}, f32[128,512]{1,0:T(8,128)}, u32[]{:S(2)}) copy-start(f32[128,512]{1,0:T(8,128)} %get-tuple-element.12.rows_ref) | copy-start | bytes 786436
  114.3 17.4 %collective-permute-start.14 = (s16[528,512]{1,0:T(8,128)(2,1)}, s16[528,512]{1,0:T(8,128)(2,1)S(1)}, u32[]{:S(2)}, u32[]{:S(2)}) collective-permute-start(s16[528,512]{1,0:T(8,128)(2,1)} %get-tuple-element.14.own_ref), channel_id=1, source_target_pairs={{0,2},{1,3},{2,6},{3,7},{4,0},{5,1},{6,4},{7,5},{8,10},{9,11},{10,... | collective-permute-start | bytes 1622024 | tf_op jit(solution)/shard_map/ppermute | solution.py:310
  117.5 41.7 %all-to-all-start.1 = ((s16[4,528,512]{2,1,0:T(8,128)(2,1)}), s16[4,528,512]{2,1,0:T(8,128)(2,1)S(1)}, u32[]{:S(2)}, u32[]{:S(2)}) async-start(s16[4,528,512]{2,1,0:T(8,128)(2,1)} %broadcast_in_dim.28), calls=%async_computation.1 | async-start | bytes 4325376 | tf_op jit(solution)/shard_map/all_to_all | solution.py:386
  131.8 14.1 %collective-permute-start.15 = (s16[528,512]{1,0:T(8,128)(2,1)S(1)}, s16[528,512]{1,0:T(8,128)(2,1)}, u32[]{:S(2)}, u32[]{:S(2)}) collective-permute-start(s16[528,512]{1,0:T(8,128)(2,1)S(1)} %collective-permute-done.14.own_ref), channel_id=1, source_target_pairs={{0,2},{1,3},{2,6},{3,7},{4,0},{5,1},{6,4},{7,5},{8,10},{9,11},{10,... | collective-permute-start | bytes 1622024 | tf_op jit(solution)/shard_map/ppermute | solution.py:310
  145.9 13.3 %collective-permute-start.16 = (s16[528,512]{1,0:T(8,128)(2,1)}, s16[528,512]{1,0:T(8,128)(2,1)S(1)}, u32[]{:S(2)}, u32[]{:S(2)}) collective-permute-start(s16[528,512]{1,0:T(8,128)(2,1)} %collective-permute-done.15.own_ref), channel_id=1, source_target_pairs={{0,2},{1,3},{2,6},{3,7},{4,0},{5,1},{6,4},{7,5},{8,10},{9,11},{10,... | collective-permute-start | bytes 1622024 | tf_op jit(solution)/shard_map/ppermute | solution.py:310
  145.9 17.6 %collective-permute-start.20 = (s16[528,512]{1,0:T(8,128)(2,1)}, s16[528,512]{1,0:T(8,128)(2,1)}, u32[]{:S(2)}, u32[]{:S(2)}) collective-permute-start(s16[528,512]{1,0:T(8,128)(2,1)} %get-tuple-element.14.own_ref), channel_id=1, source_target_pairs={{0,1},{1,0},{2,3},{3,2},{4,5},{5,4},{6,7},{7,6},{8,9},{9,8},{10,11... | collective-permute-start | bytes 1622024 | tf_op jit(solution)/shard_map/ppermute | solution.py:310
  145.9 30.4 %collective-permute-start.19 = (s16[528,512]{1,0:T(8,128)(2,1)S(1)}, s16[528,512]{1,0:T(8,128)(2,1)}, u32[]{:S(2)}, u32[]{:S(2)}) collective-permute-start(s16[528,512]{1,0:T(8,128)(2,1)S(1)} %collective-permute-done.14.own_ref), channel_id=1, source_target_pairs={{0,1},{1,0},{2,3},{3,2},{4,5},{5,4},{6,7},{7,6},{8,9},{9,8},{10,11... | collective-permute-start | bytes 1622024 | tf_op jit(solution)/shard_map/ppermute | solution.py:310
  146.4 41.5 %collective-permute-start.18 = (s16[528,512]{1,0:T(8,128)(2,1)}, s16[528,512]{1,0:T(8,128)(2,1)}, u32[]{:S(2)}, u32[]{:S(2)}) collective-permute-start(s16[528,512]{1,0:T(8,128)(2,1)} %collective-permute-done.15.own_ref), channel_id=1, source_target_pairs={{0,1},{1,0},{2,3},{3,2},{4,5},{5,4},{6,7},{7,6},{8,9},{9,8},{10,11... | collective-permute-start | bytes 1622024 | tf_op jit(solution)/shard_map/ppermute | solution.py:310
  159.2 40.6 %collective-permute-start.17 = (s16[528,512]{1,0:T(8,128)(2,1)S(1)}, s16[528,512]{1,0:T(8,128)(2,1)}, u32[]{:S(2)}, u32[]{:S(2)}) collective-permute-start(s16[528,512]{1,0:T(8,128)(2,1)S(1)} %collective-permute-done.16.own_ref), channel_id=1, source_target_pairs={{0,1},{1,0},{2,3},{3,2},{4,5},{5,4},{6,7},{7,6},{8,9},{9,8},{10,11... | collective-permute-start | bytes 1622024 | tf_op jit(solution)/shard_map/ppermute | solution.py:310
  163.5 1.0 copy-start.2

commit v2 on v0

--- a/solution.py
+++ b/solution.py
@@ -1,9 +1,19 @@
+import functools
+
 import jax
 import jax.numpy as jnp
 from jax import lax
+from jax.experimental import pallas as pl
+from jax.experimental.pallas import tpu as pltpu
 from jax.sharding import PartitionSpec as P
 
 damping = 0.5
+CODE_TOP = 32700.0
+BOTH = ("rows", "pts")
+MIB = 1 << 20
+VMEM_LIMIT = 63 * MIB
+F32 = jnp.float32
+BF16 = jnp.bfloat16
 
 
 def from_root(value, axis, source):
@@ -32,7 +42,7 @@
     return pooled
 
 
-def on_device(env_desc, point_desc, pool_index, pool_count, pool_weight, row_dest):
+def on_any_device(env_desc, point_desc, pool_index, pool_count, pool_weight, row_dest):
     groups = lax.axis_size("rows")
     slot_total = pool_index.shape[0]
     balanced = slot_total // 2
@@ -92,6 +102,473 @@
     return (design, gram_tile)
 
 
+def dot_nn(a, b):
+    return lax.dot_general(a, b, (((1,), (0,)), ((), ())), preferred_element_type=F32)
+
+
+def dot_nt(a, b):
+    return lax.dot_general(a, b, (((1,), (1,)), ((), ())), preferred_element_type=F32)
+
+
+def split(value):
+    high = value.astype(BF16)
+    return high, (value - high.astype(F32)).astype(BF16)
+
+
+def encode(value, code_ref):
+    n = value.shape[0]
+    size = jnp.abs(value)
+    top = jnp.maximum(jnp.max(size, axis=0, keepdims=True), 1e-30)
+    exponent = jnp.ceil(jnp.log(top) * 1.4426950408889634)
+    root = jnp.sqrt(size * jnp.exp2(-exponent))
+    code = jnp.minimum(root * CODE_TOP + 0.5, 32767.0).astype(jnp.int32)
+    code_ref[pl.ds(0, n), :] = jnp.where(value < 0, -code, code).astype(jnp.int16)
+    pad = code_ref.shape[0] - n
+    code_ref[pl.ds(n, pad), :] = jnp.broadcast_to(
+        exponent.astype(jnp.int32), (pad, value.shape[1])
+    ).astype(jnp.int16)
+
+
+def lane_scale(exponent_rows, extra):
+    exponent = exponent_rows.astype(jnp.int32).astype(F32)[0:1, :]
+    return jnp.exp2(exponent) * (extra / (CODE_TOP * CODE_TOP))
+
+
+def decode(codes, scale):
+    root = codes.astype(jnp.int32).astype(F32)
+    return root * jnp.abs(root) * scale
+
+
+def weights_kernel(table_ref, high_ref, low_ref):
+    groups, rows, envs = high_ref.shape
+    shares = []
+    for g in range(groups):
+        piece = table_ref[g].astype(F32)
+        index = piece[0:4] * 256.0 + piece[4:8] + float(g * envs)
+        weight = piece[8:12] + piece[12:16] + piece[16:20]
+        place = piece[20:21] * 256.0 + piece[21:22] - 1.0
+        shares.append(jnp.concatenate([index, weight, place], axis=0))
+    table = jnp.concatenate(shares, axis=1)
+    slots = table.shape[1]
+    row_id = lax.broadcasted_iota(jnp.int32, (rows, slots), 0).astype(F32)
+    chosen = jnp.where(table[8:9, :] == row_id, 1.0, 0.0)
+    by_row = lax.dot_general(
+        chosen,
+        table,
+        (((1,), (1,)), ((), ())),
+        precision=lax.Precision.HIGHEST,
+        preferred_element_type=F32,
+    )
+    env_id = lax.broadcasted_iota(jnp.int32, (rows, envs), 1).astype(F32)
+    index = jnp.floor(by_row + 0.5)
+    for group in range(groups):
+        ids = env_id + float(group * envs)
+        total = jnp.zeros((rows, envs), F32)
+        for member in range(4):
+            total = total + jnp.where(
+                index[:, member : member + 1] == ids, by_row[:, 4 + member : 5 + member], 0.0
+            )
+        high, low = split(total)
+        high_ref[group] = high
+        low_ref[group] = low
+
+
+def fourth_power(products, scale):
+    s = products * scale
+    s = s * s
+    return split(0.25 * s * s)
+
+
+def add_columns(features, weights, pts, total, first):
+    high, low = weights[0], weights[1]
+    k_high, k_low = fourth_power(dot_nt(features, pts[...]), features.shape[1] ** (-0.5))
+    part = dot_nn(high, k_high) + dot_nn(high, k_low) + dot_nn(low, k_high)
+    total[...] = part if first else total[...] + part
+
+
+def add_panel(features, weights, pts, total, first):
+    high, low = weights[0], weights[1]
+    k_high, k_low = fourth_power(dot_nt(pts[...], features), features.shape[1] ** (-0.5))
+    part = dot_nt(k_high, high) + dot_nt(k_low, high) + dot_nt(k_high, low)
+    total[...] = part if first else total[...] + part
+
+
+def started(copies):
+    for copy in copies:
+        copy.start()
+    return copies
+
+
+def waited(copies):
+    for copy in copies:
+        copy.wait()
+
+
+def group_copies(at_ref, group, mine, swapped, high, low, env, weights, sems):
+    z, core = at_ref[1], at_ref[2]
+    part = mine.shape[3]
+    out = []
+    for side, ref in ((core, mine), (1 - core, swapped)):
+        for r in range(4):
+            at = pl.multiple_of((jnp.bitwise_xor(z, r) * 2 + side) * part, part)
+            to = env.at[:, pl.ds(at, part)]
+            out.append(pltpu.make_async_copy(ref.at[group, r], to, sems.at[len(out)]))
+    for i, ref in enumerate((high, low)):
+        out.append(pltpu.make_async_copy(ref.at[group], weights.at[i], sems.at[8 + i]))
+    return out
+
+
+def design_kernel(
+    at_ref, mine, swapped, cols, pan0, pan1, pan2, pan3, high, low,
+    cols_code, panel_code, rows_out,
+    cols_pts, panel_pts, env, weights, cols_sum, panel_sum, point_sems, group_sems,
+):
+    q, z = at_ref[0], at_ref[1]
+    n_pts, comps = pan0.shape
+    points = []
+    for j in range(4):
+        to = cols_pts.at[:, pl.ds(j * comps, comps)]
+        source = cols.at[j, pl.ds(0, n_pts)]
+        points.append(pltpu.make_async_copy(source, to, point_sems.at[j]))
+    started(points)
+    copies = [
+        group_copies(at_ref, d, mine, swapped, high, low, env.at[d], weights.at[d], group_sems.at[d])
+        for d in range(4)
+    ]
+    started(copies[0])
+    panel = []
+    for t, ref in enumerate((pan0, pan1, pan2, pan3)):
+        at = pl.multiple_of(jnp.bitwise_xor(z, t) * comps, comps)
+        to = panel_pts.at[:, pl.ds(at, comps)]
+        panel.append(pltpu.make_async_copy(ref, to, point_sems.at[4 + t]))
+    started(panel)
+    for d in range(1, 4):
+        started(copies[d])
+    waited(points)
+    for d in range(4):
+        waited(copies[d])
+        add_columns(env[d], weights.at[d], cols_pts, cols_sum, d == 0)
+        if d == 0:
+            waited(panel)
+        add_panel(env[d], weights.at[d], panel_pts, panel_sum, d == 0)
+    encode(cols_sum[...], cols_code)
+    share = rows_out.shape[0]
+    rows_out[...] = cols_sum[pl.ds(pl.multiple_of(q * share, share), share), :]
+    encode(panel_sum[...], panel_code)
+
+
+def value_pair(codes, scale, out):
+    rows = out.shape[0] // 2
+    high, low = split(decode(codes, scale))
+    out[pl.ds(0, rows), :] = high
+    out[pl.ds(rows, rows), :] = low
+
+
+def near_columns_kernel(code0, code1, code2, out_ref):
+    rows = out_ref.shape[1] // 2
+    for d, ref in enumerate((code0, code1, code2)):
+
+        @pl.when(pl.program_id(0) == d)
+        def _():
+            value_pair(ref[pl.ds(0, rows), :], lane_scale(ref[pl.ds(rows, 16), :], 1.0), out_ref.at[0])
+
+
+def far_columns_kernel(at_ref, rows_ref, code1, code2, upper, lower, out_ref, design_ref):
+    q = at_ref[0]
+    rows = out_ref.shape[1] // 2
+    half, share, n_pts = upper.shape[0], rows_ref.shape[0], rows_ref.shape[1]
+    scale = lane_scale(lower[pl.ds(rows - half, 16), :], 1.0)
+    codes = jnp.concatenate([upper[...], lower[pl.ds(0, rows - half), :]], axis=0)
+    value_pair(codes, scale, out_ref.at[0])
+    start = pl.multiple_of(q * share, share)
+
+    def put(d, value):
+        at = pl.multiple_of(jnp.bitwise_xor(q, d) * n_pts, n_pts)
+        design_ref[:, pl.ds(at, n_pts)] = value
+
+    put(0, rows_ref[...])
+    for d, ref in ((1, code1), (2, code2)):
+        put(d, decode(ref[pl.ds(start, share), :], lane_scale(ref[pl.ds(rows, 16), :], 1.0)))
+
+    @pl.when(start < half)
+    def _():
+        put(3, decode(upper[pl.ds(start, share), :], scale))
+
+    @pl.when(start >= half)
+    def _():
+        put(3, decode(lower[pl.ds(pl.multiple_of(start - half, share), share), :], scale))
+
+
+def gray(value):
+    return jnp.bitwise_xor(value, lax.shift_right_logical(value, 1))
+
+
+def ring_source(z, steps):
+    return gray(jnp.bitwise_and(gray(z) - steps, 3))
+
+
+def gram_kernel(steps, first, n_near, at_ref, *refs):
+    n_codes = 2 * len(steps)
+    codes, value_refs, out_ref, left = refs[:n_codes], refs[n_codes:-2], refs[-2], refs[-1]
+    n, j = pl.program_id(0), pl.program_id(1)
+    k, z, core = at_ref[0], at_ref[1], at_ref[2]
+    source = ring_source(z, steps[0] + n)
+    n_pts = out_ref.shape[1]
+    rows = codes[0].shape[1]
+    for i in range(len(steps)):
+
+        @pl.when((j == 0) & (n == i))
+        def _():
+            for ref, side in ((codes[2 * i], core), (codes[2 * i + 1], 1 - core)):
+                scale = lane_scale(ref[pl.ds(n_pts, 16), :], 1.0 / rows)
+                high, low = split(decode(ref[pl.ds(0, n_pts), :], scale))
+                left[side, :, pl.ds(0, rows)] = high
+                left[side, :, pl.ds(rows, rows)] = low
+
+    def multiply(pair_ref):
+        for side in range(2):
+            high, low = left[side, :, pl.ds(0, rows)], left[side, :, pl.ds(rows, rows)]
+            top, rest = pair_ref[0, pl.ds(0, rows), :], pair_ref[0, pl.ds(rows, rows), :]
+            out_ref[side] = dot_nn(high, top) + dot_nn(low, top) + dot_nn(high, rest)
+
+    if first == 0 and n_near < 4:
+        multiply(value_refs[0])
+    elif first == 3:
+        multiply(value_refs[0])
+    else:
+        pl.when(j < 3)(lambda: multiply(value_refs[0]))
+        pl.when(j == 3)(lambda: multiply(value_refs[1]))
+
+    @pl.when((k == z) & (jnp.bitwise_xor(k, first + j) == source))
+    def _():
+        eye = lax.broadcasted_iota(jnp.int32, out_ref.shape[1:], 0) == lax.broadcasted_iota(
+            jnp.int32, out_ref.shape[1:], 1
+        )
+        out_ref[core] = out_ref[core] + jnp.where(eye, damping, 0.0)
+
+
+def cost(multiply_adds, nbytes):
+    return pl.CostEstimate(flops=2 * multiply_adds, bytes_accessed=nbytes, transcendentals=0)
+
+
+def whole(shape):
+    return pl.BlockSpec(shape, lambda *_: (0,) * len(shape))
+
+
+def on_device(env_desc, point_desc, pool_index, pool_count, pool_weight, row_dest):
+    groups, planes = 4, 4
+    q = lax.axis_index("rows")
+    p = lax.axis_index("pts")
+    z, core = p // 2, p % 2
+    at = jnp.stack([q, z, core]).astype(jnp.int32)
+    n_rows = pool_index.shape[0] * groups // 2
+    envs, part = env_desc.shape
+    n_pts = point_desc.shape[0] // planes
+    comps = point_desc.shape[1]
+    n_pool = pool_index.shape[1]
+    pad = n_rows + 16
+
+    def permutation(to):
+        return [
+            (r * 8 + s, to(r, s // 2, s % 2)[0] * 8 + to(r, s // 2, s % 2)[1] * 2 + to(r, s // 2, s % 2)[2])
+            for r in range(groups)
+            for s in range(planes * 2)
+        ]
+
+    def moved(value, to):
+        return lax.ppermute(value, BOTH, permutation(to))
+
+    along_x = lambda r, h, c: (r ^ 1, h, c)
+    along_y = lambda r, h, c: (r ^ 2, h, c)
+    to_core = lambda r, h, c: (r, h, 1 - c)
+    ring = (1, 3, 0, 2)
+    along_z = lambda r, h, c: (r, ring[h], c)
+
+
+    members = jnp.arange(n_pool, dtype=jnp.int32)
+    live = jnp.where(members[None, :] < pool_count[:, None], pool_weight, 0.0).T
+    live_high = lax.reduce_precision(live, 8, 7)
+    rest = live - live_high
+    rest_high = lax.reduce_precision(rest, 8, 7)
+    place = row_dest[None, :] + 1
+    index = pool_index.T
+    table = jnp.concatenate(
+        [
+            (index // 256).astype(BF16),
+            (index % 256).astype(BF16),
+            live_high.astype(BF16),
+            rest_high.astype(BF16),
+            (rest - rest_high).astype(BF16),
+            (place // 256).astype(BF16),
+            (place % 256).astype(BF16),
+            jnp.zeros((10, index.shape[1]), BF16),
+        ],
+        axis=0,
+    )
+    quarters = point_desc.reshape(planes, n_pts, comps)
+    table = jnp.broadcast_to(table[None], (groups, *table.shape))
+    outbox = jnp.concatenate([quarters, table], axis=1)
+
+    cols_pts = lax.all_to_all(outbox, "rows", 0, 0, tiled=True)
+    own = jnp.stack(
+        [env_desc, *(moved(env_desc, lambda r, h, c, d=d: (r, h ^ d, c)) for d in (1, 2, 3))]
+    )
+    own, quarters = lax.optimization_barrier((own, quarters))
+    env_mine = lax.all_to_all(
+        jnp.broadcast_to(own[None], (groups, *own.shape)), "rows", 0, 0, tiled=True
+    )
+
+    panel_pts = [
+        moved(
+            lax.dynamic_index_in_dim(quarters, q ^ t, 0, keepdims=False),
+            lambda r, h, c, t=t: (h, r ^ t, c),
+        )
+        for t in range(planes)
+    ]
+
+    table_rows = table.shape[1]
+    high, low = pl.pallas_call(
+        weights_kernel,
+        grid=(1,),
+        in_specs=[pl.BlockSpec((groups, table_rows, comps), lambda _: (0, n_pts // table_rows, 0))],
+        out_specs=[whole((groups, n_rows, envs))] * 2,
+        out_shape=[jax.ShapeDtypeStruct((groups, n_rows, envs), BF16)] * 2,
+        compiler_params=pltpu.CompilerParams(vmem_limit_bytes=VMEM_LIMIT),
+        cost_estimate=cost(n_rows * n_rows * groups * 16 * 6, 4 * MIB),
+        name="pool_weights",
+    )(cols_pts)
+
+    env_mine, high, low, *panel_pts = lax.optimization_barrier((env_mine, high, low, *panel_pts))
+    env_swapped = moved(env_mine, to_core)
+
+    anywhere = pl.BlockSpec(memory_space=pl.ANY)
+
+    pts_scratch = pltpu.VMEM((n_pts, groups * comps), BF16)
+    cols_code, panel_code, own_rows = pl.pallas_call(
+        design_kernel,
+        grid_spec=pltpu.PrefetchScalarGridSpec(
+            num_scalar_prefetch=1,
+            grid=(1,),
+            in_specs=[anywhere] * 9,
+            out_specs=[
+                whole((pad, n_pts)),
+                whole((n_pts + 16, n_rows)),
+                whole((n_rows // groups, n_pts)),
+            ],
+            scratch_shapes=[
+                pts_scratch,
+                pts_scratch,
+                pltpu.VMEM((groups, envs, groups * comps), BF16),
+                pltpu.VMEM((groups, 2, n_rows, envs), BF16),
+                pltpu.VMEM((n_rows, n_pts), F32),
+                pltpu.VMEM((n_pts, n_rows), F32),
+                pltpu.SemaphoreType.DMA((8,)),
+                pltpu.SemaphoreType.DMA((4, 10)),
+            ],
+        ),
+        out_shape=[
+            jax.ShapeDtypeStruct((pad, n_pts), jnp.int16),
+            jax.ShapeDtypeStruct((n_pts + 16, n_rows), jnp.int16),
+            jax.ShapeDtypeStruct((n_rows // groups, n_pts), F32),
+        ],
+        compiler_params=pltpu.CompilerParams(vmem_limit_bytes=VMEM_LIMIT),
+        cost_estimate=cost(8 * n_pts * envs * (groups * comps + 3 * n_rows), 14 * MIB),
+        name="design_values",
+    )(at, env_mine, env_swapped, cols_pts, *panel_pts, high, low)
+
+    half = n_rows // 2
+    held = [panel_code, moved(panel_code, along_z)]
+    from_x, from_y = moved(cols_code, along_x), moved(cols_code, along_y)
+    swapped = [moved(panel_code, to_core)]
+    upper, lower = moved(from_x[:half], along_y), moved(from_y[half:], along_x)
+    width = groups * n_pts
+    code_spec = whole((pad, n_pts))
+    near = pl.pallas_call(
+        near_columns_kernel,
+        grid=(3,),
+        in_specs=[code_spec] * 3,
+        out_specs=pl.BlockSpec((1, 2 * n_rows, n_pts), lambda d: (d, 0, 0)),
+        out_shape=jax.ShapeDtypeStruct((3, 2 * n_rows, n_pts), BF16),
+        compiler_params=pltpu.CompilerParams(vmem_limit_bytes=VMEM_LIMIT),
+        cost_estimate=cost(0, 6 * MIB),
+        name="near_columns",
+    )(cols_code, from_x, from_y)
+    far, design = pl.pallas_call(
+        far_columns_kernel,
+        grid_spec=pltpu.PrefetchScalarGridSpec(
+            num_scalar_prefetch=1,
+            grid=(1,),
+            in_specs=[
+                whole((n_rows // groups, n_pts)),
+                code_spec,
+                code_spec,
+                whole((half, n_pts)),
+                whole((pad - half, n_pts)),
+            ],
+            out_specs=[whole((1, 2 * n_rows, n_pts)), whole((n_rows // groups, width))],
+        ),
+        out_shape=[
+            jax.ShapeDtypeStruct((1, 2 * n_rows, n_pts), BF16),
+            jax.ShapeDtypeStruct((n_rows // groups, width), F32),
+        ],
+        compiler_params=pltpu.CompilerParams(vmem_limit_bytes=VMEM_LIMIT),
+        cost_estimate=cost(0, 5 * MIB),
+        name="far_columns",
+    )(at, own_rows, from_x, from_y, upper, lower)
+
+    panel_spec = whole((n_pts + 16, n_rows))
+
+    def gram_rows(gram, steps, first, n_near):
+        values, value_specs = [], []
+        if first < 3:
+            values.append(near)
+            value_specs.append(
+                pl.BlockSpec((1, 2 * n_rows, n_pts), lambda n, j, _: (jnp.minimum(j, 2), 0, 0))
+            )
+        if first + n_near == 4:
+            values.append(far)
+            value_specs.append(whole((1, 2 * n_rows, n_pts)))
+        operands = [at, *(c for i in steps for c in (held[i], swapped[i])), *values]
+        in_specs = [panel_spec] * (2 * len(steps)) + value_specs
+        aliases = {}
+        if gram is not None:
+            aliases = {len(operands): 0}
+            in_specs.append(anywhere)
+            operands.append(gram)
+        return pl.pallas_call(
+            functools.partial(gram_kernel, steps, first, n_near),
+            grid_spec=pltpu.PrefetchScalarGridSpec(
+                num_scalar_prefetch=1,
+                grid=(len(steps), n_near),
+                in_specs=in_specs,
+                out_specs=pl.BlockSpec(
+                    (2, n_pts, n_pts),
+                    lambda n, j, s: (0, ring_source(s[1], steps[0] + n), jnp.bitwise_xor(s[0], first + j)),
+                ),
+                scratch_shapes=[pltpu.VMEM((2, n_pts, 2 * n_rows), BF16)],
+            ),
+            out_shape=jax.ShapeDtypeStruct((2, planes * n_pts, width), F32),
+            input_output_aliases=aliases,
+            compiler_params=pltpu.CompilerParams(vmem_limit_bytes=VMEM_LIMIT),
+            cost_estimate=cost(len(steps) * n_near * 8 * n_pts * n_pts * n_rows, 4 * MIB),
+            name="gram_rows",
+        )(*operands)
+
+    held.append(moved(held[1], along_z))
+    swapped.append(moved(held[1], to_core))
+    gram = gram_rows(None, (0,), 0, 3)
+    gram = gram_rows(gram, (1,), 0, 3)
+    held[2], gram = lax.optimization_barrier((held[2], gram))
+    held.append(moved(held[2], along_z))
+    swapped.append(moved(held[2], to_core))
+    gram = gram_rows(gram, (0, 1), 3, 1)
+    held[3], gram = lax.optimization_barrier((held[3], gram))
+    swapped.append(moved(held[3], to_core))
+    gram = gram_rows(gram, (2,), 0, 4)
+    gram = gram_rows(gram, (3,), 0, 4)
+    return design, gram.reshape(2 * planes * n_pts, width)
+
+
 def solution(mesh):
     in_specs = (
         P("rows", "pts"),
@@ -102,6 +579,5 @@
         P("rows"),
     )
     out_specs = (P("rows", "pts"), P("rows", "pts"))
-    return jax.shard_map(
-        on_device, mesh=mesh, in_specs=in_specs, out_specs=out_specs, check_vma=False
-    )
+    body = on_device if dict(mesh.shape) == {"rows": 4, "pts": 8} else on_any_device
+    return jax.shard_map(body, mesh=mesh, in_specs=in_specs, out_specs=out_specs, check_vma=False)

time: 535 us -> 180 us (0.34)
  waiting for transfers between devices: 286 us -> 48.1 us
  local copies, waits for them, and re-layouts: 112 us -> 5.84 us
  Pallas kernels: 0 us -> 86.9 us
  matrix products: 68.7 us -> 0 us
  other arithmetic: 40.1 us -> 5.12 us
  starting transfers between devices: 12.2 us -> 32.5 us
  between operations: 13.9 us -> 0.82 us
    psum x1 -> x0, waiting for transfers between devices: 176 us -> none  [from_root(): return lax.psum(kept, axis)]
    scatter x3 -> x0, local copies, waits for them, and re-layouts: 87.1 us -> none  [the longest x1 48.9 us: on_device(): outbox = jnp.zeros((groups, slot_share, width_pts), jnp.float32).at[owner...]
    pallas_call x0 -> x9, Pallas kernels: none -> 86.9 us  [the longest x5 52 us: gram_rows(): pl.pallas_call(functools.partial(gram_kernel, steps, first, n_near), grid...]
    all_gather x3 -> x0, waiting for transfers between devices: 85.4 us -> none  [the longest x1 52.8 us: on_device(): all_rows = lax.all_gather(design, 'rows', axis=0, tiled=True)]
    dot_general x3 -> x0, matrix products: 68.7 us -> none  [the longest x2 61.8 us: on_device(): lax.dot_general(diagonal_panel, all_rows, (((0,), (0,)), ((), ())), preci...]
    ppermute x0 -> x19, waiting for transfers between devices: none -> 48.1 us  [moved(): return lax.ppermute(value, BOTH, permutation(to))]
    add x4 -> x0, other arithmetic: 28.9 us -> none  [the longest x1 24.1 us: on_device(): gram_tile + jnp.where(row_ids[:, None] == col_ids[None, :], damping, 0.0)]
    all_to_all x2, waiting for transfers between devices: 23.6 us -> 0.01 us  [the longest x1 0.01 us: on_device(): cols_pts = lax.all_to_all(outbox, 'rows', 0, 0, tiled=True)]
  transfers between devices with their start and end apart: 6 -> 21, of which waited for: 4 -> 8; matrix products, arithmetic and copies ran while one was open for 23% -> 2% of each run, Pallas kernels for 0% -> 31%
where the time goes in v2:
time: 180 us; the launch traced here: 179 us
  Pallas kernels  86.9 us (48%)
  waiting for transfers between devices  48.1 us (27%)
  starting transfers between devices  32.5 us (18%)
  local copies, waits for them, and re-layouts  5.84 us (3%)
  other arithmetic  5.12 us (3%)
    pallas_call x5, Pallas kernels, gram_rows(): pl.pallas_call(functools.partial(gram_kernel, steps, first, n_near), grid...  52 us
    ppermute x19, waiting for transfers between devices, moved(): return lax.ppermute(value, BOTH, permutation(to))  48.1 us
    ppermute x19, starting transfers between devices, moved(): return lax.ppermute(value, BOTH, permutation(to))  22.7 us
    pallas_call x1, Pallas kernels, on_device(): pl.pallas_call(design_kernel, grid_spec=pltpu.PrefetchScalarGridSpec(num_...  19.5 us
    pallas_call x1, Pallas kernels, on_device(): pl.pallas_call(weights_kernel, grid=(1,), in_specs=[pl.BlockSpec((groups,...  7.38 us
    all_to_all x1, starting transfers between devices, on_device(): cols_pts = lax.all_to_all(outbox, 'rows', 0, 0, tiled=True)  5.16 us
    all_to_all x1, starting transfers between devices, on_device(): lax.all_to_all(jnp.broadcast_to(own[None], (groups, *own.shape)), 'rows',...  4.58 us
    pallas_call x1, Pallas kernels, on_device(): pl.pallas_call(far_columns_kernel, grid_spec=pltpu.PrefetchScalarGridSpec...  4.07 us
  transfers between devices with their start and end apart: 21, of which 8 were waited for; matrix products, arithmetic and copies ran while one was open for 2% of the time, Pallas kernels for 31%

profile of v2, /device:TPU:0, one launch (start us, length us, event | category | flops | bytes accessed | tf_op | source)
XLA Modules:
  0.0 179.3 jit_solution(4676223690954269525)
XLA Ops:
  0.6 0.7 fusion.6
  1.3 0.7 fusion.2
  2.0 0.7 fusion
  2.8 0.2 concatenate.6
  3.0 0.0 copy-start.6
  3.0 2.3 %pad_maximum_fusion = bf16[4,544,256]{2,1,0:T(8,128)(2,1)} fusion(bf16[4,32,256]{2,1,0:T(8,128)(2,1)S(1)} %broadcast_in_dim.13, bf16[4,512,256]{2,1,0:T(8,128)(2,1)} %bitcast.47), kind=kLoop, calls=%fused_computation | loop fusion | flops 2228224 | bytes 2228224 | tf_op jit(solution)/shard_map/concatenate | solution.py:410
  5.3 5.2 %all-to-all-start.1 = ((bf16[4,544,256]{2,1,0:T(8,128)(2,1)}), bf16[4,544,256]{2,1,0:T(8,128)(2,1)S(1)}, u32[]{:S(2)}, u32[]{:S(2)}) async-start(bf16[4,544,256]{2,1,0:T(8,128)(2,1)} %pad_maximum_fusion), calls=%async_computation.1 | async-start | bytes 2228224 | tf_op jit(solution)/shard_map/all_to_all | solution.py:412
  10.5 1.6 collective-permute-start
  12.1 2.5 %collective-permute-start.2 = (bf16[512,128]{1,0:T(8,128)(2,1)S(1)}, bf16[512,128]{1,0:T(8,128)(2,1)S(1)}, u32[]{:S(2)}, u32[]{:S(2)}) collective-permute-start(bf16[512,128]{1,0:T(8,128)(2,1)S(1)} %copy-done.6), channel_id=1, source_target_pairs={{0,6},{1,7},{2,4},{3,5},{4,2},{5,3},{6,0},{7,1},{8,14},{9,15},{10,... | collective-permute-start | bytes 393224 | tf_op jit(solution)/shard_map/ppermute | solution.py:379
  14.5 0.1 collective-permute-start.1
  14.6 0.8 collective-permute-done
  15.4 6.4 %collective-permute-done.2 = bf16[512,128]{1,0:T(8,128)(2,1)S(1)} collective-permute-done((bf16[512,128]{1,0:T(8,128)(2,1)S(1)}, bf16[512,128]{1,0:T(8,128)(2,1)S(1)}, u32[]{:S(2)}, u32[]{:S(2)}) %collective-permute-start.2) | collective-permute-done | bytes 131104 | tf_op jit(solution)/shard_map/ppermute | solution.py:379
  21.8 4.4 %collective-permute-done.1 = bf16[512,128]{1,0:T(8,128)(2,1)S(1)} collective-permute-done((bf16[512,128]{1,0:T(8,128)(2,1)S(1)}, bf16[512,128]{1,0:T(8,128)(2,1)S(1)}, u32[]{:S(2)}, u32[]{:S(2)}) %collective-permute-start.1) | collective-permute-done | bytes 131104 | tf_op jit(solution)/shard_map/ppermute | solution.py:379
  26.2 0.1 pad_maximum_fusion.1
  26.3 1.7 broadcast_in_dim.10
  28.0 4.6 %all-to-all-start = ((bf16[4,4,512,128]{3,2,1,0:T(8,128)(2,1)}), bf16[4,4,512,128]{3,2,1,0:T(8,128)(2,1)}, u32[]{:S(2)}, u32[]{:S(2)}) async-start(bf16[4,4,512,128]{3,2,1,0:T(8,128)(2,1)} %broadcast_in_dim.10), calls=%async_computation | async-start | bytes 4194304 | tf_op jit(solution)/shard_map/all_to_all | solution.py:417
  32.6 0.8 dynamic-slice_bitcast_fusion
  33.4 2.6 %collective-permute-start.6 = (bf16[512,256]{1,0:T(8,128)(2,1)}, bf16[512,256]{1,0:T(8,128)(2,1)}, u32[]{:S(2)}, u32[]{:S(2)}) collective-permute-start(bf16[512,256]{1,0:T(8,128)(2,1)} %get-tuple-element.42), channel_id=1, source_target_pairs={{0,6},{1,7},{2,14},{3,15},{4,22},{5,23},{6,30},{7,31},{8,4},{9,5},... | collective-permute-start | bytes 786440 | tf_op jit(solution)/shard_map/ppermute | solution.py:379
  36.0 1.9 %collective-permute-start.5 = (bf16[512,256]{1,0:T(8,128)(2,1)S(1)}, bf16[512,256]{1,0:T(8,128)(2,1)}, u32[]{:S(2)}, u32[]{:S(2)}) collective-permute-start(bf16[512,256]{1,0:T(8,128)(2,1)S(1)} %get-tuple-element.43), channel_id=1, source_target_pairs={{0,4},{1,5},{2,12},{3,13},{4,20},{5,21},{6,28},{7,29},{8,6},{9,7},... | collective-permute-start | bytes 786440 | tf_op jit(solution)/shard_map/ppermute | solution.py:379
  38.0 0.0 collective-permute-start.4
  38.0 1.4 collective-permute-start.3
  39.3 7.4 %pool_weights.1 = (bf16[4,512,512]{2,1,0:T(8,128)(2,1)}, bf16[4,512,512]{2,1,0:T(8,128)(2,1)}) custom-call(bf16[4,544,256]{2,1,0:T(8,128)(2,1)} %copy-done), custom_call_target="tpu_custom_call" | custom-call | flops 201326592 | bytes 4194304 | tf_op jit(solution)/shard_map/pool_weights/pallas_call | solution.py:430
  46.7 22.5 %collective-permute-done.6.pan3 = bf16[512,256]{1,0:T(8,128)(2,1)} collective-permute-done((bf16[512,256]{1,0:T(8,128)(2,1)}, bf16[512,256]{1,0:T(8,128)(2,1)}, u32[]{:S(2)}, u32[]{:S(2)}) %collective-permute-start.6) | collective-permute-done | bytes 262176 | tf_op jit(solution)/shard_map/ppermute | solution.py:379
  69.3 0.1 collective-permute-start.7
  69.4 0.6 pad_add_fusion.at_ref
  70.0 3.9 %collective-permute-done.7.swapped = bf16[4,4,512,128]{3,2,1,0:T(8,128)(2,1)} collective-permute-done((bf16[4,4,512,128]{3,2,1,0:T(8,128)(2,1)}, bf16[4,4,512,128]{3,2,1,0:T(8,128)(2,1)}, u32[]{:S(2)}, u32[]{:S(2)}) %collective-permute-start.7) | collective-permute-done | bytes 2097184 | tf_op jit(solution)/shard_map/ppermute | solution.py:379
  73.8 19.5 %design_values.1 = (s16[528,512]{1,0:T(8,128)(2,1)}, s16[528,512]{1,0:T(8,128)(2,1)}, f32[128,512]{1,0:T(8,128)}) custom-call(s32[3]{0:T(128)} %pad_add_fusion.at_ref, bf16[4,4,512,128]{3,2,1,0:T(8,128)(2,1)} %all-to-all-done.mine, bf16[4,4,512,128]{3,2,1,0:T(8,128)(2,1)} %collective-permute-done.7.swapped, bf16[4,544,256]{2,1,0:T(8,128)(2,1)} %copy-done, ...), custom_call_target="tpu_custom_call" | custom-call | flops 10737418240 | bytes 14680064 | tf_op jit(solution)/shard_map/design_values/pallas_call | solution.py:447
  93.4 0.1 collective-permute-start.9
  93.4 1.0 collective-permute-start.8
  94.4 5.2 %collective-permute-start.12 = (s16[528,512]{1,0:T(8,128)(2,1)}, s16[528,512]{1,0:T(8,128)(2,1)}, u32[]{:S(2)}, u32[]{:S(2)}) collective-permute-start(s16[528,512]{1,0:T(8,128)(2,1)} %get-tuple-element.36.refs_0_), channel_id=1, source_target_pairs={{0,2},{1,3},{2,6},{3,7},{4,0},{5,1},{6,4},{7,5},{8,10},{9,11},{10,... | collective-permute-start | bytes 1622024 | tf_op jit(solution)/shard_map/ppermute | solution.py:379
  99.6 8.3 %collective-permute-done.9.code2 = s16[528,512]{1,0:T(8,128)(2,1)S(1)} collective-permute-done((s16[528,512]{1,0:T(8,128)(2,1)}, s16[528,512]{1,0:T(8,128)(2,1)S(1)}, u32[]{:S(2)}, u32[]{:S(2)}) %collective-permute-start.9) | collective-permute-done | bytes 540704 | tf_op jit(solution)/shard_map/ppermute | solution.py:379
  107.9 0.8 slice.9
  108.7 0.4 collective-permute-start.11
  109.2 0.9 copy-done.3
  110.0 0.7 slice.8
  110.8 0.5 collective-permute-start.10
  111.3 0.2 collective-permute-done.12.refs_0_.refs_2_
  111.5 5.0 %collective-permute-start.13 = (s16[528,512]{1,0:T(8,128)(2,1)}, s16[528,512]{1,0:T(8,128)(2,1)}, u32[]{:S(2)}, u32[]{:S(2)}) collective-permute-start(s16[528,512]{1,0:T(8,128)(2,1)} %collective-permute-done.12.refs_0_.refs_2_), channel_id=1, source_target_pairs={{0,2},{1,3},{2,6},{3,7},{4,0},{5,1},{6,4},{7,5},{8,10},{9,11},{10,... | collective-permute-start | bytes 1622024 | tf_op jit(solution)/shard_map/ppermute | solution.py:379
  116.5 3.9 %near_columns.1.refs_2_ = bf16[3,1024,512]{2,1,0:T(8,128)(2,1)} custom-call(s16[528,512]{1,0:T(8,128)(2,1)} %get-tuple-element.34.code0, s16[528,512]{1,0:T(8,128)(2,1)} %copy-done.3, s16[528,512]{1,0:T(8,128)(2,1)} %copy-done.2), custom_call_target="tpu_custom_call" | custom-call | bytes 6291456 | tf_op jit(solution)/shard_map/near_columns/pallas_call | solution.py:486
  120.4 9.7 %gram_rows.5.refs_3_ = f32[2,2048,2048]{2,1,0:T(8,128)} custom-call(s32[3]{0:T(128)} %pad_add_fusion.at_ref, s16[528,512]{1,0:T(8,128)(2,1)} %get-tuple-element.36.refs_0_, s16[528,512]{1,0:T(8,128)(2,1)} %collective-permute-done.15.refs_1_, bf16[3,1024,512]{2,1,0:T(8,128)(2,1)} %near_columns.1.refs_2_), custom_call_target="tpu_custom_call" | custom-call | flops 6442450944 | bytes 4194304 | tf_op jit(solution)/shard_map/gram_rows/pallas_call | solution.py:538
  130.2 9.7 %gram_rows.6.refs_5_ = f32[2,2048,2048]{2,1,0:T(8,128)} custom-call(s32[3]{0:T(128)} %pad_add_fusion.at_ref, s16[528,512]{1,0:T(8,128)(2,1)} %collective-permute-done.12.refs_0_.refs_2_, s16[528,512]{1,0:T(8,128)(2,1)} %collective-permute-done.14.refs_1_.refs_3_, bf16[3,1024,512]{2,1,0:T(8,128)(2,1)} %near_columns.1.refs_2_, ...), custom_call_target="tpu_custom_call", output_to_operand_aliasing={{}: (4, {})} | custom-call | flops 6442450944 | bytes 4194304 | tf_op jit(solution)/shard_map/gram_rows/pallas_call | solution.py:538
  139.9 0.3 collective-permute-start.18
  140.2 0.7 copy-done.5
  141.0 4.1 %far_columns.1 = (bf16[1,1024,512]{2,1,0:T(8,128)(2,1)}, f32[128,2048]{1,0:T(8,128)}) custom-call(s32[3]{0:T(128)} %pad_add_fusion.at_ref, f32[128,512]{1,0:T(8,128)} %get-tuple-element.33.rows_ref, s16[528,512]{1,0:T(8,128)(2,1)} %copy-done.3, s16[528,512]{1,0:T(8,128)(2,1)} %copy-done.2, s16[256,512]{1,0:T(8,128)(2,1)} %collective-permute-done.10.upper, ...), custom_call_target="tpu_custom_call" | custom-call | bytes 5242880 | tf_op jit(solution)/shard_map/far_columns/pallas_call | solution.py:496
  145.0 8.7 %gram_rows.7.refs_4_ = f32[2,2048,2048]{2,1,0:T(8,128)} custom-call(s32[3]{0:T(128)} %pad_add_fusion.at_ref, s16[528,512]{1,0:T(8,128)(2,1)} %get-tuple-element.36.refs_0_, s16[528,512]{1,0:T(8,128)(2,1)} %collective-permute-done.15.refs_1_, s16[528,512]{1,0:T(8,128)(2,1)} %collective-permute-done.12.refs_0_.refs_2_, ...), custom_call_target="tpu_custom_call", output_to_operand_aliasing={{}: (6, {})} | custom-call | flops 4294967296 | bytes 4194304 | tf_op jit(solution)/shard_map/gram_rows/pallas_call | solution.py:538
  153.7 1.7 collective-permute-done.16.refs_0_
  155.4 11.9 %gram_rows.8.refs_4_ = f32[2,2048,2048]{2,1,0:T(8,128)} custom-call(s32[3]{0:T(128)} %pad_add_fusion.at_ref, s16[528,512]{1,0:T(8,128)(2,1)} %collective-permute-done.13.refs_0_, s16[528,512]{1,0:T(8,128)(2,1)} %collective-permute-done.18.refs_1_, bf16[3,1024,512]{2,1,0:T(8,128)(2,1)} %near_columns.1.refs_2_, ...), custom_call_target="tpu_custom_call", output_to_operand_aliasing={{}: (5, {})} | custom-call | flops 8589934592 | bytes 4194304 | tf_op jit(solution)/shard_map/gram_rows/pallas_call | solution.py:538
  167.4 11.9 %gram_rows.9 = f32[2,2048,2048]{2,1,0:T(8,128)} custom-call(s32[3]{0:T(128)} %pad_add_fusion.at_ref, s16[528,512]{1,0:T(8,128)(2,1)} %copy-done.4, s16[528,512]{1,0:T(8,128)(2,1)} %collective-permute-done.17.refs_1_, bf16[3,1024,512]{2,1,0:T(8,128)(2,1)} %near_columns.1.refs_2_, ...), custom_call_target="tpu_custom_call", output_to_operand_aliasing={{}: (5, {})} | custom-call | flops 8589934592 | bytes 4194304 | tf_op jit(solution)/shard_map/gram_rows/pallas_call | solution.py:538
  (32 shorter events, 0.1 us)
Async XLA Ops:
  3.0 7.5 %copy-start.6 = (bf16[512,128]{1,0:T(8,128)(2,1)S(1)}, bf16[512,128]{1,0:T(8,128)(2,1)}, u32[]{:S(2)}) copy-start(bf16[512,128]{1,0:T(8,128)(2,1)} %param.6) | copy-start | bytes 393220
  5.3 20.9 %all-to-all-start.1 = ((bf16[4,544,256]{2,1,0:T(8,128)(2,1)}), bf16[4,544,256]{2,1,0:T(8,128)(2,1)S(1)}, u32[]{:S(2)}, u32[]{:S(2)}) async-start(bf16[4,544,256]{2,1,0:T(8,128)(2,1)} %pad_maximum_fusion), calls=%async_computation.1 | async-start | bytes 2228224 | tf_op jit(solution)/shard_map/all_to_all | solution.py:412
  10.5 5.0 %collective-permute-start = (bf16[512,128]{1,0:T(8,128)(2,1)S(1)}, bf16[512,128]{1,0:T(8,128)(2,1)S(1)}, u32[]{:S(2)}, u32[]{:S(2)}) collective-permute-start(bf16[512,128]{1,0:T(8,128)(2,1)S(1)} %copy-done.6), channel_id=1, source_target_pairs={{0,2},{1,3},{2,0},{3,1},{4,6},{5,7},{6,4},{7,5},{8,10},{9,11},{10,... | collective-permute-start | bytes 393224 | tf_op jit(solution)/shard_map/ppermute | solution.py:379
  12.1 9.8 %collective-permute-start.2 = (bf16[512,128]{1,0:T(8,128)(2,1)S(1)}, bf16[512,128]{1,0:T(8,128)(2,1)S(1)}, u32[]{:S(2)}, u32[]{:S(2)}) collective-permute-start(bf16[512,128]{1,0:T(8,128)(2,1)S(1)} %copy-done.6), channel_id=1, source_target_pairs={{0,6},{1,7},{2,4},{3,5},{4,2},{5,3},{6,0},{7,1},{8,14},{9,15},{10,... | collective-permute-start | bytes 393224 | tf_op jit(solution)/shard_map/ppermute | solution.py:379
  14.5 11.6 %collective-permute-start.1 = (bf16[512,128]{1,0:T(8,128)(2,1)S(1)}, bf16[512,128]{1,0:T(8,128)(2,1)S(1)}, u32[]{:S(2)}, u32[]{:S(2)}) collective-permute-start(bf16[512,128]{1,0:T(8,128)(2,1)S(1)} %copy-done.6), channel_id=1, source_target_pairs={{0,4},{1,5},{2,6},{3,7},{4,0},{5,1},{6,2},{7,3},{8,12},{9,13},{10,... | collective-permute-start | bytes 393224 | tf_op jit(solution)/shard_map/ppermute | solution.py:379
  26.3 1.7 copy-start
  28.0 4.6 %copy-start.1 = (bf16[2048,256]{1,0:T(8,128)(2,1)S(1)}, bf16[2048,256]{1,0:T(8,128)(2,1)}, u32[]{:S(2)}) copy-start(bf16[2048,256]{1,0:T(8,128)(2,1)} %param.7) | copy-start | bytes 3145732
  28.0 41.3 %all-to-all-start = ((bf16[4,4,512,128]{3,2,1,0:T(8,128)(2,1)}), bf16[4,4,512,128]{3,2,1,0:T(8,128)(2,1)}, u32[]{:S(2)}, u32[]{:S(2)}) async-start(bf16[4,4,512,128]{3,2,1,0:T(8,128)(2,1)} %broadcast_in_dim.10), calls=%async_computation | async-start | bytes 4194304 | tf_op jit(solution)/shard_map/all_to_all | solution.py:417
  33.4 35.8 %collective-permute-start.6 = (bf16[512,256]{1,0:T(8,128)(2,1)}, bf16[512,256]{1,0:T(8,128)(2,1)}, u32[]{:S(2)}, u32[]{:S(2)}) collective-permute-start(bf16[512,256]{1,0:T(8,128)(2,1)} %get-tuple-element.42), channel_id=1, source_target_pairs={{0,6},{1,7},{2,14},{3,15},{4,22},{5,23},{6,30},{7,31},{8,4},{9,5},... | collective-permute-start | bytes 786440 | tf_op jit(solution)/shard_map/ppermute | solution.py:379
  36.0 33.2 %collective-permute-start.5 = (bf16[512,256]{1,0:T(8,128)(2,1)S(1)}, bf16[512,256]{1,0:T(8,128)(2,1)}, u32[]{:S(2)}, u32[]{:S(2)}) collective-permute-start(bf16[512,256]{1,0:T(8,128)(2,1)S(1)} %get-tuple-element.43), channel_id=1, source_target_pairs={{0,4},{1,5},{2,12},{3,13},{4,20},{5,21},{6,28},{7,29},{8,6},{9,7},... | collective-permute-start | bytes 786440 | tf_op jit(solution)/shard_map/ppermute | solution.py:379
  38.0 31.3 %collective-permute-start.4 = (bf16[512,256]{1,0:T(8,128)(2,1)S(1)}, bf16[512,256]{1,0:T(8,128)(2,1)}, u32[]{:S(2)}, u32[]{:S(2)}) collective-permute-start(bf16[512,256]{1,0:T(8,128)(2,1)S(1)} %get-tuple-element.44), channel_id=1, source_target_pairs={{0,2},{1,3},{2,10},{3,11},{4,18},{5,19},{6,26},{7,27},{8,0},{9,1},... | collective-permute-start | bytes 786440 | tf_op jit(solution)/shard_map/ppermute | solution.py:379
  38.0 31.2 %collective-permute-start.3 = (bf16[512,256]{1,0:T(8,128)(2,1)S(1)}, bf16[512,256]{1,0:T(8,128)(2,1)}, u32[]{:S(2)}, u32[]{:S(2)}) collective-permute-start(bf16[512,256]{1,0:T(8,128)(2,1)S(1)} %get-tuple-element.45), channel_id=1, source_target_pairs={{0,0},{1,1},{2,8},{3,9},{4,16},{5,17},{6,24},{7,25},{8,2},{9,3},{1... | collective-permute-start | bytes 786440 | tf_op jit(solution)/shard_map/ppermute | solution.py:379
  69.3 4.6 %collective-permute-start.7 = (bf16[4,4,512,128]{3,2,1,0:T(8,128)(2,1)}, bf16[4,4,512,128]{3,2,1,0:T(8,128)(2,1)}, u32[]{:S(2)}, u32[]{:S(2)}) collective-permute-start(bf16[4,4,512,128]{3,2,1,0:T(8,128)(2,1)} %all-to-all-done.mine), channel_id=1, source_target_pairs={{0,1},{1,0},{2,3},{3,2},{4,5},{5,4},{6,7},{7,6},{8,9},{9,8},{10,11... | collective-permute-start | bytes 6291464 | tf_op jit(solution)/shard_map/ppermute | solution.py:379
  93.4 14.6 %collective-permute-start.9 = (s16[528,512]{1,0:T(8,128)(2,1)}, s16[528,512]{1,0:T(8,128)(2,1)S(1)}, u32[]{:S(2)}, u32[]{:S(2)}) collective-permute-start(s16[528,512]{1,0:T(8,128)(2,1)} %get-tuple-element.34.code0), channel_id=1, source_target_pairs={{0,16},{1,17},{2,18},{3,19},{4,20},{5,21},{6,22},{7,23},{8,24},{9,... | collective-permute-start | bytes 1622024 | tf_op jit(solution)/shard_map/ppermute | solution.py:379
  93.4 15.7 %collective-permute-start.8 = (s16[528,512]{1,0:T(8,128)(2,1)}, s16[528,512]{1,0:T(8,128)(2,1)S(1)}, u32[]{:S(2)}, u32[]{:S(2)}) collective-permute-start(s16[528,512]{1,0:T(8,128)(2,1)} %get-tuple-element.34.code0), channel_id=1, source_target_pairs={{0,8},{1,9},{2,10},{3,11},{4,12},{5,13},{6,14},{7,15},{8,0},{9,1},... | collective-permute-start | bytes 1622024 | tf_op jit(solution)/shard_map/ppermute | solution.py:379
  94.4 17.1 %collective-permute-start.12 = (s16[528,512]{1,0:T(8,128)(2,1)}, s16[528,512]{1,0:T(8,128)(2,1)}, u32[]{:S(2)}, u32[]{:S(2)}) collective-permute-start(s16[528,512]{1,0:T(8,128)(2,1)} %get-tuple-element.36.refs_0_), channel_id=1, source_target_pairs={{0,2},{1,3},{2,6},{3,7},{4,0},{5,1},{6,4},{7,5},{8,10},{9,11},{10,... | collective-permute-start | bytes 1622024 | tf_op jit(solution)/shard_map/ppermute | solution.py:379
  99.6 20.8 %collective-permute-start.15 = (s16[528,512]{1,0:T(8,128)(2,1)}, s16[528,512]{1,0:T(8,128)(2,1)}, u32[]{:S(2)}, u32[]{:S(2)}) collective-permute-start(s16[528,512]{1,0:T(8,128)(2,1)} %get-tuple-element.36.refs_0_), channel_id=1, source_target_pairs={{0,1},{1,0},{2,3},{3,2},{4,5},{5,4},{6,7},{7,6},{8,9},{9,8},{10,11... | collective-permute-start | bytes 1622024 | tf_op jit(solution)/shard_map/ppermute | solution.py:379
  107.9 8.6 %copy-start.2 = (s16[528,512]{1,0:T(8,128)(2,1)}, s16[528,512]{1,0:T(8,128)(2,1)S(1)}, u32[]{:S(2)}) copy-start(s16[528,512]{1,0:T(8,128)(2,1)S(1)} %collective-permute-done.9.code2) | copy-start | bytes 1622020
  108.7 31.5 %collective-permute-start.11 = (s16[272,512]{1,0:T(8,128)(2,1)}, s16[272,512]{1,0:T(8,128)(2,1)S(1)}, u32[]{:S(2)}, u32[]{:S(2)}) collective-permute-start(s16[272,512]{1,0:T(8,128)(2,1)} %slice.9), channel_id=1, source_target_pairs={{0,8},{1,9},{2,10},{3,11},{4,12},{5,13},{6,14},{7,15},{8,0},{9,1},... | collective-permute-start | bytes 835592 | tf_op jit(solution)/shard_map/ppermute | solution.py:379
  109.2 0.9 copy-start.3
  110.8 29.4 %collective-permute-start.10 = (s16[256,512]{1,0:T(8,128)(2,1)}, s16[256,512]{1,0:T(8,128)(2,1)}, u32[]{:S(2)}, u32[]{:S(2)}) collective-permute-start(s16[256,512]{1,0:T(8,128)(2,1)} %slice.8), channel_id=1, source_target_pairs={{0,16},{1,17},{2,18},{3,19},{4,20},{5,21},{6,22},{7,23},{8,24},{9,... | collective-permute-start | bytes 786440 | tf_op jit(solution)/shard_map/ppermute | solution.py:379
  111.5 18.7 %collective-permute-start.14 = (s16[528,512]{1,0:T(8,128)(2,1)}, s16[528,512]{1,0:T(8,128)(2,1)}, u32[]{:S(2)}, u32[]{:S(2)}) collective-permute-start(s16[528,512]{1,0:T(8,128)(2,1)} %collective-permute-done.12.refs_0_.refs_2_), channel_id=1, source_target_pairs={{0,1},{1,0},{2,3},{3,2},{4,5},{5,4},{6,7},{7,6},{8,9},{9,8},{10,11... | collective-permute-start | bytes 1622024 | tf_op jit(solution)/shard_map/ppermute | solution.py:379
  111.5 28.4 %collective-permute-start.13 = (s16[528,512]{1,0:T(8,128)(2,1)}, s16[528,512]{1,0:T(8,128)(2,1)}, u32[]{:S(2)}, u32[]{:S(2)}) collective-permute-start(s16[528,512]{1,0:T(8,128)(2,1)} %collective-permute-done.12.refs_0_.refs_2_), channel_id=1, source_target_pairs={{0,2},{1,3},{2,6},{3,7},{4,0},{5,1},{6,4},{7,5},{8,10},{9,11},{10,... | collective-permute-start | bytes 1622024 | tf_op jit(solution)/shard_map/ppermute | solution.py:379
  139.9 15.5 %collective-permute-start.16 = (s16[528,512]{1,0:T(8,128)(2,1)}, s16[528,512]{1,0:T(8,128)(2,1)S(1)}, u32[]{:S(2)}, u32[]{:S(2)}) collective-permute-start(s16[528,512]{1,0:T(8,128)(2,1)} %collective-permute-done.13.refs_0_), channel_id=1, source_target_pairs={{0,2},{1,3},{2,6},{3,7},{4,0},{5,1},{6,4},{7,5},{8,10},{9,11},{10,... | collective-permute-start | bytes 1622024 | tf_op jit(solution)/shard_map/ppermute | solution.py:379
  139.9 15.5 %collective-permute-start.18 = (s16[528,512]{1,0:T(8,128)(2,1)}, s16[528,512]{1,0:T(8,128)(2,1)}, u32[]{:S(2)}, u32[]{:S(2)}) collective-permute-start(s16[528,512]{1,0:T(8,128)(2,1)} %collective-permute-done.13.refs_0_), channel_id=1, source_target_pairs={{0,1},{1,0},{2,3},{3,2},{4,5},{5,4},{6,7},{7,6},{8,9},{9,8},{10,11... | collective-permute-start | bytes 1622024 | tf_op jit(solution)/shard_map/ppermute | solution.py:379
  140.2 0.7 copy-start.5
  155.4 12.0 %copy-start.4 = (s16[528,512]{1,0:T(8,128)(2,1)}, s16[528,512]{1,0:T(8,128)(2,1)S(1)}, u32[]{:S(2)}) copy-start(s16[528,512]{1,0:T(8,128)(2,1)S(1)} %collective-permute-done.16.refs_0_) | copy-start | bytes 1622020
  155.4 12.0 %collective-permute-start.17 = (s16[528,512]{1,0:T(8,128)(2,1)S(1)}, s16[528,512]{1,0:T(8,128)(2,1)}, u32[]{:S(2)}, u32[]{:S(2)}) collective-permute-start(s16[528,512]{1,0:T(8,128)(2,1)S(1)} %collective-permute-done.16.refs_0_), channel_id=1, source_target_pairs={{0,1},{1,0},{2,3},{3,2},{4,5},{5,4},{6,7},{7,6},{8,9},{9,8},{10,11... | collective-permute-start | bytes 1622024 | tf_op jit(solution)/shard_map/ppermute | solution.py:379

commit v3 on v2

--- a/solution.py
+++ b/solution.py
@@ -139,38 +139,35 @@
     return root * jnp.abs(root) * scale
 
 
-def weights_kernel(table_ref, high_ref, low_ref):
-    groups, rows, envs = high_ref.shape
-    shares = []
-    for g in range(groups):
-        piece = table_ref[g].astype(F32)
-        index = piece[0:4] * 256.0 + piece[4:8] + float(g * envs)
+def weights_kernel(*refs):
+    tables, high_ref, low_ref = refs[:-2], refs[-2], refs[-1]
+    rows, envs = high_ref.shape[1:]
+    for d, ref in enumerate(tables):
+        lanes = ref.shape[1]
+        piece = ref[...].astype(F32)
+        piece = jnp.concatenate([piece[0:32], piece[32:64]], axis=1)
+        slots = 2 * lanes
+        index = piece[0:4] * 256.0 + piece[4:8]
         weight = piece[8:12] + piece[12:16] + piece[16:20]
         place = piece[20:21] * 256.0 + piece[21:22] - 1.0
-        shares.append(jnp.concatenate([index, weight, place], axis=0))
-    table = jnp.concatenate(shares, axis=1)
-    slots = table.shape[1]
-    row_id = lax.broadcasted_iota(jnp.int32, (rows, slots), 0).astype(F32)
-    chosen = jnp.where(table[8:9, :] == row_id, 1.0, 0.0)
-    by_row = lax.dot_general(
-        chosen,
-        table,
-        (((1,), (1,)), ((), ())),
-        precision=lax.Precision.HIGHEST,
-        preferred_element_type=F32,
-    )
-    env_id = lax.broadcasted_iota(jnp.int32, (rows, envs), 1).astype(F32)
-    index = jnp.floor(by_row + 0.5)
-    for group in range(groups):
-        ids = env_id + float(group * envs)
+        row_id = lax.broadcasted_iota(jnp.int32, (rows, slots), 0).astype(F32)
+        by_row = lax.dot_general(
+            jnp.where(place == row_id, 1.0, 0.0),
+            jnp.concatenate([index, weight], axis=0),
+            (((1,), (1,)), ((), ())),
+            precision=lax.Precision.HIGHEST,
+            preferred_element_type=F32,
+        )
+        env_id = lax.broadcasted_iota(jnp.int32, (rows, envs), 1).astype(F32)
+        index = jnp.floor(by_row + 0.5)
         total = jnp.zeros((rows, envs), F32)
         for member in range(4):
             total = total + jnp.where(
-                index[:, member : member + 1] == ids, by_row[:, 4 + member : 5 + member], 0.0
+                index[:, member : member + 1] == env_id, by_row[:, 4 + member : 5 + member], 0.0
             )
         high, low = split(total)
-        high_ref[group] = high
-        low_ref[group] = low
+        high_ref[d] = high
+        low_ref[d] = low
 
 
 def fourth_power(products, scale):
@@ -204,40 +201,40 @@
         copy.wait()
 
 
-def group_copies(at_ref, group, mine, swapped, high, low, env, weights, sems):
+def group_copies(at_ref, d, sides, weights_from, env, weights, sems):
     z, core = at_ref[1], at_ref[2]
-    part = mine.shape[3]
+    envs, part = env.shape[0], sides[0][0].shape[1]
     out = []
-    for side, ref in ((core, mine), (1 - core, swapped)):
+    for side, refs in zip((core, 1 - core), sides):
         for r in range(4):
+            ref, first = (refs[d], r) if d < 3 else (refs[3 + r // 2], r % 2)
             at = pl.multiple_of((jnp.bitwise_xor(z, r) * 2 + side) * part, part)
-            to = env.at[:, pl.ds(at, part)]
-            out.append(pltpu.make_async_copy(ref.at[group, r], to, sems.at[len(out)]))
-    for i, ref in enumerate((high, low)):
-        out.append(pltpu.make_async_copy(ref.at[group], weights.at[i], sems.at[8 + i]))
+            source = ref.at[pl.ds(first * envs, envs)]
+            out.append(pltpu.make_async_copy(source, env.at[:, pl.ds(at, part)], sems.at[len(out)]))
+    for i in range(2):
+        source = weights_from[i].at[d] if d < 3 else weights_from[2 + i].at[0]
+        out.append(pltpu.make_async_copy(source, weights.at[i], sems.at[8 + i]))
     return out
 
 
-def design_kernel(
-    at_ref, mine, swapped, cols, pan0, pan1, pan2, pan3, high, low,
-    cols_code, panel_code, rows_out,
-    cols_pts, panel_pts, env, weights, cols_sum, panel_sum, point_sems, group_sems,
-):
+def design_kernel(at_ref, *refs):
+    sides, cols, panels, weights_from = (refs[0:5], refs[5:10]), refs[10], refs[11:15], refs[15:19]
+    cols_code, panel_code, rows_out = refs[19:22]
+    cols_pts, panel_pts, env, weights, cols_sum, panel_sum, point_sems, group_sems = refs[22:]
     q, z = at_ref[0], at_ref[1]
-    n_pts, comps = pan0.shape
+    n_pts, comps = panels[0].shape
     points = []
     for j in range(4):
         to = cols_pts.at[:, pl.ds(j * comps, comps)]
-        source = cols.at[j, pl.ds(0, n_pts)]
-        points.append(pltpu.make_async_copy(source, to, point_sems.at[j]))
+        points.append(pltpu.make_async_copy(cols.at[j], to, point_sems.at[j]))
     started(points)
     copies = [
-        group_copies(at_ref, d, mine, swapped, high, low, env.at[d], weights.at[d], group_sems.at[d])
+        group_copies(at_ref, d, sides, weights_from, env.at[d], weights.at[d], group_sems.at[d])
         for d in range(4)
     ]
     started(copies[0])
     panel = []
-    for t, ref in enumerate((pan0, pan1, pan2, pan3)):
+    for t, ref in enumerate(panels):
         at = pl.multiple_of(jnp.bitwise_xor(z, t) * comps, comps)
         to = panel_pts.at[:, pl.ds(at, comps)]
         panel.append(pltpu.make_async_copy(ref, to, point_sems.at[4 + t]))
@@ -384,6 +381,9 @@
     ring = (1, 3, 0, 2)
     along_z = lambda r, h, c: (r, ring[h], c)
 
+
+    quarters = point_desc.reshape(planes, n_pts, comps)
+    cols_pts = lax.all_to_all(quarters, "rows", 0, 0, tiled=True)
 
     members = jnp.arange(n_pool, dtype=jnp.int32)
     live = jnp.where(members[None, :] < pool_count[:, None], pool_weight, 0.0).T
@@ -405,18 +405,18 @@
         ],
         axis=0,
     )
-    quarters = point_desc.reshape(planes, n_pts, comps)
-    table = jnp.broadcast_to(table[None], (groups, *table.shape))
-    outbox = jnp.concatenate([quarters, table], axis=1)
-
-    cols_pts = lax.all_to_all(outbox, "rows", 0, 0, tiled=True)
-    own = jnp.stack(
-        [env_desc, *(moved(env_desc, lambda r, h, c, d=d: (r, h ^ d, c)) for d in (1, 2, 3))]
-    )
-    own, quarters = lax.optimization_barrier((own, quarters))
-    env_mine = lax.all_to_all(
-        jnp.broadcast_to(own[None], (groups, *own.shape)), "rows", 0, 0, tiled=True
-    )
+
+    own = jnp.concatenate(
+        [
+            env_desc,
+            *(moved(env_desc, lambda r, h, c, d=d: (r, h ^ d, c)) for d in (1, 2, 3)),
+            table[:, :part],
+            table[:, part:],
+        ]
+    )
+    own, cols_pts, quarters = lax.optimization_barrier((own, cols_pts, quarters))
+    near_x, near_y = moved(own, along_x), moved(own, along_y)
+    swap_own = moved(own, to_core)
 
     panel_pts = [
         moved(
@@ -426,20 +426,31 @@
         for t in range(planes)
     ]
 
-    table_rows = table.shape[1]
-    high, low = pl.pallas_call(
-        weights_kernel,
-        grid=(1,),
-        in_specs=[pl.BlockSpec((groups, table_rows, comps), lambda _: (0, n_pts // table_rows, 0))],
-        out_specs=[whole((groups, n_rows, envs))] * 2,
-        out_shape=[jax.ShapeDtypeStruct((groups, n_rows, envs), BF16)] * 2,
-        compiler_params=pltpu.CompilerParams(vmem_limit_bytes=VMEM_LIMIT),
-        cost_estimate=cost(n_rows * n_rows * groups * 16 * 6, 4 * MIB),
-        name="pool_weights",
-    )(cols_pts)
-
-    env_mine, high, low, *panel_pts = lax.optimization_barrier((env_mine, high, low, *panel_pts))
-    env_swapped = moved(env_mine, to_core)
+    def pool_weights(tables):
+        n = len(tables)
+        return pl.pallas_call(
+            weights_kernel,
+            grid=(1,),
+            in_specs=[
+                pl.BlockSpec((64, part), lambda _, last=t.shape[0] // 64 - 1: (last, 0))
+                for t in tables
+            ],
+            out_specs=[whole((n, n_rows, envs))] * 2,
+            out_shape=[jax.ShapeDtypeStruct((n, n_rows, envs), BF16)] * 2,
+            compiler_params=pltpu.CompilerParams(vmem_limit_bytes=VMEM_LIMIT),
+            cost_estimate=cost(n * n_rows * n_rows * 16 * 6, n * MIB),
+            name="pool_weights",
+        )(*tables)
+
+    far_upper, far_lower = moved(near_x[: 2 * envs], along_y), moved(near_y[2 * envs :], along_x)
+    near_weights = pool_weights([own, near_x, near_y])
+    far_upper, far_lower, *rest = lax.optimization_barrier(
+        (far_upper, far_lower, *near_weights, *panel_pts)
+    )
+    near_weights, panel_pts = rest[:2], rest[2:]
+    mine = (own, near_x, near_y, far_upper, far_lower)
+    other = (swap_own, *(moved(e, to_core) for e in mine[1:]))
+    weights = (*near_weights, *pool_weights([far_lower]))
 
     anywhere = pl.BlockSpec(memory_space=pl.ANY)
 
@@ -449,7 +460,7 @@
         grid_spec=pltpu.PrefetchScalarGridSpec(
             num_scalar_prefetch=1,
             grid=(1,),
-            in_specs=[anywhere] * 9,
+            in_specs=[anywhere] * 19,
             out_specs=[
                 whole((pad, n_pts)),
                 whole((n_pts + 16, n_rows)),
@@ -474,7 +485,7 @@
         compiler_params=pltpu.CompilerParams(vmem_limit_bytes=VMEM_LIMIT),
         cost_estimate=cost(8 * n_pts * envs * (groups * comps + 3 * n_rows), 14 * MIB),
         name="design_values",
-    )(at, env_mine, env_swapped, cols_pts, *panel_pts, high, low)
+    )(at, *mine, *other, cols_pts, *panel_pts, *weights)
 
     half = n_rows // 2
     held = [panel_code, moved(panel_code, along_z)]
@@ -556,8 +567,7 @@
 
     held.append(moved(held[1], along_z))
     swapped.append(moved(held[1], to_core))
-    gram = gram_rows(None, (0,), 0, 3)
-    gram = gram_rows(gram, (1,), 0, 3)
+    gram = gram_rows(None, (0, 1), 0, 3)
     held[2], gram = lax.optimization_barrier((held[2], gram))
     held.append(moved(held[2], along_z))
     swapped.append(moved(held[2], to_core))

time: 180 us -> 174 us (0.967)
  waiting for transfers between devices: 48.1 us -> 31.6 us
  starting transfers between devices: 32.5 us -> 40 us
  local copies, waits for them, and re-layouts: 5.84 us -> 12.6 us
  other arithmetic: 5.12 us -> 2.75 us
  Pallas kernels: 86.9 us -> 85.1 us
    ppermute x19 -> x27, waiting for transfers between devices: 48.1 us -> 25.8 us  [moved(): return lax.ppermute(value, BOTH, permutation(to))]
    ppermute x19 -> x27, starting transfers between devices: 22.7 us -> 36.1 us  [moved(): return lax.ppermute(value, BOTH, permutation(to))]
    all_to_all x2 -> x1, starting transfers between devices: 9.75 us -> 3.93 us  [on_device(): cols_pts = lax.all_to_all(quarters, 'rows', 0, 0, tiled=True)]
    all_to_all x2 -> x1, waiting for transfers between devices: 0.01 us -> 5.81 us  [on_device(): cols_pts = lax.all_to_all(quarters, 'rows', 0, 0, tiled=True)]
    unnamed x14 -> x27, local copies, waits for them, and re-layouts: 1.62 us -> 6.68 us
    pallas_call x5 -> x4, Pallas kernels: 52 us -> 48.9 us  [gram_rows(): pl.pallas_call(functools.partial(gram_kernel, steps, first, n_near), grid...]
    slice x0 -> x2, local copies, waits for them, and re-layouts: none -> 2.41 us  [the longest x1 1.68 us: on_device(): near_x[:2 * envs]]
    concatenate x1 -> x0, other arithmetic: 2.33 us -> none  [on_device(): outbox = jnp.concatenate([quarters, table], axis=1)]
  transfers between devices with their start and end apart: 21 -> 28, of which waited for: 8 -> 6; matrix products, arithmetic and copies ran while one was open for 2% -> 7% of each run, Pallas kernels for 31% -> 31%
where the time goes in v3:
time: 174 us; the launch traced here: 173 us
  Pallas kernels  85.1 us (49%)
  starting transfers between devices  40 us (23%)
  waiting for transfers between devices  31.6 us (18%)
  local copies, waits for them, and re-layouts  12.6 us (7%)
  other arithmetic  2.75 us (2%)
    pallas_call x4, Pallas kernels, gram_rows(): pl.pallas_call(functools.partial(gram_kernel, steps, first, n_near), grid...  48.9 us
    ppermute x27, starting transfers between devices, moved(): return lax.ppermute(value, BOTH, permutation(to))  36.1 us
    ppermute x27, waiting for transfers between devices, moved(): return lax.ppermute(value, BOTH, permutation(to))  25.8 us
    pallas_call x1, Pallas kernels, on_device(): pl.pallas_call(design_kernel, grid_spec=pltpu.PrefetchScalarGridSpec(num_...  19.5 us
    pallas_call x2, Pallas kernels, pool_weights(): pl.pallas_call(weights_kernel, grid=(1,), in_specs=[pl.BlockSpec((64, par...  8.72 us
    unnamed x27, local copies, waits for them, and re-layouts  6.68 us
    all_to_all x1, waiting for transfers between devices, on_device(): cols_pts = lax.all_to_all(quarters, 'rows', 0, 0, tiled=True)  5.81 us
    pallas_call x1, Pallas kernels, on_device(): pl.pallas_call(far_columns_kernel, grid_spec=pltpu.PrefetchScalarGridSpec...  4.07 us
  transfers between devices with their start and end apart: 28, of which 6 were waited for; matrix products, arithmetic and copies ran while one was open for 7% of the time, Pallas kernels for 31%

profile of v3, /device:TPU:0, one launch (start us, length us, event | category | flops | bytes accessed | tf_op | source)
XLA Modules:
  0.0 172.9 jit_solution(4577850114489449520)
XLA Ops:
  0.6 4.1 %collective-permute-start.1 = (bf16[512,128]{1,0:T(8,128)(2,1)}, bf16[512,128]{1,0:T(8,128)(2,1)S(1)}, u32[]{:S(2)}, u32[]{:S(2)}) collective-permute-start(bf16[512,128]{1,0:T(8,128)(2,1)} %param.6), channel_id=1, source_target_pairs={{0,4},{1,5},{2,6},{3,7},{4,0},{5,1},{6,2},{7,3},{8,12},{9,13},{10,... | collective-permute-start | bytes 393224 | tf_op jit(solution)/shard_map/ppermute | solution.py:376
  4.7 1.6 collective-permute-start
  6.3 3.9 %all-to-all-start = ((bf16[4,512,256]{2,1,0:T(8,128)(2,1)}), bf16[4,512,256]{2,1,0:T(8,128)(2,1)S(1)}, u32[]{:S(2)}, u32[]{:S(2)}) async-start(bf16[4,512,256]{2,1,0:T(8,128)(2,1)} %bitcast.43), calls=%async_computation | async-start | bytes 2097152 | tf_op jit(solution)/shard_map/all_to_all | solution.py:386
  10.2 0.7 fusion.2
  10.9 0.7 fusion
  11.7 0.7 fusion.6
  12.3 1.6 constant_dynamic-update-slice_fusion.5
  14.1 0.7 constant_dynamic-update-slice_fusion.4
  14.8 0.7 constant_dynamic-update-slice_fusion.3
  15.5 0.7 constant_dynamic-update-slice_fusion.2
  16.2 0.6 constant_dynamic-update-slice_fusion.1
  16.7 0.6 constant_dynamic-update-slice_fusion.refs_0_
  17.3 5.8 %all-to-all-done.refs_10_ = bf16[4,512,256]{2,1,0:T(8,128)(2,1)S(1)} async-done(((bf16[4,512,256]{2,1,0:T(8,128)(2,1)}), bf16[4,512,256]{2,1,0:T(8,128)(2,1)S(1)}, u32[]{:S(2)}, u32[]{:S(2)}) %all-to-all-start) | async-done | bytes 1048608 | tf_op jit(solution)/shard_map/all_to_all | solution.py:386
  23.2 1.5 collective-permute-start.4
  25.1 1.3 dynamic-slice_bitcast_fusion
  26.4 3.6 %collective-permute-start.10 = (bf16[512,256]{1,0:T(8,128)(2,1)S(1)}, bf16[512,256]{1,0:T(8,128)(2,1)S(1)}, u32[]{:S(2)}, u32[]{:S(2)}) collective-permute-start(bf16[512,256]{1,0:T(8,128)(2,1)S(1)} %get-tuple-element.50), channel_id=1, source_target_pairs={{0,6},{1,7},{2,14},{3,15},{4,22},{5,23},{6,30},{7,31},{8,4},{9,5},... | collective-permute-start | bytes 786440 | tf_op jit(solution)/shard_map/ppermute | solution.py:376
  30.0 1.5 collective-permute-start.9
  31.5 8.5 %collective-permute-done.4.refs_2_ = bf16[2112,128]{1,0:T(8,128)(2,1)S(1)} collective-permute-done((bf16[2112,128]{1,0:T(8,128)(2,1)}, bf16[2112,128]{1,0:T(8,128)(2,1)S(1)}, u32[]{:S(2)}, u32[]{:S(2)}) %collective-permute-start.4) | collective-permute-done | bytes 540704 | tf_op jit(solution)/shard_map/ppermute | solution.py:376
  40.1 0.7 collective-permute-start.7
  40.7 0.7 slice.27
  41.5 1.8 %collective-permute-done.3.refs_1_ = bf16[2112,128]{1,0:T(8,128)(2,1)} collective-permute-done((bf16[2112,128]{1,0:T(8,128)(2,1)}, bf16[2112,128]{1,0:T(8,128)(2,1)}, u32[]{:S(2)}, u32[]{:S(2)}) %collective-permute-start.3) | collective-permute-done | bytes 540704 | tf_op jit(solution)/shard_map/ppermute | solution.py:376
  43.3 9.3 %collective-permute-start.6 = (bf16[1088,128]{1,0:T(8,128)(2,1)}, bf16[1088,128]{1,0:T(8,128)(2,1)S(1)}, u32[]{:S(2)}, u32[]{:S(2)}) collective-permute-start(bf16[1088,128]{1,0:T(8,128)(2,1)} %slice.27), channel_id=1, source_target_pairs={{0,8},{1,9},{2,10},{3,11},{4,12},{5,13},{6,14},{7,15},{8,0},{9,1},... | collective-permute-start | bytes 835592 | tf_op jit(solution)/shard_map/ppermute | solution.py:376
  52.5 1.7 slice.26
  54.2 2.3 %collective-permute-start.5 = (bf16[1024,128]{1,0:T(8,128)(2,1)}, bf16[1024,128]{1,0:T(8,128)(2,1)}, u32[]{:S(2)}, u32[]{:S(2)}) collective-permute-start(bf16[1024,128]{1,0:T(8,128)(2,1)} %slice.26), channel_id=1, source_target_pairs={{0,16},{1,17},{2,18},{3,19},{4,20},{5,21},{6,22},{7,23},{8,24},{9,... | collective-permute-start | bytes 786440 | tf_op jit(solution)/shard_map/ppermute | solution.py:376
  56.6 0.5 collective-permute-start.13
  57.4 0.7 copy-done.10
  58.5 5.8 %pool_weights.2 = (bf16[3,512,512]{2,1,0:T(8,128)(2,1)}, bf16[3,512,512]{2,1,0:T(8,128)(2,1)}) custom-call(bf16[2112,128]{1,0:T(8,128)(2,1)} %constant_dynamic-update-slice_fusion.refs_0_, bf16[2112,128]{1,0:T(8,128)(2,1)} %collective-permute-done.3.refs_1_, bf16[2112,128]{1,0:T(8,128)(2,1)} %copy-done.2), custom_call_target="tpu_custom_call" | custom-call | flops 150994944 | bytes 3145728 | tf_op jit(solution)/shard_map/pool_weights/pallas_call | solution.py:431
  64.3 2.1 %collective-permute-done.6.refs_0_.refs_4_ = bf16[1088,128]{1,0:T(8,128)(2,1)S(1)} collective-permute-done((bf16[1088,128]{1,0:T(8,128)(2,1)}, bf16[1088,128]{1,0:T(8,128)(2,1)S(1)}, u32[]{:S(2)}, u32[]{:S(2)}) %collective-permute-start.6) | collective-permute-done | bytes 278560 | tf_op jit(solution)/shard_map/ppermute | solution.py:376
  66.9 0.7 pad_add_fusion.at_ref
  67.6 2.9 %pool_weights.3 = (bf16[1,512,512]{2,1,0:T(8,128)(2,1)}, bf16[1,512,512]{2,1,0:T(8,128)(2,1)}) custom-call(bf16[1088,128]{1,0:T(8,128)(2,1)} %copy-done.5), custom_call_target="tpu_custom_call" | custom-call | flops 50331648 | bytes 1048576 | tf_op jit(solution)/shard_map/pool_weights/pallas_call | solution.py:431
  70.5 19.5 %design_values.1 = (s16[528,512]{1,0:T(8,128)(2,1)}, s16[528,512]{1,0:T(8,128)(2,1)}, f32[128,512]{1,0:T(8,128)}) custom-call(s32[3]{0:T(128)} %pad_add_fusion.at_ref, bf16[2112,128]{1,0:T(8,128)(2,1)} %constant_dynamic-update-slice_fusion.refs_0_, bf16[2112,128]{1,0:T(8,128)(2,1)} %collective-permute-done.3.refs_1_, bf16[2112,128]{1,0:T(8,128)(2,1)} %copy-done.2, ...), custom_call_target="tpu_custom_call" | custom-call | flops 10737418240 | bytes 14680064 | tf_op jit(solution)/shard_map/design_values/pallas_call | solution.py:458
  90.0 2.7 %collective-permute-start.20 = (s16[528,512]{1,0:T(8,128)(2,1)}, s16[528,512]{1,0:T(8,128)(2,1)}, u32[]{:S(2)}, u32[]{:S(2)}) collective-permute-start(s16[528,512]{1,0:T(8,128)(2,1)} %get-tuple-element.44.refs_0_), channel_id=1, source_target_pairs={{0,2},{1,3},{2,6},{3,7},{4,0},{5,1},{6,4},{7,5},{8,10},{9,11},{10,... | collective-permute-start | bytes 1622024 | tf_op jit(solution)/shard_map/ppermute | solution.py:376
  92.7 0.5 collective-permute-start.17
  93.9 11.6 %collective-permute-done.20.refs_2_ = s16[528,512]{1,0:T(8,128)(2,1)} collective-permute-done((s16[528,512]{1,0:T(8,128)(2,1)}, s16[528,512]{1,0:T(8,128)(2,1)}, u32[]{:S(2)}, u32[]{:S(2)}) %collective-permute-start.20) | collective-permute-done | bytes 540704 | tf_op jit(solution)/shard_map/ppermute | solution.py:376
  105.5 1.8 %collective-permute-done.17.code2 = s16[528,512]{1,0:T(8,128)(2,1)S(1)} collective-permute-done((s16[528,512]{1,0:T(8,128)(2,1)}, s16[528,512]{1,0:T(8,128)(2,1)S(1)}, u32[]{:S(2)}, u32[]{:S(2)}) %collective-permute-start.17) | collective-permute-done | bytes 540704 | tf_op jit(solution)/shard_map/ppermute | solution.py:376
  107.2 0.8 slice.29
  108.0 2.2 %collective-permute-start.19 = (s16[272,512]{1,0:T(8,128)(2,1)}, s16[272,512]{1,0:T(8,128)(2,1)S(1)}, u32[]{:S(2)}, u32[]{:S(2)}) collective-permute-start(s16[272,512]{1,0:T(8,128)(2,1)} %slice.29), channel_id=1, source_target_pairs={{0,8},{1,9},{2,10},{3,11},{4,12},{5,13},{6,14},{7,15},{8,0},{9,1},... | collective-permute-start | bytes 835592 | tf_op jit(solution)/shard_map/ppermute | solution.py:376
  110.2 0.9 copy-done.1
  111.1 0.7 slice.28
  111.8 1.7 collective-permute-start.21
  113.5 3.9 %near_columns.1.refs_4_.refs_2_ = bf16[3,1024,512]{2,1,0:T(8,128)(2,1)} custom-call(s16[528,512]{1,0:T(8,128)(2,1)} %get-tuple-element.42.code0, s16[528,512]{1,0:T(8,128)(2,1)} %copy-done.1, s16[528,512]{1,0:T(8,128)(2,1)} %copy-done), custom_call_target="tpu_custom_call" | custom-call | bytes 6291456 | tf_op jit(solution)/shard_map/near_columns/pallas_call | solution.py:497
  117.5 16.4 %gram_rows.4.refs_5_ = f32[2,2048,2048]{2,1,0:T(8,128)} custom-call(s32[3]{0:T(128)} %pad_add_fusion.at_ref, s16[528,512]{1,0:T(8,128)(2,1)} %get-tuple-element.44.refs_0_, s16[528,512]{1,0:T(8,128)(2,1)} %collective-permute-done.22.refs_1_, s16[528,512]{1,0:T(8,128)(2,1)} %collective-permute-done.20.refs_2_, ...), custom_call_target="tpu_custom_call" | custom-call | flops 12884901888 | bytes 4194304 | tf_op jit(solution)/shard_map/gram_rows/pallas_call | solution.py:549
  133.8 1.2 collective-permute-start.24
  135.1 0.7 copy-done.6
  135.8 4.1 %far_columns.1 = (bf16[1,1024,512]{2,1,0:T(8,128)(2,1)}, f32[128,2048]{1,0:T(8,128)}) custom-call(s32[3]{0:T(128)} %pad_add_fusion.at_ref, f32[128,512]{1,0:T(8,128)} %get-tuple-element.41.rows_ref, s16[528,512]{1,0:T(8,128)(2,1)} %copy-done.1, s16[528,512]{1,0:T(8,128)(2,1)} %copy-done, s16[256,512]{1,0:T(8,128)(2,1)} %collective-permute-done.18.upper, ...), custom_call_target="tpu_custom_call" | custom-call | bytes 5242880 | tf_op jit(solution)/shard_map/far_columns/pallas_call | solution.py:507
  139.8 8.7 %gram_rows.5.refs_4_ = f32[2,2048,2048]{2,1,0:T(8,128)} custom-call(s32[3]{0:T(128)} %pad_add_fusion.at_ref, s16[528,512]{1,0:T(8,128)(2,1)} %get-tuple-element.44.refs_0_, s16[528,512]{1,0:T(8,128)(2,1)} %collective-permute-done.22.refs_1_, s16[528,512]{1,0:T(8,128)(2,1)} %collective-permute-done.20.refs_2_, ...), custom_call_target="tpu_custom_call", output_to_operand_aliasing={{}: (6, {})} | custom-call | flops 4294967296 | bytes 4194304 | tf_op jit(solution)/shard_map/gram_rows/pallas_call | solution.py:549
  149.0 11.9 %gram_rows.6.refs_4_ = f32[2,2048,2048]{2,1,0:T(8,128)} custom-call(s32[3]{0:T(128)} %pad_add_fusion.at_ref, s16[528,512]{1,0:T(8,128)(2,1)} %collective-permute-done.21.refs_0_, s16[528,512]{1,0:T(8,128)(2,1)} %collective-permute-done.26.refs_1_, bf16[3,1024,512]{2,1,0:T(8,128)(2,1)} %near_columns.1.refs_4_.refs_2_, ...), custom_call_target="tpu_custom_call", output_to_operand_aliasing={{}: (5, {})} | custom-call | flops 8589934592 | bytes 4194304 | tf_op jit(solution)/shard_map/gram_rows/pallas_call | solution.py:549
  161.0 11.9 %gram_rows.7 = f32[2,2048,2048]{2,1,0:T(8,128)} custom-call(s32[3]{0:T(128)} %pad_add_fusion.at_ref, s16[528,512]{1,0:T(8,128)(2,1)} %copy-done.4, s16[528,512]{1,0:T(8,128)(2,1)} %collective-permute-done.25.refs_1_, bf16[3,1024,512]{2,1,0:T(8,128)(2,1)} %near_columns.1.refs_4_.refs_2_, ...), custom_call_target="tpu_custom_call", output_to_operand_aliasing={{}: (5, {})} | custom-call | flops 8589934592 | bytes 4194304 | tf_op jit(solution)/shard_map/gram_rows/pallas_call | solution.py:549
  (58 shorter events, 3.2 us)
Async XLA Ops:
  0.6 14.2 %collective-permute-start.1 = (bf16[512,128]{1,0:T(8,128)(2,1)}, bf16[512,128]{1,0:T(8,128)(2,1)S(1)}, u32[]{:S(2)}, u32[]{:S(2)}) collective-permute-start(bf16[512,128]{1,0:T(8,128)(2,1)} %param.6), channel_id=1, source_target_pairs={{0,4},{1,5},{2,6},{3,7},{4,0},{5,1},{6,2},{7,3},{8,12},{9,13},{10,... | collective-permute-start | bytes 393224 | tf_op jit(solution)/shard_map/ppermute | solution.py:376
  4.7 9.4 %collective-permute-start = (bf16[512,128]{1,0:T(8,128)(2,1)}, bf16[512,128]{1,0:T(8,128)(2,1)S(1)}, u32[]{:S(2)}, u32[]{:S(2)}) collective-permute-start(bf16[512,128]{1,0:T(8,128)(2,1)} %param.6), channel_id=1, source_target_pairs={{0,2},{1,3},{2,0},{3,1},{4,6},{5,7},{6,4},{7,5},{8,10},{9,11},{10,... | collective-permute-start | bytes 393224 | tf_op jit(solution)/shard_map/ppermute | solution.py:376
  6.3 9.2 %collective-permute-start.2 = (bf16[512,128]{1,0:T(8,128)(2,1)}, bf16[512,128]{1,0:T(8,128)(2,1)S(1)}, u32[]{:S(2)}, u32[]{:S(2)}) collective-permute-start(bf16[512,128]{1,0:T(8,128)(2,1)} %param.6), channel_id=1, source_target_pairs={{0,6},{1,7},{2,4},{3,5},{4,2},{5,3},{6,0},{7,1},{8,14},{9,15},{10,... | collective-permute-start | bytes 393224 | tf_op jit(solution)/shard_map/ppermute | solution.py:376
  6.3 16.8 %all-to-all-start = ((bf16[4,512,256]{2,1,0:T(8,128)(2,1)}), bf16[4,512,256]{2,1,0:T(8,128)(2,1)S(1)}, u32[]{:S(2)}, u32[]{:S(2)}) async-start(bf16[4,512,256]{2,1,0:T(8,128)(2,1)} %bitcast.43), calls=%async_computation | async-start | bytes 2097152 | tf_op jit(solution)/shard_map/all_to_all | solution.py:386
  23.2 33.4 %copy-start.3 = (bf16[4,512,256]{2,1,0:T(8,128)(2,1)}, bf16[4,512,256]{2,1,0:T(8,128)(2,1)S(1)}, u32[]{:S(2)}) copy-start(bf16[4,512,256]{2,1,0:T(8,128)(2,1)S(1)} %all-to-all-done.refs_10_) | copy-start | bytes 3145732
  23.2 16.9 %collective-permute-start.4 = (bf16[2112,128]{1,0:T(8,128)(2,1)}, bf16[2112,128]{1,0:T(8,128)(2,1)S(1)}, u32[]{:S(2)}, u32[]{:S(2)}) collective-permute-start(bf16[2112,128]{1,0:T(8,128)(2,1)} %constant_dynamic-update-slice_fusion.refs_0_), channel_id=1, source_target_pairs={{0,16},{1,17},{2,18},{3,19},{4,20},{5,21},{6,22},{7,23},{8,24},{9,... | collective-permute-start | bytes 1622024 | tf_op jit(solution)/shard_map/ppermute | solution.py:376
  24.6 18.6 %collective-permute-start.3 = (bf16[2112,128]{1,0:T(8,128)(2,1)}, bf16[2112,128]{1,0:T(8,128)(2,1)}, u32[]{:S(2)}, u32[]{:S(2)}) collective-permute-start(bf16[2112,128]{1,0:T(8,128)(2,1)} %constant_dynamic-update-slice_fusion.refs_0_), channel_id=1, source_target_pairs={{0,8},{1,9},{2,10},{3,11},{4,12},{5,13},{6,14},{7,15},{8,0},{9,1},... | collective-permute-start | bytes 1622024 | tf_op jit(solution)/shard_map/ppermute | solution.py:376
  26.4 27.8 %collective-permute-start.10 = (bf16[512,256]{1,0:T(8,128)(2,1)S(1)}, bf16[512,256]{1,0:T(8,128)(2,1)S(1)}, u32[]{:S(2)}, u32[]{:S(2)}) collective-permute-start(bf16[512,256]{1,0:T(8,128)(2,1)S(1)} %get-tuple-element.50), channel_id=1, source_target_pairs={{0,6},{1,7},{2,14},{3,15},{4,22},{5,23},{6,30},{7,31},{8,4},{9,5},... | collective-permute-start | bytes 786440 | tf_op jit(solution)/shard_map/ppermute | solution.py:376
  30.0 26.6 %collective-permute-start.9 = (bf16[512,256]{1,0:T(8,128)(2,1)S(1)}, bf16[512,256]{1,0:T(8,128)(2,1)S(1)}, u32[]{:S(2)}, u32[]{:S(2)}) collective-permute-start(bf16[512,256]{1,0:T(8,128)(2,1)S(1)} %get-tuple-element.51), channel_id=1, source_target_pairs={{0,4},{1,5},{2,12},{3,13},{4,20},{5,21},{6,28},{7,29},{8,6},{9,7},... | collective-permute-start | bytes 786440 | tf_op jit(solution)/shard_map/ppermute | solution.py:376
  31.5 25.1 %collective-permute-start.8 = (bf16[512,256]{1,0:T(8,128)(2,1)S(1)}, bf16[512,256]{1,0:T(8,128)(2,1)S(1)}, u32[]{:S(2)}, u32[]{:S(2)}) collective-permute-start(bf16[512,256]{1,0:T(8,128)(2,1)S(1)} %get-tuple-element.52), channel_id=1, source_target_pairs={{0,2},{1,3},{2,10},{3,11},{4,18},{5,19},{6,26},{7,27},{8,0},{9,1},... | collective-permute-start | bytes 786440 | tf_op jit(solution)/shard_map/ppermute | solution.py:376
  40.1 18.5 %copy-start.2 = (bf16[2112,128]{1,0:T(8,128)(2,1)}, bf16[2112,128]{1,0:T(8,128)(2,1)S(1)}, u32[]{:S(2)}) copy-start(bf16[2112,128]{1,0:T(8,128)(2,1)S(1)} %collective-permute-done.4.refs_2_) | copy-start | bytes 1622020
  40.1 17.1 %collective-permute-start.7 = (bf16[512,256]{1,0:T(8,128)(2,1)S(1)}, bf16[512,256]{1,0:T(8,128)(2,1)S(1)}, u32[]{:S(2)}, u32[]{:S(2)}) collective-permute-start(bf16[512,256]{1,0:T(8,128)(2,1)S(1)} %get-tuple-element.53), channel_id=1, source_target_pairs={{0,0},{1,1},{2,8},{3,9},{4,16},{5,17},{6,24},{7,25},{8,2},{9,3},{1... | collective-permute-start | bytes 786440 | tf_op jit(solution)/shard_map/ppermute | solution.py:376
  43.3 23.1 %collective-permute-start.6 = (bf16[1088,128]{1,0:T(8,128)(2,1)}, bf16[1088,128]{1,0:T(8,128)(2,1)S(1)}, u32[]{:S(2)}, u32[]{:S(2)}) collective-permute-start(bf16[1088,128]{1,0:T(8,128)(2,1)} %slice.27), channel_id=1, source_target_pairs={{0,8},{1,9},{2,10},{3,11},{4,12},{5,13},{6,14},{7,15},{8,0},{9,1},... | collective-permute-start | bytes 835592 | tf_op jit(solution)/shard_map/ppermute | solution.py:376
  54.2 2.9 %copy-start.7 = (bf16[512,256]{1,0:T(8,128)(2,1)}, bf16[512,256]{1,0:T(8,128)(2,1)S(1)}, u32[]{:S(2)}) copy-start(bf16[512,256]{1,0:T(8,128)(2,1)S(1)} %collective-permute-done.10.refs_14_) | copy-start | bytes 786436
  54.2 10.1 %collective-permute-start.5 = (bf16[1024,128]{1,0:T(8,128)(2,1)}, bf16[1024,128]{1,0:T(8,128)(2,1)}, u32[]{:S(2)}, u32[]{:S(2)}) collective-permute-start(bf16[1024,128]{1,0:T(8,128)(2,1)} %slice.26), channel_id=1, source_target_pairs={{0,16},{1,17},{2,18},{3,19},{4,20},{5,21},{6,22},{7,23},{8,24},{9,... | collective-permute-start | bytes 786440 | tf_op jit(solution)/shard_map/ppermute | solution.py:376
  56.6 0.7 copy-start.8
  56.6 13.9 %collective-permute-start.11 = (bf16[2112,128]{1,0:T(8,128)(2,1)}, bf16[2112,128]{1,0:T(8,128)(2,1)}, u32[]{:S(2)}, u32[]{:S(2)}) collective-permute-start(bf16[2112,128]{1,0:T(8,128)(2,1)} %constant_dynamic-update-slice_fusion.refs_0_), channel_id=1, source_target_pairs={{0,1},{1,0},{2,3},{3,2},{4,5},{5,4},{6,7},{7,6},{8,9},{9,8},{10,11... | collective-permute-start | bytes 1622024 | tf_op jit(solution)/shard_map/ppermute | solution.py:376
  56.6 0.8 copy-start.9
  56.6 13.9 %collective-permute-start.13 = (bf16[2112,128]{1,0:T(8,128)(2,1)S(1)}, bf16[2112,128]{1,0:T(8,128)(2,1)}, u32[]{:S(2)}, u32[]{:S(2)}) collective-permute-start(bf16[2112,128]{1,0:T(8,128)(2,1)S(1)} %collective-permute-done.4.refs_2_), channel_id=1, source_target_pairs={{0,1},{1,0},{2,3},{3,2},{4,5},{5,4},{6,7},{7,6},{8,9},{9,8},{10,11... | collective-permute-start | bytes 1622024 | tf_op jit(solution)/shard_map/ppermute | solution.py:376
  57.4 0.7 copy-start.10
  58.1 12.4 %collective-permute-start.12 = (bf16[2112,128]{1,0:T(8,128)(2,1)}, bf16[2112,128]{1,0:T(8,128)(2,1)}, u32[]{:S(2)}, u32[]{:S(2)}) collective-permute-start(bf16[2112,128]{1,0:T(8,128)(2,1)} %collective-permute-done.3.refs_1_), channel_id=1, source_target_pairs={{0,1},{1,0},{2,3},{3,2},{4,5},{5,4},{6,7},{7,6},{8,9},{9,8},{10,11... | collective-permute-start | bytes 1622024 | tf_op jit(solution)/shard_map/ppermute | solution.py:376
  66.4 1.2 copy-start.5
  66.4 4.1 %collective-permute-start.15 = (bf16[1088,128]{1,0:T(8,128)(2,1)S(1)}, bf16[1088,128]{1,0:T(8,128)(2,1)}, u32[]{:S(2)}, u32[]{:S(2)}) collective-permute-start(bf16[1088,128]{1,0:T(8,128)(2,1)S(1)} %collective-permute-done.6.refs_0_.refs_4_), channel_id=1, source_target_pairs={{0,1},{1,0},{2,3},{3,2},{4,5},{5,4},{6,7},{7,6},{8,9},{9,8},{10,11... | collective-permute-start | bytes 835592 | tf_op jit(solution)/shard_map/ppermute | solution.py:376
  66.4 4.1 %collective-permute-start.14 = (bf16[1024,128]{1,0:T(8,128)(2,1)}, bf16[1024,128]{1,0:T(8,128)(2,1)}, u32[]{:S(2)}, u32[]{:S(2)}) collective-permute-start(bf16[1024,128]{1,0:T(8,128)(2,1)} %collective-permute-done.5.refs_3_), channel_id=1, source_target_pairs={{0,1},{1,0},{2,3},{3,2},{4,5},{5,4},{6,7},{7,6},{8,9},{9,8},{10,11... | collective-permute-start | bytes 786440 | tf_op jit(solution)/shard_map/ppermute | solution.py:376
  90.0 15.4 %collective-permute-start.20 = (s16[528,512]{1,0:T(8,128)(2,1)}, s16[528,512]{1,0:T(8,128)(2,1)}, u32[]{:S(2)}, u32[]{:S(2)}) collective-permute-start(s16[528,512]{1,0:T(8,128)(2,1)} %get-tuple-element.44.refs_0_), channel_id=1, source_target_pairs={{0,2},{1,3},{2,6},{3,7},{4,0},{5,1},{6,4},{7,5},{8,10},{9,11},{10,... | collective-permute-start | bytes 1622024 | tf_op jit(solution)/shard_map/ppermute | solution.py:376
  92.7 14.5 %collective-permute-start.17 = (s16[528,512]{1,0:T(8,128)(2,1)}, s16[528,512]{1,0:T(8,128)(2,1)S(1)}, u32[]{:S(2)}, u32[]{:S(2)}) collective-permute-start(s16[528,512]{1,0:T(8,128)(2,1)} %get-tuple-element.42.code0), channel_id=1, source_target_pairs={{0,16},{1,17},{2,18},{3,19},{4,20},{5,21},{6,22},{7,23},{8,24},{9,... | collective-permute-start | bytes 1622024 | tf_op jit(solution)/shard_map/ppermute | solution.py:376
  93.2 17.0 %collective-permute-start.16 = (s16[528,512]{1,0:T(8,128)(2,1)}, s16[528,512]{1,0:T(8,128)(2,1)S(1)}, u32[]{:S(2)}, u32[]{:S(2)}) collective-permute-start(s16[528,512]{1,0:T(8,128)(2,1)} %get-tuple-element.42.code0), channel_id=1, source_target_pairs={{0,8},{1,9},{2,10},{3,11},{4,12},{5,13},{6,14},{7,15},{8,0},{9,1},... | collective-permute-start | bytes 1622024 | tf_op jit(solution)/shard_map/ppermute | solution.py:376
  93.8 23.7 %collective-permute-start.22 = (s16[528,512]{1,0:T(8,128)(2,1)}, s16[528,512]{1,0:T(8,128)(2,1)}, u32[]{:S(2)}, u32[]{:S(2)}) collective-permute-start(s16[528,512]{1,0:T(8,128)(2,1)} %get-tuple-element.44.refs_0_), channel_id=1, source_target_pairs={{0,1},{1,0},{2,3},{3,2},{4,5},{5,4},{6,7},{7,6},{8,9},{9,8},{10,11... | collective-permute-start | bytes 1622024 | tf_op jit(solution)/shard_map/ppermute | solution.py:376
  105.5 12.0 %collective-permute-start.23 = (s16[528,512]{1,0:T(8,128)(2,1)}, s16[528,512]{1,0:T(8,128)(2,1)}, u32[]{:S(2)}, u32[]{:S(2)}) collective-permute-start(s16[528,512]{1,0:T(8,128)(2,1)} %collective-permute-done.20.refs_2_), channel_id=1, source_target_pairs={{0,1},{1,0},{2,3},{3,2},{4,5},{5,4},{6,7},{7,6},{8,9},{9,8},{10,11... | collective-permute-start | bytes 1622024 | tf_op jit(solution)/shard_map/ppermute | solution.py:376
  107.2 6.3 %copy-start = (s16[528,512]{1,0:T(8,128)(2,1)}, s16[528,512]{1,0:T(8,128)(2,1)S(1)}, u32[]{:S(2)}) copy-start(s16[528,512]{1,0:T(8,128)(2,1)S(1)} %collective-permute-done.17.code2) | copy-start | bytes 1622020
  108.0 27.0 %collective-permute-start.19 = (s16[272,512]{1,0:T(8,128)(2,1)}, s16[272,512]{1,0:T(8,128)(2,1)S(1)}, u32[]{:S(2)}, u32[]{:S(2)}) collective-permute-start(s16[272,512]{1,0:T(8,128)(2,1)} %slice.29), channel_id=1, source_target_pairs={{0,8},{1,9},{2,10},{3,11},{4,12},{5,13},{6,14},{7,15},{8,0},{9,1},... | collective-permute-start | bytes 835592 | tf_op jit(solution)/shard_map/ppermute | solution.py:376
  110.2 0.9 copy-start.1
  111.8 23.3 %collective-permute-start.18 = (s16[256,512]{1,0:T(8,128)(2,1)}, s16[256,512]{1,0:T(8,128)(2,1)}, u32[]{:S(2)}, u32[]{:S(2)}) collective-permute-start(s16[256,512]{1,0:T(8,128)(2,1)} %slice.28), channel_id=1, source_target_pairs={{0,16},{1,17},{2,18},{3,19},{4,20},{5,21},{6,22},{7,23},{8,24},{9,... | collective-permute-start | bytes 786440 | tf_op jit(solution)/shard_map/ppermute | solution.py:376
  111.8 22.0 %collective-permute-start.21 = (s16[528,512]{1,0:T(8,128)(2,1)}, s16[528,512]{1,0:T(8,128)(2,1)}, u32[]{:S(2)}, u32[]{:S(2)}) collective-permute-start(s16[528,512]{1,0:T(8,128)(2,1)} %collective-permute-done.20.refs_2_), channel_id=1, source_target_pairs={{0,2},{1,3},{2,6},{3,7},{4,0},{5,1},{6,4},{7,5},{8,10},{9,11},{10,... | collective-permute-start | bytes 1622024 | tf_op jit(solution)/shard_map/ppermute | solution.py:376
  133.8 14.7 %collective-permute-start.24 = (s16[528,512]{1,0:T(8,128)(2,1)}, s16[528,512]{1,0:T(8,128)(2,1)S(1)}, u32[]{:S(2)}, u32[]{:S(2)}) collective-permute-start(s16[528,512]{1,0:T(8,128)(2,1)} %collective-permute-done.21.refs_0_), channel_id=1, source_target_pairs={{0,2},{1,3},{2,6},{3,7},{4,0},{5,1},{6,4},{7,5},{8,10},{9,11},{10,... | collective-permute-start | bytes 1622024 | tf_op jit(solution)/shard_map/ppermute | solution.py:376
  135.0 14.0 %collective-permute-start.26 = (s16[528,512]{1,0:T(8,128)(2,1)}, s16[528,512]{1,0:T(8,128)(2,1)}, u32[]{:S(2)}, u32[]{:S(2)}) collective-permute-start(s16[528,512]{1,0:T(8,128)(2,1)} %collective-permute-done.21.refs_0_), channel_id=1, source_target_pairs={{0,1},{1,0},{2,3},{3,2},{4,5},{5,4},{6,7},{7,6},{8,9},{9,8},{10,11... | collective-permute-start | bytes 1622024 | tf_op jit(solution)/shard_map/ppermute | solution.py:376
  135.1 0.7 copy-start.6
  148.5 12.5 %copy-start.4 = (s16[528,512]{1,0:T(8,128)(2,1)}, s16[528,512]{1,0:T(8,128)(2,1)S(1)}, u32[]{:S(2)}) copy-start(s16[528,512]{1,0:T(8,128)(2,1)S(1)} %collective-permute-done.24.refs_0_) | copy-start | bytes 1622020
  148.5 12.5 %collective-permute-start.25 = (s16[528,512]{1,0:T(8,128)(2,1)S(1)}, s16[528,512]{1,0:T(8,128)(2,1)}, u32[]{:S(2)}, u32[]{:S(2)}) collective-permute-start(s16[528,512]{1,0:T(8,128)(2,1)S(1)} %collective-permute-done.24.refs_0_), channel_id=1, source_target_pairs={{0,1},{1,0},{2,3},{3,2},{4,5},{5,4},{6,7},{7,6},{8,9},{9,8},{10,11... | collective-permute-start | bytes 1622024 | tf_op jit(solution)/shard_map/ppermute | solution.py:376

commit v4 on v3

--- a/solution.py
+++ b/solution.py
@@ -207,9 +207,8 @@
     out = []
     for side, refs in zip((core, 1 - core), sides):
         for r in range(4):
-            ref, first = (refs[d], r) if d < 3 else (refs[3 + r // 2], r % 2)
             at = pl.multiple_of((jnp.bitwise_xor(z, r) * 2 + side) * part, part)
-            source = ref.at[pl.ds(first * envs, envs)]
+            source = refs[d].at[pl.ds(r * envs, envs)]
             out.append(pltpu.make_async_copy(source, env.at[:, pl.ds(at, part)], sems.at[len(out)]))
     for i in range(2):
         source = weights_from[i].at[d] if d < 3 else weights_from[2 + i].at[0]
@@ -218,9 +217,9 @@
 
 
 def design_kernel(at_ref, *refs):
-    sides, cols, panels, weights_from = (refs[0:5], refs[5:10]), refs[10], refs[11:15], refs[15:19]
-    cols_code, panel_code, rows_out = refs[19:22]
-    cols_pts, panel_pts, env, weights, cols_sum, panel_sum, point_sems, group_sems = refs[22:]
+    sides, cols, panels, weights_from = (refs[0:4], refs[4:8]), refs[8], refs[9:13], refs[13:17]
+    cols_code, panel_code, rows_out = refs[17:20]
+    cols_pts, panel_pts, env, weights, cols_sum, panel_sum, point_sems, group_sems = refs[20:]
     q, z = at_ref[0], at_ref[1]
     n_pts, comps = panels[0].shape
     points = []
@@ -270,13 +269,11 @@
             value_pair(ref[pl.ds(0, rows), :], lane_scale(ref[pl.ds(rows, 16), :], 1.0), out_ref.at[0])
 
 
-def far_columns_kernel(at_ref, rows_ref, code1, code2, upper, lower, out_ref, design_ref):
+def far_columns_kernel(at_ref, rows_ref, code1, code2, code3, out_ref, design_ref):
     q = at_ref[0]
     rows = out_ref.shape[1] // 2
-    half, share, n_pts = upper.shape[0], rows_ref.shape[0], rows_ref.shape[1]
-    scale = lane_scale(lower[pl.ds(rows - half, 16), :], 1.0)
-    codes = jnp.concatenate([upper[...], lower[pl.ds(0, rows - half), :]], axis=0)
-    value_pair(codes, scale, out_ref.at[0])
+    share, n_pts = rows_ref.shape
+    value_pair(code3[pl.ds(0, rows), :], lane_scale(code3[pl.ds(rows, 16), :], 1.0), out_ref.at[0])
     start = pl.multiple_of(q * share, share)
 
     def put(d, value):
@@ -284,16 +281,8 @@
         design_ref[:, pl.ds(at, n_pts)] = value
 
     put(0, rows_ref[...])
-    for d, ref in ((1, code1), (2, code2)):
+    for d, ref in enumerate((code1, code2, code3), 1):
         put(d, decode(ref[pl.ds(start, share), :], lane_scale(ref[pl.ds(rows, 16), :], 1.0)))
-
-    @pl.when(start < half)
-    def _():
-        put(3, decode(upper[pl.ds(start, share), :], scale))
-
-    @pl.when(start >= half)
-    def _():
-        put(3, decode(lower[pl.ds(pl.multiple_of(start - half, share), share), :], scale))
 
 
 def gray(value):
@@ -414,7 +403,7 @@
             table[:, part:],
         ]
     )
-    own, cols_pts, quarters = lax.optimization_barrier((own, cols_pts, quarters))
+    own, cols_pts, quarters, at = lax.optimization_barrier((own, cols_pts, quarters, at))
     near_x, near_y = moved(own, along_x), moved(own, along_y)
     swap_own = moved(own, to_core)
 
@@ -442,15 +431,15 @@
             name="pool_weights",
         )(*tables)
 
-    far_upper, far_lower = moved(near_x[: 2 * envs], along_y), moved(near_y[2 * envs :], along_x)
+    far = moved(near_y, along_x)
     near_weights = pool_weights([own, near_x, near_y])
-    far_upper, far_lower, *rest = lax.optimization_barrier(
-        (far_upper, far_lower, *near_weights, *panel_pts)
-    )
+    near_x, near_y, *near_weights = lax.optimization_barrier((near_x, near_y, *near_weights))
+    swap_x, swap_y = moved(near_x, to_core), moved(near_y, to_core)
+    far, *rest = lax.optimization_barrier((far, *near_weights, *panel_pts))
     near_weights, panel_pts = rest[:2], rest[2:]
-    mine = (own, near_x, near_y, far_upper, far_lower)
-    other = (swap_own, *(moved(e, to_core) for e in mine[1:]))
-    weights = (*near_weights, *pool_weights([far_lower]))
+    mine = (own, near_x, near_y, far)
+    other = (swap_own, swap_x, swap_y, moved(far, to_core))
+    weights = (*near_weights, *pool_weights([far]))
 
     anywhere = pl.BlockSpec(memory_space=pl.ANY)
 
@@ -460,7 +449,7 @@
         grid_spec=pltpu.PrefetchScalarGridSpec(
             num_scalar_prefetch=1,
             grid=(1,),
-            in_specs=[anywhere] * 19,
+            in_specs=[anywhere] * 17,
             out_specs=[
                 whole((pad, n_pts)),
                 whole((n_pts + 16, n_rows)),
@@ -487,11 +476,10 @@
         name="design_values",
     )(at, *mine, *other, cols_pts, *panel_pts, *weights)
 
-    half = n_rows // 2
     held = [panel_code, moved(panel_code, along_z)]
     from_x, from_y = moved(cols_code, along_x), moved(cols_code, along_y)
     swapped = [moved(panel_code, to_core)]
-    upper, lower = moved(from_x[:half], along_y), moved(from_y[half:], along_x)
+    from_far = moved(from_y, along_x)
     width = groups * n_pts
     code_spec = whole((pad, n_pts))
     near = pl.pallas_call(
@@ -513,8 +501,7 @@
                 whole((n_rows // groups, n_pts)),
                 code_spec,
                 code_spec,
-                whole((half, n_pts)),
-                whole((pad - half, n_pts)),
+                code_spec,
             ],
             out_specs=[whole((1, 2 * n_rows, n_pts)), whole((n_rows // groups, width))],
         ),
@@ -525,7 +512,7 @@
         compiler_params=pltpu.CompilerParams(vmem_limit_bytes=VMEM_LIMIT),
         cost_estimate=cost(0, 5 * MIB),
         name="far_columns",
-    )(at, own_rows, from_x, from_y, upper, lower)
+    )(at, own_rows, from_x, from_y, from_far)
 
     panel_spec = whole((n_pts + 16, n_rows))
 

time: 174 us -> 170 us (0.977)
  waiting for transfers between devices: 31.6 us -> 42.8 us
  local copies, waits for them, and re-layouts: 12.6 us -> 5.14 us
  starting transfers between devices: 40 us -> 33.1 us
    ppermute x27 -> x24, waiting for transfers between devices: 25.8 us -> 34.1 us  [moved(): return lax.ppermute(value, BOTH, permutation(to))]
    ppermute x27 -> x24, starting transfers between devices: 36.1 us -> 28.9 us  [moved(): return lax.ppermute(value, BOTH, permutation(to))]
    slice x4 -> x0, local copies, waits for them, and re-layouts: 3.91 us -> none  [the longest x1 1.68 us: on_device(): near_x[:2 * envs]]
    unnamed x27 -> x15, local copies, waits for them, and re-layouts: 6.68 us -> 2.81 us
    all_to_all x1, waiting for transfers between devices: 5.81 us -> 8.65 us  [on_device(): cols_pts = lax.all_to_all(quarters, 'rows', 0, 0, tiled=True)]
  transfers between devices with their start and end apart: 28 -> 25, of which waited for: 6 -> 8; matrix products, arithmetic and copies ran while one was open for 7% -> 4% of each run, Pallas kernels for 31% -> 32%
where the time goes in v4:
time: 170 us; the launch traced here: 169 us
  Pallas kernels  84.9 us (50%)
  waiting for transfers between devices  42.8 us (25%)
  starting transfers between devices  33.1 us (19%)
  local copies, waits for them, and re-layouts  5.14 us (3%)
  other arithmetic  2.76 us (2%)
    pallas_call x4, Pallas kernels, gram_rows(): pl.pallas_call(functools.partial(gram_kernel, steps, first, n_near), grid...  48.9 us
    ppermute x24, waiting for transfers between devices, moved(): return lax.ppermute(value, BOTH, permutation(to))  34.1 us
    ppermute x24, starting transfers between devices, moved(): return lax.ppermute(value, BOTH, permutation(to))  28.9 us
    pallas_call x1, Pallas kernels, on_device(): pl.pallas_call(design_kernel, grid_spec=pltpu.PrefetchScalarGridSpec(num_...  19.5 us
    pallas_call x2, Pallas kernels, pool_weights(): pl.pallas_call(weights_kernel, grid=(1,), in_specs=[pl.BlockSpec((64, par...  8.82 us
    all_to_all x1, waiting for transfers between devices, on_device(): cols_pts = lax.all_to_all(quarters, 'rows', 0, 0, tiled=True)  8.65 us
    all_to_all x1, starting transfers between devices, on_device(): cols_pts = lax.all_to_all(quarters, 'rows', 0, 0, tiled=True)  4.24 us
    pallas_call x1, Pallas kernels, on_device(): pl.pallas_call(near_columns_kernel, grid=(3,), in_specs=[code_spec] * 3,...  3.91 us
  transfers between devices with their start and end apart: 25, of which 8 were waited for; matrix products, arithmetic and copies ran while one was open for 4% of the time, Pallas kernels for 32%

profile of v4, /device:TPU:0, one launch (start us, length us, event | category | flops | bytes accessed | tf_op | source)
XLA Modules:
  0.0 169.5 jit_solution(1755391797005463142)
XLA Ops:
  0.6 4.1 %collective-permute-start.1 = (bf16[512,128]{1,0:T(8,128)(2,1)}, bf16[512,128]{1,0:T(8,128)(2,1)S(1)}, u32[]{:S(2)}, u32[]{:S(2)}) collective-permute-start(bf16[512,128]{1,0:T(8,128)(2,1)} %param.6), channel_id=1, source_target_pairs={{0,4},{1,5},{2,6},{3,7},{4,0},{5,1},{6,2},{7,3},{8,12},{9,13},{10,... | collective-permute-start | bytes 393224 | tf_op jit(solution)/shard_map/ppermute | solution.py:365
  4.7 1.6 collective-permute-start
  6.3 4.2 %all-to-all-start = ((bf16[4,512,256]{2,1,0:T(8,128)(2,1)}), bf16[4,512,256]{2,1,0:T(8,128)(2,1)}, u32[]{:S(2)}, u32[]{:S(2)}) async-start(bf16[4,512,256]{2,1,0:T(8,128)(2,1)} %bitcast.43), calls=%async_computation | async-start | bytes 2097152 | tf_op jit(solution)/shard_map/all_to_all | solution.py:375
  10.6 0.7 fusion.6
  11.3 0.7 fusion.2
  12.0 0.7 fusion
  12.7 0.9 constant_dynamic-update-slice_fusion.5
  13.6 0.7 pad_add_fusion.at_ref
  14.3 0.2 concatenate.6
  14.5 0.7 collective-permute-done.2
  15.3 0.0 copy-start.1
  15.3 8.6 %all-to-all-done.refs_8_ = bf16[4,512,256]{2,1,0:T(8,128)(2,1)} async-done(((bf16[4,512,256]{2,1,0:T(8,128)(2,1)}), bf16[4,512,256]{2,1,0:T(8,128)(2,1)}, u32[]{:S(2)}, u32[]{:S(2)}) %all-to-all-start) | async-done | bytes 1048608 | tf_op jit(solution)/shard_map/all_to_all | solution.py:375
  24.0 1.5 collective-permute-start.4
  25.4 0.5 collective-permute-start.3
  26.0 11.3 %collective-permute-done.4.refs_2_ = bf16[2112,128]{1,0:T(8,128)(2,1)} collective-permute-done((bf16[2112,128]{1,0:T(8,128)(2,1)S(1)}, bf16[2112,128]{1,0:T(8,128)(2,1)}, u32[]{:S(2)}, u32[]{:S(2)}) %collective-permute-start.4) | collective-permute-done | bytes 540704 | tf_op jit(solution)/shard_map/ppermute | solution.py:365
  37.3 0.8 collective-permute-start.5
  38.0 2.1 %dynamic-slice_bitcast_fusion = (bf16[512,256]{1,0:T(8,128)(2,1)}, bf16[512,256]{1,0:T(8,128)(2,1)}, bf16[512,256]{1,0:T(8,128)(2,1)}, bf16[512,256]{1,0:T(8,128)(2,1)S(1)}) fusion(bf16[4,512,256]{2,1,0:T(8,128)(2,1)} %bitcast.44, s32[]{:T(128)S(6)} %select_n.62, s32[]{:T(128)S(6)} %select_n.61, s32[]{:T(128)S(6)} %select_n.60, s32[]{:T(128)S(6)} %select_n.59), kind=kLoop, calls=%fused_computation | loop fusion | bytes 2097168 | tf_op jit(solution)/shard_map/jit(dynamic_index_in_dim)/squeeze | solution.py:412
  40.2 3.3 %collective-permute-start.9 = (bf16[512,256]{1,0:T(8,128)(2,1)}, bf16[512,256]{1,0:T(8,128)(2,1)}, u32[]{:S(2)}, u32[]{:S(2)}) collective-permute-start(bf16[512,256]{1,0:T(8,128)(2,1)} %get-tuple-element.58), channel_id=1, source_target_pairs={{0,6},{1,7},{2,14},{3,15},{4,22},{5,23},{6,30},{7,31},{8,4},{9,5},... | collective-permute-start | bytes 786440 | tf_op jit(solution)/shard_map/ppermute | solution.py:365
  43.4 0.6 collective-permute-start.8
  44.0 0.9 collective-permute-start.7
  45.0 0.0 collective-permute-done.3.refs_1_
  45.0 0.8 copy-done.3
  45.8 1.3 collective-permute-start.6
  47.1 5.9 %pool_weights.2 = (bf16[3,512,512]{2,1,0:T(8,128)(2,1)}, bf16[3,512,512]{2,1,0:T(8,128)(2,1)}) custom-call(bf16[2112,128]{1,0:T(8,128)(2,1)} %copy-done.1, bf16[2112,128]{1,0:T(8,128)(2,1)} %copy-done.3, bf16[2112,128]{1,0:T(8,128)(2,1)} %collective-permute-done.4.refs_2_), custom_call_target="tpu_custom_call" | custom-call | flops 150994944 | bytes 3145728 | tf_op jit(solution)/shard_map/pool_weights/pallas_call | solution.py:420
  53.0 8.3 %collective-permute-done.9.refs_12_ = bf16[512,256]{1,0:T(8,128)(2,1)} collective-permute-done((bf16[512,256]{1,0:T(8,128)(2,1)}, bf16[512,256]{1,0:T(8,128)(2,1)}, u32[]{:S(2)}, u32[]{:S(2)}) %collective-permute-start.9) | collective-permute-done | bytes 262176 | tf_op jit(solution)/shard_map/ppermute | solution.py:365
  61.3 0.5 collective-permute-start.11
  61.8 0.1 collective-permute-start.12
  61.9 0.4 collective-permute-start.13
  62.3 3.0 %pool_weights.3 = (bf16[1,512,512]{2,1,0:T(8,128)(2,1)}, bf16[1,512,512]{2,1,0:T(8,128)(2,1)}) custom-call(bf16[2112,128]{1,0:T(8,128)(2,1)} %collective-permute-done.5.refs_0_.refs_3_), custom_call_target="tpu_custom_call" | custom-call | flops 50331648 | bytes 1048576 | tf_op jit(solution)/shard_map/pool_weights/pallas_call | solution.py:420
  65.3 0.6 collective-permute-done.13.refs_7_
  65.9 0.2 copy-done.4
  66.1 19.5 %design_values.1 = (s16[528,512]{1,0:T(8,128)(2,1)}, s16[528,512]{1,0:T(8,128)(2,1)}, f32[128,512]{1,0:T(8,128)}) custom-call(s32[3]{0:T(128)} %pad_add_fusion.at_ref, bf16[2112,128]{1,0:T(8,128)(2,1)} %copy-done.1, bf16[2112,128]{1,0:T(8,128)(2,1)} %copy-done.3, bf16[2112,128]{1,0:T(8,128)(2,1)} %collective-permute-done.4.refs_2_, ...), custom_call_target="tpu_custom_call" | custom-call | flops 10737418240 | bytes 14680064 | tf_op jit(solution)/shard_map/design_values/pallas_call | solution.py:447
  85.5 3.8 %collective-permute-start.17 = (s16[528,512]{1,0:T(8,128)(2,1)}, s16[528,512]{1,0:T(8,128)(2,1)}, u32[]{:S(2)}, u32[]{:S(2)}) collective-permute-start(s16[528,512]{1,0:T(8,128)(2,1)} %get-tuple-element.52.refs_0_), channel_id=1, source_target_pairs={{0,2},{1,3},{2,6},{3,7},{4,0},{5,1},{6,4},{7,5},{8,10},{9,11},{10,... | collective-permute-start | bytes 1622024 | tf_op jit(solution)/shard_map/ppermute | solution.py:365
  89.4 5.1 %collective-permute-start.15 = (s16[528,512]{1,0:T(8,128)(2,1)}, s16[528,512]{1,0:T(8,128)(2,1)S(1)}, u32[]{:S(2)}, u32[]{:S(2)}) collective-permute-start(s16[528,512]{1,0:T(8,128)(2,1)} %get-tuple-element.50.code0), channel_id=1, source_target_pairs={{0,16},{1,17},{2,18},{3,19},{4,20},{5,21},{6,22},{7,23},{8,24},{9,... | collective-permute-start | bytes 1622024 | tf_op jit(solution)/shard_map/ppermute | solution.py:365
  94.5 9.4 %collective-permute-done.17.refs_2_ = s16[528,512]{1,0:T(8,128)(2,1)} collective-permute-done((s16[528,512]{1,0:T(8,128)(2,1)}, s16[528,512]{1,0:T(8,128)(2,1)}, u32[]{:S(2)}, u32[]{:S(2)}) %collective-permute-start.17) | collective-permute-done | bytes 540704 | tf_op jit(solution)/shard_map/ppermute | solution.py:365
  103.9 0.4 collective-permute-start.18
  104.3 3.0 %collective-permute-done.15.code2 = s16[528,512]{1,0:T(8,128)(2,1)S(1)} collective-permute-done((s16[528,512]{1,0:T(8,128)(2,1)}, s16[528,512]{1,0:T(8,128)(2,1)S(1)}, u32[]{:S(2)}, u32[]{:S(2)}) %collective-permute-start.15) | collective-permute-done | bytes 540704 | tf_op jit(solution)/shard_map/ppermute | solution.py:365
  107.3 0.8 collective-permute-start.16
  108.2 0.7 collective-permute-done.14.code1
  108.9 3.9 %near_columns.1.refs_4_.refs_2_ = bf16[3,1024,512]{2,1,0:T(8,128)(2,1)} custom-call(s16[528,512]{1,0:T(8,128)(2,1)} %get-tuple-element.50.code0, s16[528,512]{1,0:T(8,128)(2,1)} %collective-permute-done.14.code1, s16[528,512]{1,0:T(8,128)(2,1)} %copy-done), custom_call_target="tpu_custom_call" | custom-call | bytes 6291456 | tf_op jit(solution)/shard_map/near_columns/pallas_call | solution.py:485
  112.8 16.4 %gram_rows.4.refs_5_ = f32[2,2048,2048]{2,1,0:T(8,128)} custom-call(s32[3]{0:T(128)} %pad_add_fusion.at_ref, s16[528,512]{1,0:T(8,128)(2,1)} %get-tuple-element.52.refs_0_, s16[528,512]{1,0:T(8,128)(2,1)} %collective-permute-done.19.refs_1_, s16[528,512]{1,0:T(8,128)(2,1)} %collective-permute-done.17.refs_2_, ...), custom_call_target="tpu_custom_call" | custom-call | flops 12884901888 | bytes 4194304 | tf_op jit(solution)/shard_map/gram_rows/pallas_call | solution.py:536
  129.2 2.6 %collective-permute-start.21 = (s16[528,512]{1,0:T(8,128)(2,1)}, s16[528,512]{1,0:T(8,128)(2,1)}, u32[]{:S(2)}, u32[]{:S(2)}) collective-permute-start(s16[528,512]{1,0:T(8,128)(2,1)} %collective-permute-done.18.refs_0_), channel_id=1, source_target_pairs={{0,2},{1,3},{2,6},{3,7},{4,0},{5,1},{6,4},{7,5},{8,10},{9,11},{10,... | collective-permute-start | bytes 1622024 | tf_op jit(solution)/shard_map/ppermute | solution.py:365
  131.8 3.8 %far_columns.1 = (bf16[1,1024,512]{2,1,0:T(8,128)(2,1)}, f32[128,2048]{1,0:T(8,128)}) custom-call(s32[3]{0:T(128)} %pad_add_fusion.at_ref, f32[128,512]{1,0:T(8,128)} %get-tuple-element.49.rows_ref, s16[528,512]{1,0:T(8,128)(2,1)} %collective-permute-done.14.code1, s16[528,512]{1,0:T(8,128)(2,1)} %copy-done, s16[528,512]{1,0:T(8,128)(2,1)} %collective-permute-done.16.code3), custom_call_target="tpu_custom_call" | custom-call | bytes 5242880 | tf_op jit(solution)/shard_map/far_columns/pallas_call | solution.py:495
  135.6 8.7 %gram_rows.5.refs_4_ = f32[2,2048,2048]{2,1,0:T(8,128)} custom-call(s32[3]{0:T(128)} %pad_add_fusion.at_ref, s16[528,512]{1,0:T(8,128)(2,1)} %get-tuple-element.52.refs_0_, s16[528,512]{1,0:T(8,128)(2,1)} %collective-permute-done.19.refs_1_, s16[528,512]{1,0:T(8,128)(2,1)} %collective-permute-done.17.refs_2_, ...), custom_call_target="tpu_custom_call", output_to_operand_aliasing={{}: (6, {})} | custom-call | flops 4294967296 | bytes 4194304 | tf_op jit(solution)/shard_map/gram_rows/pallas_call | solution.py:536
  144.3 0.5 collective-permute-start.22
  144.8 11.9 %gram_rows.6.refs_4_ = f32[2,2048,2048]{2,1,0:T(8,128)} custom-call(s32[3]{0:T(128)} %pad_add_fusion.at_ref, s16[528,512]{1,0:T(8,128)(2,1)} %collective-permute-done.18.refs_0_, s16[528,512]{1,0:T(8,128)(2,1)} %collective-permute-done.23.refs_1_, bf16[3,1024,512]{2,1,0:T(8,128)(2,1)} %near_columns.1.refs_4_.refs_2_, ...), custom_call_target="tpu_custom_call", output_to_operand_aliasing={{}: (5, {})} | custom-call | flops 8589934592 | bytes 4194304 | tf_op jit(solution)/shard_map/gram_rows/pallas_call | solution.py:536
  156.8 0.8 copy-done.2
  157.6 11.9 %gram_rows.7 = f32[2,2048,2048]{2,1,0:T(8,128)} custom-call(s32[3]{0:T(128)} %pad_add_fusion.at_ref, s16[528,512]{1,0:T(8,128)(2,1)} %collective-permute-done.21.refs_0_, s16[528,512]{1,0:T(8,128)(2,1)} %copy-done.2, bf16[3,1024,512]{2,1,0:T(8,128)(2,1)} %near_columns.1.refs_4_.refs_2_, ...), custom_call_target="tpu_custom_call", output_to_operand_aliasing={{}: (5, {})} | custom-call | flops 8589934592 | bytes 4194304 | tf_op jit(solution)/shard_map/gram_rows/pallas_call | solution.py:536
  (36 shorter events, 0.2 us)
Async XLA Ops:
  0.6 13.9 %collective-permute-start.1 = (bf16[512,128]{1,0:T(8,128)(2,1)}, bf16[512,128]{1,0:T(8,128)(2,1)S(1)}, u32[]{:S(2)}, u32[]{:S(2)}) collective-permute-start(bf16[512,128]{1,0:T(8,128)(2,1)} %param.6), channel_id=1, source_target_pairs={{0,4},{1,5},{2,6},{3,7},{4,0},{5,1},{6,2},{7,3},{8,12},{9,13},{10,... | collective-permute-start | bytes 393224 | tf_op jit(solution)/shard_map/ppermute | solution.py:365
  4.7 9.7 %collective-permute-start = (bf16[512,128]{1,0:T(8,128)(2,1)}, bf16[512,128]{1,0:T(8,128)(2,1)S(1)}, u32[]{:S(2)}, u32[]{:S(2)}) collective-permute-start(bf16[512,128]{1,0:T(8,128)(2,1)} %param.6), channel_id=1, source_target_pairs={{0,2},{1,3},{2,0},{3,1},{4,6},{5,7},{6,4},{7,5},{8,10},{9,11},{10,... | collective-permute-start | bytes 393224 | tf_op jit(solution)/shard_map/ppermute | solution.py:365
  6.3 9.0 %collective-permute-start.2 = (bf16[512,128]{1,0:T(8,128)(2,1)}, bf16[512,128]{1,0:T(8,128)(2,1)S(1)}, u32[]{:S(2)}, u32[]{:S(2)}) collective-permute-start(bf16[512,128]{1,0:T(8,128)(2,1)} %param.6), channel_id=1, source_target_pairs={{0,6},{1,7},{2,4},{3,5},{4,2},{5,3},{6,0},{7,1},{8,14},{9,15},{10,... | collective-permute-start | bytes 393224 | tf_op jit(solution)/shard_map/ppermute | solution.py:365
  6.3 17.7 %all-to-all-start = ((bf16[4,512,256]{2,1,0:T(8,128)(2,1)}), bf16[4,512,256]{2,1,0:T(8,128)(2,1)}, u32[]{:S(2)}, u32[]{:S(2)}) async-start(bf16[4,512,256]{2,1,0:T(8,128)(2,1)} %bitcast.43), calls=%async_computation | async-start | bytes 2097152 | tf_op jit(solution)/shard_map/all_to_all | solution.py:375
  15.3 31.8 %copy-start.1 = (bf16[2112,128]{1,0:T(8,128)(2,1)}, bf16[2112,128]{1,0:T(8,128)(2,1)S(1)}, u32[]{:S(2)}) copy-start(bf16[2112,128]{1,0:T(8,128)(2,1)S(1)} %constant_dynamic-update-slice_fusion.refs_0_) | copy-start | bytes 1622020
  24.0 13.3 %collective-permute-start.4 = (bf16[2112,128]{1,0:T(8,128)(2,1)S(1)}, bf16[2112,128]{1,0:T(8,128)(2,1)}, u32[]{:S(2)}, u32[]{:S(2)}) collective-permute-start(bf16[2112,128]{1,0:T(8,128)(2,1)S(1)} %constant_dynamic-update-slice_fusion.refs_0_), channel_id=1, source_target_pairs={{0,16},{1,17},{2,18},{3,19},{4,20},{5,21},{6,22},{7,23},{8,24},{9,... | collective-permute-start | bytes 1622024 | tf_op jit(solution)/shard_map/ppermute | solution.py:365
  25.4 19.5 %collective-permute-start.3 = (bf16[2112,128]{1,0:T(8,128)(2,1)S(1)}, bf16[2112,128]{1,0:T(8,128)(2,1)S(1)}, u32[]{:S(2)}, u32[]{:S(2)}) collective-permute-start(bf16[2112,128]{1,0:T(8,128)(2,1)S(1)} %constant_dynamic-update-slice_fusion.refs_0_), channel_id=1, source_target_pairs={{0,8},{1,9},{2,10},{3,11},{4,12},{5,13},{6,14},{7,15},{8,0},{9,1},... | collective-permute-start | bytes 1622024 | tf_op jit(solution)/shard_map/ppermute | solution.py:365
  37.3 24.6 %collective-permute-start.5 = (bf16[2112,128]{1,0:T(8,128)(2,1)}, bf16[2112,128]{1,0:T(8,128)(2,1)}, u32[]{:S(2)}, u32[]{:S(2)}) collective-permute-start(bf16[2112,128]{1,0:T(8,128)(2,1)} %collective-permute-done.4.refs_2_), channel_id=1, source_target_pairs={{0,8},{1,9},{2,10},{3,11},{4,12},{5,13},{6,14},{7,15},{8,0},{9,1},... | collective-permute-start | bytes 1622024 | tf_op jit(solution)/shard_map/ppermute | solution.py:365
  40.2 21.1 %collective-permute-start.9 = (bf16[512,256]{1,0:T(8,128)(2,1)}, bf16[512,256]{1,0:T(8,128)(2,1)}, u32[]{:S(2)}, u32[]{:S(2)}) collective-permute-start(bf16[512,256]{1,0:T(8,128)(2,1)} %get-tuple-element.58), channel_id=1, source_target_pairs={{0,6},{1,7},{2,14},{3,15},{4,22},{5,23},{6,30},{7,31},{8,4},{9,5},... | collective-permute-start | bytes 786440 | tf_op jit(solution)/shard_map/ppermute | solution.py:365
  43.4 17.9 %collective-permute-start.8 = (bf16[512,256]{1,0:T(8,128)(2,1)}, bf16[512,256]{1,0:T(8,128)(2,1)}, u32[]{:S(2)}, u32[]{:S(2)}) collective-permute-start(bf16[512,256]{1,0:T(8,128)(2,1)} %get-tuple-element.59), channel_id=1, source_target_pairs={{0,4},{1,5},{2,12},{3,13},{4,20},{5,21},{6,28},{7,29},{8,6},{9,7},... | collective-permute-start | bytes 786440 | tf_op jit(solution)/shard_map/ppermute | solution.py:365
  44.0 17.7 %collective-permute-start.7 = (bf16[512,256]{1,0:T(8,128)(2,1)}, bf16[512,256]{1,0:T(8,128)(2,1)}, u32[]{:S(2)}, u32[]{:S(2)}) collective-permute-start(bf16[512,256]{1,0:T(8,128)(2,1)} %get-tuple-element.60), channel_id=1, source_target_pairs={{0,2},{1,3},{2,10},{3,11},{4,18},{5,19},{6,26},{7,27},{8,0},{9,1},... | collective-permute-start | bytes 786440 | tf_op jit(solution)/shard_map/ppermute | solution.py:365
  45.0 0.8 copy-start.3
  45.8 16.1 %collective-permute-start.6 = (bf16[512,256]{1,0:T(8,128)(2,1)S(1)}, bf16[512,256]{1,0:T(8,128)(2,1)}, u32[]{:S(2)}, u32[]{:S(2)}) collective-permute-start(bf16[512,256]{1,0:T(8,128)(2,1)S(1)} %get-tuple-element.61), channel_id=1, source_target_pairs={{0,0},{1,1},{2,8},{3,9},{4,16},{5,17},{6,24},{7,25},{8,2},{9,3},{1... | collective-permute-start | bytes 786440 | tf_op jit(solution)/shard_map/ppermute | solution.py:365
  61.3 4.0 %collective-permute-start.10 = (bf16[2112,128]{1,0:T(8,128)(2,1)}, bf16[2112,128]{1,0:T(8,128)(2,1)S(1)}, u32[]{:S(2)}, u32[]{:S(2)}) collective-permute-start(bf16[2112,128]{1,0:T(8,128)(2,1)} %copy-done.1), channel_id=1, source_target_pairs={{0,1},{1,0},{2,3},{3,2},{4,5},{5,4},{6,7},{7,6},{8,9},{9,8},{10,11... | collective-permute-start | bytes 1622024 | tf_op jit(solution)/shard_map/ppermute | solution.py:365
  61.3 4.0 %collective-permute-start.11 = (bf16[2112,128]{1,0:T(8,128)(2,1)}, bf16[2112,128]{1,0:T(8,128)(2,1)}, u32[]{:S(2)}, u32[]{:S(2)}) collective-permute-start(bf16[2112,128]{1,0:T(8,128)(2,1)} %copy-done.3), channel_id=1, source_target_pairs={{0,1},{1,0},{2,3},{3,2},{4,5},{5,4},{6,7},{7,6},{8,9},{9,8},{10,11... | collective-permute-start | bytes 1622024 | tf_op jit(solution)/shard_map/ppermute | solution.py:365
  61.8 3.5 %collective-permute-start.12 = (bf16[2112,128]{1,0:T(8,128)(2,1)}, bf16[2112,128]{1,0:T(8,128)(2,1)}, u32[]{:S(2)}, u32[]{:S(2)}) collective-permute-start(bf16[2112,128]{1,0:T(8,128)(2,1)} %collective-permute-done.4.refs_2_), channel_id=1, source_target_pairs={{0,1},{1,0},{2,3},{3,2},{4,5},{5,4},{6,7},{7,6},{8,9},{9,8},{10,11... | collective-permute-start | bytes 1622024 | tf_op jit(solution)/shard_map/ppermute | solution.py:365
  61.9 4.0 %collective-permute-start.13 = (bf16[2112,128]{1,0:T(8,128)(2,1)}, bf16[2112,128]{1,0:T(8,128)(2,1)}, u32[]{:S(2)}, u32[]{:S(2)}) collective-permute-start(bf16[2112,128]{1,0:T(8,128)(2,1)} %collective-permute-done.5.refs_0_.refs_3_), channel_id=1, source_target_pairs={{0,1},{1,0},{2,3},{3,2},{4,5},{5,4},{6,7},{7,6},{8,9},{9,8},{10,11... | collective-permute-start | bytes 1622024 | tf_op jit(solution)/shard_map/ppermute | solution.py:365
  65.3 0.8 copy-start.4
  85.5 18.4 %collective-permute-start.17 = (s16[528,512]{1,0:T(8,128)(2,1)}, s16[528,512]{1,0:T(8,128)(2,1)}, u32[]{:S(2)}, u32[]{:S(2)}) collective-permute-start(s16[528,512]{1,0:T(8,128)(2,1)} %get-tuple-element.52.refs_0_), channel_id=1, source_target_pairs={{0,2},{1,3},{2,6},{3,7},{4,0},{5,1},{6,4},{7,5},{8,10},{9,11},{10,... | collective-permute-start | bytes 1622024 | tf_op jit(solution)/shard_map/ppermute | solution.py:365
  89.4 18.0 %collective-permute-start.15 = (s16[528,512]{1,0:T(8,128)(2,1)}, s16[528,512]{1,0:T(8,128)(2,1)S(1)}, u32[]{:S(2)}, u32[]{:S(2)}) collective-permute-start(s16[528,512]{1,0:T(8,128)(2,1)} %get-tuple-element.50.code0), channel_id=1, source_target_pairs={{0,16},{1,17},{2,18},{3,19},{4,20},{5,21},{6,22},{7,23},{8,24},{9,... | collective-permute-start | bytes 1622024 | tf_op jit(solution)/shard_map/ppermute | solution.py:365
  94.5 14.4 %collective-permute-start.14 = (s16[528,512]{1,0:T(8,128)(2,1)}, s16[528,512]{1,0:T(8,128)(2,1)}, u32[]{:S(2)}, u32[]{:S(2)}) collective-permute-start(s16[528,512]{1,0:T(8,128)(2,1)} %get-tuple-element.50.code0), channel_id=1, source_target_pairs={{0,8},{1,9},{2,10},{3,11},{4,12},{5,13},{6,14},{7,15},{8,0},{9,1},... | collective-permute-start | bytes 1622024 | tf_op jit(solution)/shard_map/ppermute | solution.py:365
  94.5 18.4 %collective-permute-start.19 = (s16[528,512]{1,0:T(8,128)(2,1)}, s16[528,512]{1,0:T(8,128)(2,1)}, u32[]{:S(2)}, u32[]{:S(2)}) collective-permute-start(s16[528,512]{1,0:T(8,128)(2,1)} %get-tuple-element.52.refs_0_), channel_id=1, source_target_pairs={{0,1},{1,0},{2,3},{3,2},{4,5},{5,4},{6,7},{7,6},{8,9},{9,8},{10,11... | collective-permute-start | bytes 1622024 | tf_op jit(solution)/shard_map/ppermute | solution.py:365
  103.9 8.9 %collective-permute-start.20 = (s16[528,512]{1,0:T(8,128)(2,1)}, s16[528,512]{1,0:T(8,128)(2,1)}, u32[]{:S(2)}, u32[]{:S(2)}) collective-permute-start(s16[528,512]{1,0:T(8,128)(2,1)} %collective-permute-done.17.refs_2_), channel_id=1, source_target_pairs={{0,1},{1,0},{2,3},{3,2},{4,5},{5,4},{6,7},{7,6},{8,9},{9,8},{10,11... | collective-permute-start | bytes 1622024 | tf_op jit(solution)/shard_map/ppermute | solution.py:365
  103.9 25.3 %collective-permute-start.18 = (s16[528,512]{1,0:T(8,128)(2,1)}, s16[528,512]{1,0:T(8,128)(2,1)}, u32[]{:S(2)}, u32[]{:S(2)}) collective-permute-start(s16[528,512]{1,0:T(8,128)(2,1)} %collective-permute-done.17.refs_2_), channel_id=1, source_target_pairs={{0,2},{1,3},{2,6},{3,7},{4,0},{5,1},{6,4},{7,5},{8,10},{9,11},{10,... | collective-permute-start | bytes 1622024 | tf_op jit(solution)/shard_map/ppermute | solution.py:365
  107.3 1.6 copy-start
  107.3 24.5 %collective-permute-start.16 = (s16[528,512]{1,0:T(8,128)(2,1)S(1)}, s16[528,512]{1,0:T(8,128)(2,1)}, u32[]{:S(2)}, u32[]{:S(2)}) collective-permute-start(s16[528,512]{1,0:T(8,128)(2,1)S(1)} %collective-permute-done.15.code2), channel_id=1, source_target_pairs={{0,8},{1,9},{2,10},{3,11},{4,12},{5,13},{6,14},{7,15},{8,0},{9,1},... | collective-permute-start | bytes 1622024 | tf_op jit(solution)/shard_map/ppermute | solution.py:365
  129.2 15.1 %collective-permute-start.21 = (s16[528,512]{1,0:T(8,128)(2,1)}, s16[528,512]{1,0:T(8,128)(2,1)}, u32[]{:S(2)}, u32[]{:S(2)}) collective-permute-start(s16[528,512]{1,0:T(8,128)(2,1)} %collective-permute-done.18.refs_0_), channel_id=1, source_target_pairs={{0,2},{1,3},{2,6},{3,7},{4,0},{5,1},{6,4},{7,5},{8,10},{9,11},{10,... | collective-permute-start | bytes 1622024 | tf_op jit(solution)/shard_map/ppermute | solution.py:365
  131.8 13.0 %collective-permute-start.23 = (s16[528,512]{1,0:T(8,128)(2,1)}, s16[528,512]{1,0:T(8,128)(2,1)}, u32[]{:S(2)}, u32[]{:S(2)}) collective-permute-start(s16[528,512]{1,0:T(8,128)(2,1)} %collective-permute-done.18.refs_0_), channel_id=1, source_target_pairs={{0,1},{1,0},{2,3},{3,2},{4,5},{5,4},{6,7},{7,6},{8,9},{9,8},{10,11... | collective-permute-start | bytes 1622024 | tf_op jit(solution)/shard_map/ppermute | solution.py:365
  144.3 12.5 %collective-permute-start.22 = (s16[528,512]{1,0:T(8,128)(2,1)}, s16[528,512]{1,0:T(8,128)(2,1)S(1)}, u32[]{:S(2)}, u32[]{:S(2)}) collective-permute-start(s16[528,512]{1,0:T(8,128)(2,1)} %collective-permute-done.21.refs_0_), channel_id=1, source_target_pairs={{0,1},{1,0},{2,3},{3,2},{4,5},{5,4},{6,7},{7,6},{8,9},{9,8},{10,11... | collective-permute-start | bytes 1622024 | tf_op jit(solution)/shard_map/ppermute | solution.py:365
  156.8 0.8 copy-start.2

commit v5 on v4

--- a/solution.py
+++ b/solution.py
@@ -561,8 +561,7 @@
     gram = gram_rows(gram, (0, 1), 3, 1)
     held[3], gram = lax.optimization_barrier((held[3], gram))
     swapped.append(moved(held[3], to_core))
-    gram = gram_rows(gram, (2,), 0, 4)
-    gram = gram_rows(gram, (3,), 0, 4)
+    gram = gram_rows(gram, (2, 3), 0, 4)
     return design, gram.reshape(2 * planes * n_pts, width)
 
 

time: 170 us -> 169 us (level)
  Pallas kernels: 84.9 us -> 81.5 us
  waiting for transfers between devices: 42.8 us -> 44.8 us
    pallas_call x4 -> x3, Pallas kernels: 48.9 us -> 45.5 us  [gram_rows(): pl.pallas_call(functools.partial(gram_kernel, steps, first, n_near), grid...]
    ppermute x24, waiting for transfers between devices: 34.1 us -> 36.1 us  [moved(): return lax.ppermute(value, BOTH, permutation(to))]
  transfers between devices with their start and end apart: 25 -> 25, of which waited for: 8 -> 9; matrix products, arithmetic and copies ran while one was open for 4% -> 4% of each run, Pallas kernels for 32% -> 25%
where the time goes in v5:
time: 169 us; the launch traced here: 168 us
  Pallas kernels  81.5 us (48%)
  waiting for transfers between devices  44.8 us (27%)
  starting transfers between devices  33.1 us (20%)
  local copies, waits for them, and re-layouts  5.06 us (3%)
  other arithmetic  2.68 us (2%)
    pallas_call x3, Pallas kernels, gram_rows(): pl.pallas_call(functools.partial(gram_kernel, steps, first, n_near), grid...  45.5 us
    ppermute x24, waiting for transfers between devices, moved(): return lax.ppermute(value, BOTH, permutation(to))  36.1 us
    ppermute x24, starting transfers between devices, moved(): return lax.ppermute(value, BOTH, permutation(to))  28.8 us
    pallas_call x1, Pallas kernels, on_device(): pl.pallas_call(design_kernel, grid_spec=pltpu.PrefetchScalarGridSpec(num_...  19.5 us
    pallas_call x2, Pallas kernels, pool_weights(): pl.pallas_call(weights_kernel, grid=(1,), in_specs=[pl.BlockSpec((64, par...  8.72 us
    all_to_all x1, waiting for transfers between devices, on_device(): cols_pts = lax.all_to_all(quarters, 'rows', 0, 0, tiled=True)  8.65 us
    all_to_all x1, starting transfers between devices, on_device(): cols_pts = lax.all_to_all(quarters, 'rows', 0, 0, tiled=True)  4.25 us
    pallas_call x1, Pallas kernels, on_device(): pl.pallas_call(near_columns_kernel, grid=(3,), in_specs=[code_spec] * 3,...  3.9 us
  transfers between devices with their start and end apart: 25, of which 9 were waited for; matrix products, arithmetic and copies ran while one was open for 4% of the time, Pallas kernels for 25%

profile of v5, /device:TPU:0, one launch (start us, length us, event | category | flops | bytes accessed | tf_op | source)
XLA Modules:
  0.0 167.8 jit_solution(8463658489354878733)
XLA Ops:
  0.6 4.1 %collective-permute-start.1 = (bf16[512,128]{1,0:T(8,128)(2,1)}, bf16[512,128]{1,0:T(8,128)(2,1)S(1)}, u32[]{:S(2)}, u32[]{:S(2)}) collective-permute-start(bf16[512,128]{1,0:T(8,128)(2,1)} %param.6), channel_id=1, source_target_pairs={{0,4},{1,5},{2,6},{3,7},{4,0},{5,1},{6,2},{7,3},{8,12},{9,13},{10,... | collective-permute-start | bytes 393224 | tf_op jit(solution)/shard_map/ppermute | solution.py:365
  4.7 1.6 collective-permute-start
  6.3 0.0 collective-permute-start.2
  6.3 4.2 %all-to-all-start = ((bf16[4,512,256]{2,1,0:T(8,128)(2,1)}), bf16[4,512,256]{2,1,0:T(8,128)(2,1)}, u32[]{:S(2)}, u32[]{:S(2)}) async-start(bf16[4,512,256]{2,1,0:T(8,128)(2,1)} %bitcast.43), calls=%async_computation | async-start | bytes 2097152 | tf_op jit(solution)/shard_map/all_to_all | solution.py:375
  10.6 0.7 fusion.6
  11.3 0.7 fusion.2
  12.0 0.7 fusion
  12.7 0.9 constant_dynamic-update-slice_fusion.5
  13.6 0.6 pad_add_fusion.at_ref
  14.2 0.2 concatenate.6
  14.5 0.8 collective-permute-done.2
  15.3 0.0 copy-start.1
  15.3 8.7 %all-to-all-done.refs_8_ = bf16[4,512,256]{2,1,0:T(8,128)(2,1)} async-done(((bf16[4,512,256]{2,1,0:T(8,128)(2,1)}), bf16[4,512,256]{2,1,0:T(8,128)(2,1)}, u32[]{:S(2)}, u32[]{:S(2)}) %all-to-all-start) | async-done | bytes 1048608 | tf_op jit(solution)/shard_map/all_to_all | solution.py:375
  24.0 1.5 collective-permute-start.4
  25.4 0.5 collective-permute-start.3
  26.0 11.3 %collective-permute-done.4.refs_2_ = bf16[2112,128]{1,0:T(8,128)(2,1)} collective-permute-done((bf16[2112,128]{1,0:T(8,128)(2,1)S(1)}, bf16[2112,128]{1,0:T(8,128)(2,1)}, u32[]{:S(2)}, u32[]{:S(2)}) %collective-permute-start.4) | collective-permute-done | bytes 540704 | tf_op jit(solution)/shard_map/ppermute | solution.py:365
  37.3 0.8 collective-permute-start.5
  38.0 2.1 %dynamic-slice_bitcast_fusion = (bf16[512,256]{1,0:T(8,128)(2,1)}, bf16[512,256]{1,0:T(8,128)(2,1)}, bf16[512,256]{1,0:T(8,128)(2,1)}, bf16[512,256]{1,0:T(8,128)(2,1)S(1)}) fusion(bf16[4,512,256]{2,1,0:T(8,128)(2,1)} %bitcast.44, s32[]{:T(128)S(6)} %select_n.62, s32[]{:T(128)S(6)} %select_n.61, s32[]{:T(128)S(6)} %select_n.60, s32[]{:T(128)S(6)} %select_n.59), kind=kLoop, calls=%fused_computation | loop fusion | bytes 2097168 | tf_op jit(solution)/shard_map/jit(dynamic_index_in_dim)/squeeze | solution.py:412
  40.1 3.3 %collective-permute-start.9 = (bf16[512,256]{1,0:T(8,128)(2,1)}, bf16[512,256]{1,0:T(8,128)(2,1)}, u32[]{:S(2)}, u32[]{:S(2)}) collective-permute-start(bf16[512,256]{1,0:T(8,128)(2,1)} %get-tuple-element.58), channel_id=1, source_target_pairs={{0,6},{1,7},{2,14},{3,15},{4,22},{5,23},{6,30},{7,31},{8,4},{9,5},... | collective-permute-start | bytes 786440 | tf_op jit(solution)/shard_map/ppermute | solution.py:365
  43.4 0.6 collective-permute-start.8
  44.0 0.9 collective-permute-start.7
  44.9 0.8 copy-done.3
  45.7 1.3 collective-permute-start.6
  47.1 5.8 %pool_weights.2 = (bf16[3,512,512]{2,1,0:T(8,128)(2,1)}, bf16[3,512,512]{2,1,0:T(8,128)(2,1)}) custom-call(bf16[2112,128]{1,0:T(8,128)(2,1)} %copy-done.1, bf16[2112,128]{1,0:T(8,128)(2,1)} %copy-done.3, bf16[2112,128]{1,0:T(8,128)(2,1)} %collective-permute-done.4.refs_2_), custom_call_target="tpu_custom_call" | custom-call | flops 150994944 | bytes 3145728 | tf_op jit(solution)/shard_map/pool_weights/pallas_call | solution.py:420
  52.9 8.4 %collective-permute-done.9.refs_12_ = bf16[512,256]{1,0:T(8,128)(2,1)} collective-permute-done((bf16[512,256]{1,0:T(8,128)(2,1)}, bf16[512,256]{1,0:T(8,128)(2,1)}, u32[]{:S(2)}, u32[]{:S(2)}) %collective-permute-start.9) | collective-permute-done | bytes 262176 | tf_op jit(solution)/shard_map/ppermute | solution.py:365
  61.3 0.5 collective-permute-start.11
  61.8 0.1 collective-permute-start.12
  61.9 0.4 collective-permute-start.13
  62.3 2.9 %pool_weights.3 = (bf16[1,512,512]{2,1,0:T(8,128)(2,1)}, bf16[1,512,512]{2,1,0:T(8,128)(2,1)}) custom-call(bf16[2112,128]{1,0:T(8,128)(2,1)} %collective-permute-done.5.refs_0_.refs_3_), custom_call_target="tpu_custom_call" | custom-call | flops 50331648 | bytes 1048576 | tf_op jit(solution)/shard_map/pool_weights/pallas_call | solution.py:420
  65.2 0.6 collective-permute-done.13.refs_7_
  65.9 0.2 copy-done.4
  66.0 19.5 %design_values.1 = (s16[528,512]{1,0:T(8,128)(2,1)}, s16[528,512]{1,0:T(8,128)(2,1)}, f32[128,512]{1,0:T(8,128)}) custom-call(s32[3]{0:T(128)} %pad_add_fusion.at_ref, bf16[2112,128]{1,0:T(8,128)(2,1)} %copy-done.1, bf16[2112,128]{1,0:T(8,128)(2,1)} %copy-done.3, bf16[2112,128]{1,0:T(8,128)(2,1)} %collective-permute-done.4.refs_2_, ...), custom_call_target="tpu_custom_call" | custom-call | flops 10737418240 | bytes 14680064 | tf_op jit(solution)/shard_map/design_values/pallas_call | solution.py:447
  85.5 3.8 %collective-permute-start.17 = (s16[528,512]{1,0:T(8,128)(2,1)}, s16[528,512]{1,0:T(8,128)(2,1)}, u32[]{:S(2)}, u32[]{:S(2)}) collective-permute-start(s16[528,512]{1,0:T(8,128)(2,1)} %get-tuple-element.52.refs_0_), channel_id=1, source_target_pairs={{0,2},{1,3},{2,6},{3,7},{4,0},{5,1},{6,4},{7,5},{8,10},{9,11},{10,... | collective-permute-start | bytes 1622024 | tf_op jit(solution)/shard_map/ppermute | solution.py:365
  89.3 5.1 %collective-permute-start.15 = (s16[528,512]{1,0:T(8,128)(2,1)}, s16[528,512]{1,0:T(8,128)(2,1)S(1)}, u32[]{:S(2)}, u32[]{:S(2)}) collective-permute-start(s16[528,512]{1,0:T(8,128)(2,1)} %get-tuple-element.50.code0), channel_id=1, source_target_pairs={{0,16},{1,17},{2,18},{3,19},{4,20},{5,21},{6,22},{7,23},{8,24},{9,... | collective-permute-start | bytes 1622024 | tf_op jit(solution)/shard_map/ppermute | solution.py:365
  94.4 9.5 %collective-permute-done.17.refs_2_ = s16[528,512]{1,0:T(8,128)(2,1)} collective-permute-done((s16[528,512]{1,0:T(8,128)(2,1)}, s16[528,512]{1,0:T(8,128)(2,1)}, u32[]{:S(2)}, u32[]{:S(2)}) %collective-permute-start.17) | collective-permute-done | bytes 540704 | tf_op jit(solution)/shard_map/ppermute | solution.py:365
  103.9 0.4 collective-permute-start.18
  104.2 3.0 %collective-permute-done.15.code2 = s16[528,512]{1,0:T(8,128)(2,1)S(1)} collective-permute-done((s16[528,512]{1,0:T(8,128)(2,1)}, s16[528,512]{1,0:T(8,128)(2,1)S(1)}, u32[]{:S(2)}, u32[]{:S(2)}) %collective-permute-start.15) | collective-permute-done | bytes 540704 | tf_op jit(solution)/shard_map/ppermute | solution.py:365
  107.3 0.9 collective-permute-start.16
  108.1 0.7 collective-permute-done.14.code1
  108.8 3.9 %near_columns.1.refs_4_ = bf16[3,1024,512]{2,1,0:T(8,128)(2,1)} custom-call(s16[528,512]{1,0:T(8,128)(2,1)} %get-tuple-element.50.code0, s16[528,512]{1,0:T(8,128)(2,1)} %collective-permute-done.14.code1, s16[528,512]{1,0:T(8,128)(2,1)} %copy-done), custom_call_target="tpu_custom_call" | custom-call | bytes 6291456 | tf_op jit(solution)/shard_map/near_columns/pallas_call | solution.py:485
  112.8 16.4 %gram_rows.3.refs_5_ = f32[2,2048,2048]{2,1,0:T(8,128)} custom-call(s32[3]{0:T(128)} %pad_add_fusion.at_ref, s16[528,512]{1,0:T(8,128)(2,1)} %get-tuple-element.52.refs_0_, s16[528,512]{1,0:T(8,128)(2,1)} %collective-permute-done.19.refs_1_, s16[528,512]{1,0:T(8,128)(2,1)} %collective-permute-done.17.refs_2_, ...), custom_call_target="tpu_custom_call" | custom-call | flops 12884901888 | bytes 4194304 | tf_op jit(solution)/shard_map/gram_rows/pallas_call | solution.py:536
  129.1 2.6 %collective-permute-start.22 = (s16[528,512]{1,0:T(8,128)(2,1)}, s16[528,512]{1,0:T(8,128)(2,1)}, u32[]{:S(2)}, u32[]{:S(2)}) collective-permute-start(s16[528,512]{1,0:T(8,128)(2,1)} %collective-permute-done.18.refs_0_), channel_id=1, source_target_pairs={{0,2},{1,3},{2,6},{3,7},{4,0},{5,1},{6,4},{7,5},{8,10},{9,11},{10,... | collective-permute-start | bytes 1622024 | tf_op jit(solution)/shard_map/ppermute | solution.py:365
  131.7 3.8 %far_columns.1 = (bf16[1,1024,512]{2,1,0:T(8,128)(2,1)}, f32[128,2048]{1,0:T(8,128)}) custom-call(s32[3]{0:T(128)} %pad_add_fusion.at_ref, f32[128,512]{1,0:T(8,128)} %get-tuple-element.49.rows_ref, s16[528,512]{1,0:T(8,128)(2,1)} %collective-permute-done.14.code1, s16[528,512]{1,0:T(8,128)(2,1)} %copy-done, s16[528,512]{1,0:T(8,128)(2,1)} %collective-permute-done.16.code3), custom_call_target="tpu_custom_call" | custom-call | bytes 5242880 | tf_op jit(solution)/shard_map/far_columns/pallas_call | solution.py:495
  135.6 8.7 %gram_rows.4.refs_6_ = f32[2,2048,2048]{2,1,0:T(8,128)} custom-call(s32[3]{0:T(128)} %pad_add_fusion.at_ref, s16[528,512]{1,0:T(8,128)(2,1)} %get-tuple-element.52.refs_0_, s16[528,512]{1,0:T(8,128)(2,1)} %collective-permute-done.19.refs_1_, s16[528,512]{1,0:T(8,128)(2,1)} %collective-permute-done.17.refs_2_, ...), custom_call_target="tpu_custom_call", output_to_operand_aliasing={{}: (6, {})} | custom-call | flops 4294967296 | bytes 4194304 | tf_op jit(solution)/shard_map/gram_rows/pallas_call | solution.py:536
  144.3 0.5 collective-permute-start.23
  144.8 1.8 %collective-permute-done.23.refs_3_ = s16[528,512]{1,0:T(8,128)(2,1)S(1)} collective-permute-done((s16[528,512]{1,0:T(8,128)(2,1)}, s16[528,512]{1,0:T(8,128)(2,1)S(1)}, u32[]{:S(2)}, u32[]{:S(2)}) %collective-permute-start.23) | collective-permute-done | bytes 540704 | tf_op jit(solution)/shard_map/ppermute | solution.py:365
  146.5 0.8 copy-done.2
  147.3 20.5 %gram_rows.5 = f32[2,2048,2048]{2,1,0:T(8,128)} custom-call(s32[3]{0:T(128)} %pad_add_fusion.at_ref, s16[528,512]{1,0:T(8,128)(2,1)} %collective-permute-done.18.refs_0_, s16[528,512]{1,0:T(8,128)(2,1)} %collective-permute-done.21.refs_1_, s16[528,512]{1,0:T(8,128)(2,1)} %collective-permute-done.22.refs_2_, ...), custom_call_target="tpu_custom_call", output_to_operand_aliasing={{}: (7, {})} | custom-call | flops 17179869184 | bytes 4194304 | tf_op jit(solution)/shard_map/gram_rows/pallas_call | solution.py:536
  (35 shorter events, 0.2 us)
Async XLA Ops:
  0.6 13.8 %collective-permute-start.1 = (bf16[512,128]{1,0:T(8,128)(2,1)}, bf16[512,128]{1,0:T(8,128)(2,1)S(1)}, u32[]{:S(2)}, u32[]{:S(2)}) collective-permute-start(bf16[512,128]{1,0:T(8,128)(2,1)} %param.6), channel_id=1, source_target_pairs={{0,4},{1,5},{2,6},{3,7},{4,0},{5,1},{6,2},{7,3},{8,12},{9,13},{10,... | collective-permute-start | bytes 393224 | tf_op jit(solution)/shard_map/ppermute | solution.py:365
  4.7 9.7 %collective-permute-start = (bf16[512,128]{1,0:T(8,128)(2,1)}, bf16[512,128]{1,0:T(8,128)(2,1)S(1)}, u32[]{:S(2)}, u32[]{:S(2)}) collective-permute-start(bf16[512,128]{1,0:T(8,128)(2,1)} %param.6), channel_id=1, source_target_pairs={{0,2},{1,3},{2,0},{3,1},{4,6},{5,7},{6,4},{7,5},{8,10},{9,11},{10,... | collective-permute-start | bytes 393224 | tf_op jit(solution)/shard_map/ppermute | solution.py:365
  6.3 9.0 %collective-permute-start.2 = (bf16[512,128]{1,0:T(8,128)(2,1)}, bf16[512,128]{1,0:T(8,128)(2,1)S(1)}, u32[]{:S(2)}, u32[]{:S(2)}) collective-permute-start(bf16[512,128]{1,0:T(8,128)(2,1)} %param.6), channel_id=1, source_target_pairs={{0,6},{1,7},{2,4},{3,5},{4,2},{5,3},{6,0},{7,1},{8,14},{9,15},{10,... | collective-permute-start | bytes 393224 | tf_op jit(solution)/shard_map/ppermute | solution.py:365
  6.3 17.7 %all-to-all-start = ((bf16[4,512,256]{2,1,0:T(8,128)(2,1)}), bf16[4,512,256]{2,1,0:T(8,128)(2,1)}, u32[]{:S(2)}, u32[]{:S(2)}) async-start(bf16[4,512,256]{2,1,0:T(8,128)(2,1)} %bitcast.43), calls=%async_computation | async-start | bytes 2097152 | tf_op jit(solution)/shard_map/all_to_all | solution.py:375
  15.3 31.8 %copy-start.1 = (bf16[2112,128]{1,0:T(8,128)(2,1)}, bf16[2112,128]{1,0:T(8,128)(2,1)S(1)}, u32[]{:S(2)}) copy-start(bf16[2112,128]{1,0:T(8,128)(2,1)S(1)} %constant_dynamic-update-slice_fusion.refs_0_) | copy-start | bytes 1622020
  24.0 13.3 %collective-permute-start.4 = (bf16[2112,128]{1,0:T(8,128)(2,1)S(1)}, bf16[2112,128]{1,0:T(8,128)(2,1)}, u32[]{:S(2)}, u32[]{:S(2)}) collective-permute-start(bf16[2112,128]{1,0:T(8,128)(2,1)S(1)} %constant_dynamic-update-slice_fusion.refs_0_), channel_id=1, source_target_pairs={{0,16},{1,17},{2,18},{3,19},{4,20},{5,21},{6,22},{7,23},{8,24},{9,... | collective-permute-start | bytes 1622024 | tf_op jit(solution)/shard_map/ppermute | solution.py:365
  25.4 19.5 %collective-permute-start.3 = (bf16[2112,128]{1,0:T(8,128)(2,1)S(1)}, bf16[2112,128]{1,0:T(8,128)(2,1)S(1)}, u32[]{:S(2)}, u32[]{:S(2)}) collective-permute-start(bf16[2112,128]{1,0:T(8,128)(2,1)S(1)} %constant_dynamic-update-slice_fusion.refs_0_), channel_id=1, source_target_pairs={{0,8},{1,9},{2,10},{3,11},{4,12},{5,13},{6,14},{7,15},{8,0},{9,1},... | collective-permute-start | bytes 1622024 | tf_op jit(solution)/shard_map/ppermute | solution.py:365
  37.3 24.6 %collective-permute-start.5 = (bf16[2112,128]{1,0:T(8,128)(2,1)}, bf16[2112,128]{1,0:T(8,128)(2,1)}, u32[]{:S(2)}, u32[]{:S(2)}) collective-permute-start(bf16[2112,128]{1,0:T(8,128)(2,1)} %collective-permute-done.4.refs_2_), channel_id=1, source_target_pairs={{0,8},{1,9},{2,10},{3,11},{4,12},{5,13},{6,14},{7,15},{8,0},{9,1},... | collective-permute-start | bytes 1622024 | tf_op jit(solution)/shard_map/ppermute | solution.py:365
  40.1 21.2 %collective-permute-start.9 = (bf16[512,256]{1,0:T(8,128)(2,1)}, bf16[512,256]{1,0:T(8,128)(2,1)}, u32[]{:S(2)}, u32[]{:S(2)}) collective-permute-start(bf16[512,256]{1,0:T(8,128)(2,1)} %get-tuple-element.58), channel_id=1, source_target_pairs={{0,6},{1,7},{2,14},{3,15},{4,22},{5,23},{6,30},{7,31},{8,4},{9,5},... | collective-permute-start | bytes 786440 | tf_op jit(solution)/shard_map/ppermute | solution.py:365
  43.4 17.9 %collective-permute-start.8 = (bf16[512,256]{1,0:T(8,128)(2,1)}, bf16[512,256]{1,0:T(8,128)(2,1)}, u32[]{:S(2)}, u32[]{:S(2)}) collective-permute-start(bf16[512,256]{1,0:T(8,128)(2,1)} %get-tuple-element.59), channel_id=1, source_target_pairs={{0,4},{1,5},{2,12},{3,13},{4,20},{5,21},{6,28},{7,29},{8,6},{9,7},... | collective-permute-start | bytes 786440 | tf_op jit(solution)/shard_map/ppermute | solution.py:365
  44.0 17.8 %collective-permute-start.7 = (bf16[512,256]{1,0:T(8,128)(2,1)}, bf16[512,256]{1,0:T(8,128)(2,1)}, u32[]{:S(2)}, u32[]{:S(2)}) collective-permute-start(bf16[512,256]{1,0:T(8,128)(2,1)} %get-tuple-element.60), channel_id=1, source_target_pairs={{0,2},{1,3},{2,10},{3,11},{4,18},{5,19},{6,26},{7,27},{8,0},{9,1},... | collective-permute-start | bytes 786440 | tf_op jit(solution)/shard_map/ppermute | solution.py:365
  44.9 0.8 copy-start.3
  45.7 16.1 %collective-permute-start.6 = (bf16[512,256]{1,0:T(8,128)(2,1)S(1)}, bf16[512,256]{1,0:T(8,128)(2,1)}, u32[]{:S(2)}, u32[]{:S(2)}) collective-permute-start(bf16[512,256]{1,0:T(8,128)(2,1)S(1)} %get-tuple-element.61), channel_id=1, source_target_pairs={{0,0},{1,1},{2,8},{3,9},{4,16},{5,17},{6,24},{7,25},{8,2},{9,3},{1... | collective-permute-start | bytes 786440 | tf_op jit(solution)/shard_map/ppermute | solution.py:365
  61.3 3.9 %collective-permute-start.10 = (bf16[2112,128]{1,0:T(8,128)(2,1)}, bf16[2112,128]{1,0:T(8,128)(2,1)S(1)}, u32[]{:S(2)}, u32[]{:S(2)}) collective-permute-start(bf16[2112,128]{1,0:T(8,128)(2,1)} %copy-done.1), channel_id=1, source_target_pairs={{0,1},{1,0},{2,3},{3,2},{4,5},{5,4},{6,7},{7,6},{8,9},{9,8},{10,11... | collective-permute-start | bytes 1622024 | tf_op jit(solution)/shard_map/ppermute | solution.py:365
  61.3 3.9 %collective-permute-start.11 = (bf16[2112,128]{1,0:T(8,128)(2,1)}, bf16[2112,128]{1,0:T(8,128)(2,1)}, u32[]{:S(2)}, u32[]{:S(2)}) collective-permute-start(bf16[2112,128]{1,0:T(8,128)(2,1)} %copy-done.3), channel_id=1, source_target_pairs={{0,1},{1,0},{2,3},{3,2},{4,5},{5,4},{6,7},{7,6},{8,9},{9,8},{10,11... | collective-permute-start | bytes 1622024 | tf_op jit(solution)/shard_map/ppermute | solution.py:365
  61.8 3.4 %collective-permute-start.12 = (bf16[2112,128]{1,0:T(8,128)(2,1)}, bf16[2112,128]{1,0:T(8,128)(2,1)}, u32[]{:S(2)}, u32[]{:S(2)}) collective-permute-start(bf16[2112,128]{1,0:T(8,128)(2,1)} %collective-permute-done.4.refs_2_), channel_id=1, source_target_pairs={{0,1},{1,0},{2,3},{3,2},{4,5},{5,4},{6,7},{7,6},{8,9},{9,8},{10,11... | collective-permute-start | bytes 1622024 | tf_op jit(solution)/shard_map/ppermute | solution.py:365
  61.9 4.0 %collective-permute-start.13 = (bf16[2112,128]{1,0:T(8,128)(2,1)}, bf16[2112,128]{1,0:T(8,128)(2,1)}, u32[]{:S(2)}, u32[]{:S(2)}) collective-permute-start(bf16[2112,128]{1,0:T(8,128)(2,1)} %collective-permute-done.5.refs_0_.refs_3_), channel_id=1, source_target_pairs={{0,1},{1,0},{2,3},{3,2},{4,5},{5,4},{6,7},{7,6},{8,9},{9,8},{10,11... | collective-permute-start | bytes 1622024 | tf_op jit(solution)/shard_map/ppermute | solution.py:365
  65.2 0.8 copy-start.4
  85.5 18.3 %collective-permute-start.17 = (s16[528,512]{1,0:T(8,128)(2,1)}, s16[528,512]{1,0:T(8,128)(2,1)}, u32[]{:S(2)}, u32[]{:S(2)}) collective-permute-start(s16[528,512]{1,0:T(8,128)(2,1)} %get-tuple-element.52.refs_0_), channel_id=1, source_target_pairs={{0,2},{1,3},{2,6},{3,7},{4,0},{5,1},{6,4},{7,5},{8,10},{9,11},{10,... | collective-permute-start | bytes 1622024 | tf_op jit(solution)/shard_map/ppermute | solution.py:365
  89.3 18.0 %collective-permute-start.15 = (s16[528,512]{1,0:T(8,128)(2,1)}, s16[528,512]{1,0:T(8,128)(2,1)S(1)}, u32[]{:S(2)}, u32[]{:S(2)}) collective-permute-start(s16[528,512]{1,0:T(8,128)(2,1)} %get-tuple-element.50.code0), channel_id=1, source_target_pairs={{0,16},{1,17},{2,18},{3,19},{4,20},{5,21},{6,22},{7,23},{8,24},{9,... | collective-permute-start | bytes 1622024 | tf_op jit(solution)/shard_map/ppermute | solution.py:365
  94.4 14.4 %collective-permute-start.14 = (s16[528,512]{1,0:T(8,128)(2,1)}, s16[528,512]{1,0:T(8,128)(2,1)}, u32[]{:S(2)}, u32[]{:S(2)}) collective-permute-start(s16[528,512]{1,0:T(8,128)(2,1)} %get-tuple-element.50.code0), channel_id=1, source_target_pairs={{0,8},{1,9},{2,10},{3,11},{4,12},{5,13},{6,14},{7,15},{8,0},{9,1},... | collective-permute-start | bytes 1622024 | tf_op jit(solution)/shard_map/ppermute | solution.py:365
  94.4 18.4 %collective-permute-start.19 = (s16[528,512]{1,0:T(8,128)(2,1)}, s16[528,512]{1,0:T(8,128)(2,1)}, u32[]{:S(2)}, u32[]{:S(2)}) collective-permute-start(s16[528,512]{1,0:T(8,128)(2,1)} %get-tuple-element.52.refs_0_), channel_id=1, source_target_pairs={{0,1},{1,0},{2,3},{3,2},{4,5},{5,4},{6,7},{7,6},{8,9},{9,8},{10,11... | collective-permute-start | bytes 1622024 | tf_op jit(solution)/shard_map/ppermute | solution.py:365
  103.9 8.9 %collective-permute-start.20 = (s16[528,512]{1,0:T(8,128)(2,1)}, s16[528,512]{1,0:T(8,128)(2,1)}, u32[]{:S(2)}, u32[]{:S(2)}) collective-permute-start(s16[528,512]{1,0:T(8,128)(2,1)} %collective-permute-done.17.refs_2_), channel_id=1, source_target_pairs={{0,1},{1,0},{2,3},{3,2},{4,5},{5,4},{6,7},{7,6},{8,9},{9,8},{10,11... | collective-permute-start | bytes 1622024 | tf_op jit(solution)/shard_map/ppermute | solution.py:365
  103.9 25.3 %collective-permute-start.18 = (s16[528,512]{1,0:T(8,128)(2,1)}, s16[528,512]{1,0:T(8,128)(2,1)}, u32[]{:S(2)}, u32[]{:S(2)}) collective-permute-start(s16[528,512]{1,0:T(8,128)(2,1)} %collective-permute-done.17.refs_2_), channel_id=1, source_target_pairs={{0,2},{1,3},{2,6},{3,7},{4,0},{5,1},{6,4},{7,5},{8,10},{9,11},{10,... | collective-permute-start | bytes 1622024 | tf_op jit(solution)/shard_map/ppermute | solution.py:365
  107.3 1.6 copy-start
  107.3 24.5 %collective-permute-start.16 = (s16[528,512]{1,0:T(8,128)(2,1)S(1)}, s16[528,512]{1,0:T(8,128)(2,1)}, u32[]{:S(2)}, u32[]{:S(2)}) collective-permute-start(s16[528,512]{1,0:T(8,128)(2,1)S(1)} %collective-permute-done.15.code2), channel_id=1, source_target_pairs={{0,8},{1,9},{2,10},{3,11},{4,12},{5,13},{6,14},{7,15},{8,0},{9,1},... | collective-permute-start | bytes 1622024 | tf_op jit(solution)/shard_map/ppermute | solution.py:365
  129.1 15.1 %collective-permute-start.22 = (s16[528,512]{1,0:T(8,128)(2,1)}, s16[528,512]{1,0:T(8,128)(2,1)}, u32[]{:S(2)}, u32[]{:S(2)}) collective-permute-start(s16[528,512]{1,0:T(8,128)(2,1)} %collective-permute-done.18.refs_0_), channel_id=1, source_target_pairs={{0,2},{1,3},{2,6},{3,7},{4,0},{5,1},{6,4},{7,5},{8,10},{9,11},{10,... | collective-permute-start | bytes 1622024 | tf_op jit(solution)/shard_map/ppermute | solution.py:365
  131.7 13.0 %collective-permute-start.21 = (s16[528,512]{1,0:T(8,128)(2,1)}, s16[528,512]{1,0:T(8,128)(2,1)}, u32[]{:S(2)}, u32[]{:S(2)}) collective-permute-start(s16[528,512]{1,0:T(8,128)(2,1)} %collective-permute-done.18.refs_0_), channel_id=1, source_target_pairs={{0,1},{1,0},{2,3},{3,2},{4,5},{5,4},{6,7},{7,6},{8,9},{9,8},{10,11... | collective-permute-start | bytes 1622024 | tf_op jit(solution)/shard_map/ppermute | solution.py:365
  144.3 2.3 %collective-permute-start.23 = (s16[528,512]{1,0:T(8,128)(2,1)}, s16[528,512]{1,0:T(8,128)(2,1)S(1)}, u32[]{:S(2)}, u32[]{:S(2)}) collective-permute-start(s16[528,512]{1,0:T(8,128)(2,1)} %collective-permute-done.22.refs_2_), channel_id=1, source_target_pairs={{0,1},{1,0},{2,3},{3,2},{4,5},{5,4},{6,7},{7,6},{8,9},{9,8},{10,11... | collective-permute-start | bytes 1622024 | tf_op jit(solution)/shard_map/ppermute | solution.py:365
  146.5 0.8 copy-start.2
